TPU v7x, 32 devices: a whole 2x2x4 slice. The times are simulated.
32 devices in a mesh: groups: 2 (over y), beam: 4 (over x, core), tile: 4 (over z).
Axes of the slice: x: 2, y: 2, z: 4, core: 2. Of those that a mesh axis runs over, the one named last changes fastest.
Arguments:
- smatrix: bfloat16 [2, 512, 512, 128], P(None, ('groups', 'beam'), 'tile'), parts along dimension 1, may hold values from -6 to 6
- beam_table: float32 [3, 256], P(None, 'beam'), may hold values from -8 to 8
- probes: int32 [64, 2], P(('groups', 'tile')), parts along dimension 0, may hold values from 0 to 2047, as said below
Outputs:
- diffraction: float32 [64, 32, 32], P(('groups', 'tile'), 'beam'), parts along dimension 0
There are 2 independent parts, one for each index of `groups`. A program takes and returns all parts, laid end to end along the dimension named above; an argument that names none is the same for every part. Nothing has to cross between parts.
Inputs may be any that keep to these rules, and one draw needn't show every extreme that they name: A probe's window starts at reduced row (row // 4 - 128 // 2) mod 512; the block of 128 rows holding that start is its window tile. Among the 8 probes of one index of tile at most 2 have the same window tile, and in every draw one window tile has exactly 2 probes from every index of tile. Columns lie below 512.
All inputs are finite; a program needn't handle non-finite values.
Results may differ from a plain program's by a relative error of at most 0.01.
Values may be sent and summed in bfloat16 or wider, within the bound.
No kernel may reach another device: no remote copies, remote signals or barrier semaphores. Data moves between devices by JAX's collectives and lax.ppermute only.
A program may use at most 64 MiB of HBM per device.

v0:
```python
import math

import jax
import jax.numpy as jnp
from jax import lax
from jax.sharding import PartitionSpec as P

IF = 4
BIN = 2
CAP = 2


two_pi = 2.0 * math.pi


def passed_along(array, axis, by):
    size = lax.axis_size(axis)
    return lax.ppermute(array, axis, [(i, (i + by) % size) for i in range(size)])


def dft_tables(window, kept_freq):
    column_idx = jnp.arange(window, dtype=jnp.int32)
    v_freq = jnp.arange(kept_freq, dtype=jnp.int32) - kept_freq // 2
    angle_v = (
        two_pi / window * jnp.mod(column_idx[:, None] * v_freq[None, :], window).astype(jnp.float32)
    )
    return (jnp.cos(angle_v).astype(jnp.bfloat16), jnp.sin(angle_v).astype(jnp.bfloat16))


def unpack(records, window, field_rows):
    pos_row = jnp.maximum(records[:, 0], 0)
    pos_col = jnp.maximum(records[:, 1], 0)
    start_row = jnp.mod(pos_row // IF - window // 2, field_rows)
    offset = jnp.mod(start_row, window)
    shift_x = jnp.mod(pos_col // IF - window // 2, window)
    return (pos_row, pos_col, offset, shift_x)


def phases(pos_row, pos_col, beam_table, window):
    phase = beam_table[2][None, :] + two_pi / (window * IF) * (
        beam_table[0][None, :] * pos_row[:, None].astype(jnp.float32)
        + beam_table[1][None, :] * pos_col[:, None].astype(jnp.float32)
    )
    return (jnp.cos(phase).astype(jnp.bfloat16), (-jnp.sin(phase)).astype(jnp.bfloat16))


def coefficients(pos_row, pos_col, beam_table, window):
    alpha_re, alpha_im = phases(pos_row, pos_col, beam_table, window)
    upper = jnp.concatenate([alpha_re, -alpha_im], axis=1)
    lower_rows = jnp.concatenate([alpha_im, alpha_re], axis=1)
    return jnp.concatenate([upper, lower_rows], axis=0)


def exit_waves(coeff_matrix, strips):
    beams_here = strips.shape[1]
    row_count = strips.shape[2]
    kept_freq = strips.shape[3]
    slot_count = coeff_matrix.shape[0] // 2
    flat = strips.reshape(2 * beams_here, row_count * kept_freq)
    waves = jnp.dot(coeff_matrix, flat, preferred_element_type=jnp.float32).astype(jnp.bfloat16)
    return waves.reshape(2, slot_count, row_count, kept_freq)


def row_kernels(offset, row_base, row_count, first_freq, freq_count, kept_freq, window):
    u_freq = jnp.arange(freq_count, dtype=jnp.int32) + first_freq - kept_freq // 2
    row_pos = (
        jnp.arange(row_count, dtype=jnp.int32)[None, None, :] + row_base - offset[:, None, None]
    )
    inside = (row_pos >= 0) & (row_pos < window)
    angle_u = (
        -two_pi / window * jnp.mod(u_freq[None, :, None] * row_pos, window).astype(jnp.float32)
    )
    kern_re = jnp.where(inside, jnp.cos(angle_u), 0.0).astype(jnp.bfloat16)
    kern_im = jnp.where(inside, jnp.sin(angle_u), 0.0).astype(jnp.bfloat16)
    return (kern_re, kern_im)


def local_terms(exit_wave, offset, row_base, shift_x, first_freq, freq_count, window):
    row_count = exit_wave.shape[2]
    kept_freq = exit_wave.shape[3]
    kern_re, kern_im = row_kernels(
        offset, row_base, row_count, first_freq, freq_count, kept_freq, window
    )
    wave_re = exit_wave[0]
    wave_im = exit_wave[1]
    out_re = jnp.einsum(
        "pur,prv->upv", kern_re, wave_re, preferred_element_type=jnp.float32
    ) - jnp.einsum("pur,prv->upv", kern_im, wave_im, preferred_element_type=jnp.float32)
    out_im = jnp.einsum(
        "pur,prv->upv", kern_re, wave_im, preferred_element_type=jnp.float32
    ) + jnp.einsum("pur,prv->upv", kern_im, wave_re, preferred_element_type=jnp.float32)
    v_freq = jnp.arange(kept_freq, dtype=jnp.int32) - kept_freq // 2
    turn = two_pi / window * jnp.mod(v_freq[None, :] * shift_x[:, None], window).astype(jnp.float32)
    cos_turn = jnp.cos(turn)[None]
    sin_turn = jnp.sin(turn)[None]
    return jnp.concatenate(
        [out_re * cos_turn - out_im * sin_turn, out_re * sin_turn + out_im * cos_turn], axis=2
    )


def per_device(smatrix, beam_table, probes):
    window = smatrix.shape[3]
    beams_here = smatrix.shape[1]
    kept_freq = window // 2
    n_tile = lax.axis_size("tile")
    n_beam = lax.axis_size("beam")
    field_rows = window * n_tile
    all_beams = beams_here * n_beam
    freq_share = kept_freq // n_beam
    start_row = jnp.mod(probes[:, 0] // IF - window // 2, field_rows)
    owner_tile = start_row // window
    onehot = (owner_tile[:, None] == jnp.arange(n_tile, dtype=jnp.int32)[None, :]).astype(jnp.int32)
    before = jnp.cumsum(onehot, axis=0) - onehot
    slot_index = jnp.sum(before * onehot, axis=1)
    target = owner_tile * CAP + slot_index
    outgoing = (
        jnp.full((n_tile * CAP, 2), -1, jnp.int32).at[target].set(probes).reshape(n_tile, CAP, 2)
    )
    arrived = lax.all_to_all(outgoing, "tile", split_axis=0, concat_axis=0, tiled=True).reshape(
        n_tile * CAP, 2
    )
    table_cos, table_sin = dft_tables(window, kept_freq)
    real_rows = smatrix[0].reshape(-1, window)
    imag_rows = smatrix[1].reshape(-1, window)
    spec_re = jnp.dot(real_rows, table_cos, preferred_element_type=jnp.float32) + jnp.dot(
        imag_rows, table_sin, preferred_element_type=jnp.float32
    )
    spec_im = jnp.dot(imag_rows, table_cos, preferred_element_type=jnp.float32) - jnp.dot(
        real_rows, table_sin, preferred_element_type=jnp.float32
    )
    spectra = (
        jnp.stack([spec_re, spec_im]).astype(jnp.bfloat16).reshape(2, beams_here, window, kept_freq)
    )
    pos_row, pos_col, offset, shift_x = unpack(arrived, window, field_rows)
    slot_count = n_tile * CAP
    coeff_matrix = coefficients(pos_row, pos_col, beam_table, window)
    exit_wave = exit_waves(coeff_matrix, spectra)
    carried = passed_along(arrived, "tile", 1)
    carry_row, carry_col, carry_offset, carry_shift = unpack(carried, window, field_rows)
    carry_wave = exit_waves(coefficients(carry_row, carry_col, beam_table, window), spectra)
    lower_part = local_terms(carry_wave, carry_offset, window, carry_shift, 0, kept_freq, window)
    returned = passed_along(lower_part.astype(jnp.bfloat16), "tile", -1).astype(lower_part.dtype)
    own_part = local_terms(exit_wave, offset, 0, shift_x, 0, kept_freq, window)
    summed = lax.psum((own_part + returned).astype(jnp.bfloat16), "beam").astype(jnp.float32)
    own_rows = lax.dynamic_slice_in_dim(summed, lax.axis_index("beam") * freq_share, freq_share, 0)
    real_part = own_rows[:, :, :kept_freq]
    imag_part = own_rows[:, :, kept_freq:]
    intensity = (real_part * real_part + imag_part * imag_part) / float(window * window * all_beams)
    binned = intensity.reshape(freq_share // BIN, BIN, slot_count, kept_freq // BIN, BIN).mean(
        axis=(1, 4)
    )
    outgoing_results = jnp.transpose(binned, (1, 0, 2)).reshape(
        n_tile, CAP, freq_share // BIN, kept_freq // BIN
    )
    results_home = lax.all_to_all(outgoing_results, "tile", split_axis=0, concat_axis=0, tiled=True)
    results_home = results_home.reshape(n_tile * CAP, freq_share // BIN, kept_freq // BIN)
    return results_home[target]


def solution(mesh):
    in_specs = (
        P(None, ("groups", "beam"), "tile", None),
        P(None, "beam"),
        P(("groups", "tile"), None),
    )
    out_specs = P(("groups", "tile"), "beam", None)
    return jax.shard_map(
        per_device, mesh=mesh, in_specs=in_specs, out_specs=out_specs, check_vma=False
    )
```

profile of v0, /device:TPU:0, one launch (start us, length us, event | category | flops | bytes accessed | tf_op | source)
XLA Modules:
  0.0 109.8 jit_solution(12363563301686514883)
XLA Ops:
  6.5 0.7 fusion.141
  7.2 0.8 copy.54
  8.0 0.2 reduce_window_sum.11
  8.2 0.7 fusion.63
  8.9 0.6 scatter_custom_fusion
  9.5 0.7 copy.56
  10.2 6.3 %all-to-all-start = ((s32[4,2,2]{1,2,0:T(2,128)}), s32[4,2,2]{1,2,0:T(2,128)S(1)}, u32[]{:S(2)}, u32[]{:S(2)}) async-start(s32[4,2,2]{1,2,0:T(2,128)} %copy.56), calls=%async_computation | async-start | bytes 8192 | tf_op jit(solution)/shard_map/all_to_all | solution.py:119
  16.5 2.7 %fusion.124 = (bf16[1,64,128,128]{3,2,1,0:T(8,128)(2,1)S(1)}, bf16[1,64,128,128]{3,2,1,0:T(8,128)(2,1)S(1)}) fusion(bf16[2,64,128,128]{3,2,1,0:T(8,128)(2,1)} %param.3), kind=kLoop, calls=%fused_computation.235 | loop fusion | bytes 8388608 | tf_op jit(solution)/shard_map/slice | solution.py:123
  19.3 1.1 %fusion.25 = f32[64,8192]{1,0:T(8,128)S(1)} fusion(bf16[8192,128]{1,0:T(8,128)(2,1)S(1)} %bitcast.82, s32[64]{0:T(128)S(1)} %iota_add_fusion.1), kind=kOutput, calls=%fused_computation.65 | convolution fusion | flops 134340608 | bytes 4194560 | tf_op jit(solution)/shard_map/dot_general | solution.py:128
  20.4 1.1 %fusion.26 = f32[64,8192]{1,0:T(8,128)S(1)} fusion(bf16[8192,128]{1,0:T(8,128)(2,1)S(1)} %bitcast.84, s32[64]{0:T(128)S(1)} %iota_add_fusion.1), kind=kOutput, calls=%fused_computation.66 | convolution fusion | flops 134340608 | bytes 4194560 | tf_op jit(solution)/shard_map/dot_general | solution.py:125
  21.5 1.1 %fusion.2 = bf16[1,8192,64]{1,2,0:T(8,128)(2,1)S(1)} fusion(f32[64,8192]{1,0:T(8,128)S(1)} %fusion.25, bf16[8192,128]{1,0:T(8,128)(2,1)S(1)} %bitcast.85, s32[64]{0:T(128)S(1)} %iota_add_fusion.1), kind=kOutput, calls=%fused_computation.6 | convolution fusion | flops 135389184 | bytes 5243136 | tf_op jit(solution)/shard_map/dot_general | solution.py:128
  22.6 1.1 %fusion.3 = bf16[1,8192,64]{1,2,0:T(8,128)(2,1)S(1)} fusion(f32[64,8192]{1,0:T(8,128)S(1)} %fusion.26, bf16[8192,128]{1,0:T(8,128)(2,1)S(1)} %bitcast.83, s32[64]{0:T(128)S(1)} %iota_add_fusion.1), kind=kOutput, calls=%fused_computation.7 | convolution fusion | flops 135389184 | bytes 5243136 | tf_op jit(solution)/shard_map/dot_general | solution.py:125
  23.8 0.2 pad_maximum_fusion
  24.0 3.2 %copy.58 = bf16[2,8192,64]{2,1,0:T(8,128)(2,1)} copy(bf16[2,8192,64]{1,2,0:T(8,128)(2,1)S(1)} %pad_maximum_fusion) | data formatting | bytes 4194304 | tf_op jit(solution)/shard_map/stack | solution.py:132
  27.2 5.7 %convert_element_type.121 = bf16[128,8192]{1,0:T(8,128)(2,1)S(1)} reshape(bf16[2,8192,64]{2,1,0:T(8,128)(2,1)} %copy.58) | data formatting | bytes 4194304 | tf_op jit(solution)/shard_map/convert_element_type | solution.py:132
  32.9 2.2 %collective-permute-start = (s32[8,2]{0,1:T(2,128)S(1)}, s32[8,2]{0,1:T(2,128)S(1)}, u32[]{:S(2)}, u32[]{:S(2)}) collective-permute-start(s32[8,2]{0,1:T(2,128)S(1)} %reshape.386), channel_id=1, source_target_pairs={{0,1},{1,2},{2,3},{3,0},{4,5},{5,6},{6,7},{7,4},{8,9},{9,10},{10,1... | collective-permute-start | bytes 200 | tf_op jit(solution)/shard_map/ppermute | solution.py:18
  35.3 3.2 %collective-permute-done = s32[8,2]{0,1:T(2,128)S(1)} collective-permute-done((s32[8,2]{0,1:T(2,128)S(1)}, s32[8,2]{0,1:T(2,128)S(1)}, u32[]{:S(2)}, u32[]{:S(2)}) %collective-permute-start) | collective-permute-done | bytes 96 | tf_op jit(solution)/shard_map/ppermute | solution.py:18
  38.7 0.1 fusion.122
  38.8 0.2 cosine_convert_fusion.3
  39.0 0.4 convolution_convert_fusion.1
  39.4 0.2 squeeze.18
  39.7 0.2 squeeze.8
  39.9 1.1 %fusion.16 = f32[8,64,64]{1,2,0:T(8,128)S(1)} fusion(bf16[8,128,64]{2,1,0:T(8,128)(2,1)S(1)} %squeeze.18, s32[8,128]{1,0:T(8,128)S(1)} %iota_subtract_fusion, s32[64]{0:T(128)S(1)} %iota_add_fusion.1, pred[8,128]{1,0:T(8,128)(4,1)S(1)} %compare_and_fusion.1), kind=kOutput, calls=%fused_computation.48 | convolution fusion | flops 9437184 | bytes 267520 | tf_op jit(solution)/shard_map/pur,prv->upv/dot_general | solution.py:89
  41.1 1.2 %fusion.15 = f32[8,64,64]{1,2,0:T(8,128)S(1)} fusion(bf16[8,128,64]{2,1,0:T(8,128)(2,1)S(1)} %squeeze.8, s32[8,128]{1,0:T(8,128)S(1)} %iota_subtract_fusion, s32[64]{0:T(128)S(1)} %iota_add_fusion.1, pred[8,128]{1,0:T(8,128)(4,1)S(1)} %compare_and_fusion.1), kind=kOutput, calls=%fused_computation.47 | convolution fusion | flops 9437184 | bytes 267520 | tf_op jit(solution)/shard_map/pur,prv->upv/dot_general | solution.py:86
  42.2 1.2 %convolution_add_fusion.2 = f32[8,64,64]{1,2,0:T(8,128)S(1)} fusion(f32[8,64,64]{1,2,0:T(8,128)S(1)} %fusion.16, bf16[8,128,64]{2,1,0:T(8,128)(2,1)S(1)} %squeeze.8, s32[8,128]{1,0:T(8,128)S(1)} %iota_subtract_fusion, s32[64]{0:T(128)S(1)} %iota_add_fusion.1, pred[8,128]{1,0:T(8,128)(4,1)S(1)} %compare_and_fusion.1), kind=kOutput, calls=%fused_computation.13 | convolution fusion | flops 9469952 | bytes 398592 | tf_op jit(solution)/shard_map/pur,prv->upv/dot_general | solution.py:91
  43.4 0.4 convolution_convert_fusion
  43.9 0.2 squeeze.19
  44.1 0.2 squeeze.20
  44.4 1.1 %fusion.13 = f32[8,64,64]{1,2,0:T(8,128)S(1)} fusion(bf16[8,128,64]{2,1,0:T(8,128)(2,1)S(1)} %squeeze.19, s32[8,128]{1,0:T(8,128)S(1)} %broadcast_subtract_fusion, s32[64]{0:T(128)S(1)} %iota_add_fusion.1, pred[8,128]{1,0:T(8,128)(4,1)S(1)} %compare_and_fusion), kind=kOutput, calls=%fused_computation.45 | convolution fusion | flops 9437184 | bytes 267520 | tf_op jit(solution)/shard_map/pur,prv->upv/dot_general | solution.py:86
  45.5 1.2 %fusion.14 = f32[8,64,64]{1,2,0:T(8,128)S(1)} fusion(bf16[8,128,64]{2,1,0:T(8,128)(2,1)S(1)} %squeeze.20, s32[8,128]{1,0:T(8,128)S(1)} %broadcast_subtract_fusion, s32[64]{0:T(128)S(1)} %iota_add_fusion.1, pred[8,128]{1,0:T(8,128)(4,1)S(1)} %compare_and_fusion), kind=kOutput, calls=%fused_computation.46 | convolution fusion | flops 9437184 | bytes 267520 | tf_op jit(solution)/shard_map/pur,prv->upv/dot_general | solution.py:89
  46.7 1.2 %convolution_subtract_fusion.1 = f32[8,64,64]{1,2,0:T(8,128)S(1)} fusion(f32[8,64,64]{1,2,0:T(8,128)S(1)} %fusion.13, bf16[8,128,64]{2,1,0:T(8,128)(2,1)S(1)} %squeeze.20, s32[8,128]{1,0:T(8,128)S(1)} %broadcast_subtract_fusion, s32[64]{0:T(128)S(1)} %iota_add_fusion.1, pred[8,128]{1,0:T(8,128)(4,1)S(1)} %compare_and_fusion), kind=kOutput, calls=%fused_computation.12 | convolution fusion | flops 9469952 | bytes 398592 | tf_op jit(solution)/shard_map/pur,prv->upv/dot_general | solution.py:88
  47.9 1.2 %fusion.11 = (bf16[64,8,64]{2,0,1:T(8,128)(2,1)S(1)}, bf16[64,8,64]{2,0,1:T(8,128)(2,1)S(1)}) fusion(f32[8,64,64]{1,2,0:T(8,128)S(1)} %convolution_subtract_fusion.1, f32[8,64]{1,0:T(8,128)S(1)} %get-tuple-element.40, f32[8,64]{1,0:T(8,128)S(1)} %get-tuple-element.41, f32[8,64,64]{1,2,0:T(8,128)S(1)} %fusion.14, bf16[8,128,64]{2,1,0:T(8,128)(2,1)S(1)} %squeeze.19, ...), kind=kOutput, calls=%fused_computation.41 | convolution fusion | flops 9732096 | bytes 533760 | tf_op jit(solution)/shard_map/pur,prv->upv/dot_general | solution.py:91
  49.0 0.1 pad_maximum_fusion.1
  49.2 2.1 %collective-permute-start.1 = (bf16[64,8,128]{2,0,1:T(8,128)(2,1)S(1)}, bf16[64,8,128]{2,0,1:T(8,128)(2,1)S(1)}, u32[]{:S(2)}, u32[]{:S(2)}) collective-permute-start(bf16[64,8,128]{2,0,1:T(8,128)(2,1)S(1)} %pad_maximum_fusion.1), channel_id=1, source_target_pairs={{0,3},{1,0},{2,1},{3,2},{4,7},{5,4},{6,5},{7,6},{8,11},{9,8},{10,9... | collective-permute-start | bytes 393224 | tf_op jit(solution)/shard_map/ppermute | solution.py:18
  51.2 1.2 %subtract_bitcast_fusion = (f32[64,8,64]{2,0,1:T(8,128)S(1)}, f32[64,8,64]{2,0,1:T(8,128)S(1)}) fusion(f32[8,64,64]{1,2,0:T(8,128)S(1)} %convolution_add_fusion.2, f32[8,64]{1,0:T(8,128)S(1)} %get-tuple-element.39, f32[8,64]{1,0:T(8,128)S(1)} %get-tuple-element.38, f32[8,64,64]{1,2,0:T(8,128)S(1)} %fusion.15, bf16[8,128,64]{2,1,0:T(8,128)(2,1)S(1)} %squeeze.18, ...), kind=kOutput, calls=%fused_computation.38 | convolution fusion | flops 9666560 | bytes 664832 | tf_op jit(solution)/shard_map/pur,prv->upv/dot_general | solution.py:88
  52.4 1.8 %collective-permute-done.1 = bf16[64,8,128]{2,0,1:T(8,128)(2,1)S(1)} collective-permute-done((bf16[64,8,128]{2,0,1:T(8,128)(2,1)S(1)}, bf16[64,8,128]{2,0,1:T(8,128)(2,1)S(1)}, u32[]{:S(2)}, u32[]{:S(2)}) %collective-permute-start.1) | collective-permute-done | bytes 131104 | tf_op jit(solution)/shard_map/ppermute | solution.py:18
  54.2 0.8 fusion.10
  55.0 33.0 %all-reduce.2.cloned.1.call-done = bf16[64,8,128]{2,0,1:T(8,128)(2,1)} async-done(((bf16[64,8,128]{2,0,1:T(8,128)(2,1)}), bf16[64,8,128]{2,0,1:T(8,128)(2,1)}) %all-reduce.2.cloned.1.call-update) | async-done | bytes 131088 | tf_op jit(solution)/shard_map/psum | solution.py:144
  88.0 0.8 dynamic-slice_convert_fusion
  88.9 0.2 copy.67
  89.1 0.4 reduce_sum.22
  89.5 0.1 copy.68
  89.6 0.7 reshape.408
  90.3 4.6 %all-to-all-start.1 = ((f32[4,1,512]{2,1,0:T(1,128)}), f32[4,1,512]{2,1,0:T(1,128)S(1)}, u32[]{:S(2)}, u32[]{:S(2)}) async-start(f32[4,1,512]{2,1,0:T(1,128)} %reshape.408), calls=%async_computation.1 | async-start | bytes 16384 | tf_op jit(solution)/shard_map/all_to_all | solution.py:155
  94.9 5.6 %all-to-all-done.1 = f32[4,1,512]{2,1,0:T(1,128)S(1)} async-done(((f32[4,1,512]{2,1,0:T(1,128)}), f32[4,1,512]{2,1,0:T(1,128)S(1)}, u32[]{:S(2)}, u32[]{:S(2)}) %all-to-all-start.1) | async-done | bytes 8224 | tf_op jit(solution)/shard_map/all_to_all | solution.py:155
  100.5 0.5 broadcast.749
  101.0 0.7 reduce
  101.8 1.2 %gather_fusion = f32[8,8,32]{2,1,0:T(8,128)} fusion(f32[8,8,32]{2,1,0:T(8,128)S(1)} %bitcast.88, s32[1024]{0:T(1024)S(1)} %pad_clamp_fusion), kind=kCustom, calls=%fused_computation | custom fusion | bytes 16416 | tf_op jit(solution)/shard_map/gather | solution.py:157
  (26 shorter events, 0.8 us)
Async XLA Ops:
  10.2 22.6 %all-to-all-start = ((s32[4,2,2]{1,2,0:T(2,128)}), s32[4,2,2]{1,2,0:T(2,128)S(1)}, u32[]{:S(2)}, u32[]{:S(2)}) async-start(s32[4,2,2]{1,2,0:T(2,128)} %copy.56), calls=%async_computation | async-start | bytes 8192 | tf_op jit(solution)/shard_map/all_to_all | solution.py:119
  16.5 71.5 %all-reduce.2.cloned.1.call-start = ((), (), s32[]{:S(2)}) async-start(), calls=%async_computation.2 | async-start | bytes 262144 | tf_op jit(solution)/shard_map/psum | solution.py:144
  24.0 3.2 %copy-start = (f32[3,64]{1,0:T(4,128)S(1)}, f32[3,64]{1,0:T(4,128)}, u32[]{:S(2)}) copy-start(f32[3,64]{1,0:T(4,128)} %param.4) | copy-start | bytes 2308
  32.9 5.5 %collective-permute-start = (s32[8,2]{0,1:T(2,128)S(1)}, s32[8,2]{0,1:T(2,128)S(1)}, u32[]{:S(2)}, u32[]{:S(2)}) collective-permute-start(s32[8,2]{0,1:T(2,128)S(1)} %reshape.386), channel_id=1, source_target_pairs={{0,1},{1,2},{2,3},{3,0},{4,5},{5,6},{6,7},{7,4},{8,9},{9,10},{10,1... | collective-permute-start | bytes 200 | tf_op jit(solution)/shard_map/ppermute | solution.py:18
  49.2 5.0 %collective-permute-start.1 = (bf16[64,8,128]{2,0,1:T(8,128)(2,1)S(1)}, bf16[64,8,128]{2,0,1:T(8,128)(2,1)S(1)}, u32[]{:S(2)}, u32[]{:S(2)}) collective-permute-start(bf16[64,8,128]{2,0,1:T(8,128)(2,1)S(1)} %pad_maximum_fusion.1), channel_id=1, source_target_pairs={{0,3},{1,0},{2,1},{3,2},{4,7},{5,4},{6,5},{7,6},{8,11},{9,8},{10,9... | collective-permute-start | bytes 393224 | tf_op jit(solution)/shard_map/ppermute | solution.py:18
  90.3 10.2 %all-to-all-start.1 = ((f32[4,1,512]{2,1,0:T(1,128)}), f32[4,1,512]{2,1,0:T(1,128)S(1)}, u32[]{:S(2)}, u32[]{:S(2)}) async-start(f32[4,1,512]{2,1,0:T(1,128)} %reshape.408), calls=%async_computation.1 | async-start | bytes 16384 | tf_op jit(solution)/shard_map/all_to_all | solution.py:155
Sparse Core Ops, SparseCore 0:
  55.1 32.8 all-reduce.1
where the time goes:
time: 110 us
  waiting for transfers between devices  43.5 us (40%)
  local copies, waits for them, and re-layouts  17.5 us (16%)
  starting transfers between devices  15.2 us (14%)
  matrix products  14.6 us (13%)
  between operations  13.6 us (12%)
  other arithmetic  5.32 us (5%)
    psum x1, waiting for transfers between devices, per_device(): lax.psum((own_part + returned).astype(jnp.bfloat16), 'beam')  33 us
    all_to_all x1, starting transfers between devices, per_device(): lax.all_to_all(outgoing, 'tile', split_axis=0, concat_axis=0, tiled=True)  6.32 us
    convert_element_type x1, local copies, waits for them, and re-layouts, per_device(): jnp.stack([spec_re, spec_im]).astype(jnp.bfloat16)  5.66 us
    all_to_all x1, waiting for transfers between devices, per_device(): lax.all_to_all(outgoing_results, 'tile', split_axis=0, concat_axis=0, til...  5.58 us
    ppermute x2, waiting for transfers between devices, passed_along(): lax.ppermute(array, axis, [(i, (i + by) % size) for i in range(size)])  4.93 us
    all_to_all x1, starting transfers between devices, per_device(): lax.all_to_all(outgoing_results, 'tile', split_axis=0, concat_axis=0, til...  4.6 us
    ppermute x2, starting transfers between devices, passed_along(): lax.ppermute(array, axis, [(i, (i + by) % size) for i in range(size)])  4.27 us
    another operation x1, local copies, waits for them, and re-layouts, per_device(): jnp.stack([spec_re, spec_im]).astype(jnp.bfloat16)  3.18 us
  transfers between devices with their start and end apart: 5, of which 4 were waited for; matrix products, arithmetic and copies ran while one was open for 16% of the time, Pallas kernels for 0%

commit v1 on v0

v1 whole, which is shorter than its diff:
```python
import functools
import math

import jax
import jax.numpy as jnp
from jax import lax
from jax.experimental import pallas as pl
from jax.experimental.pallas import tpu as pltpu
from jax.sharding import PartitionSpec as P

IF = 4
BIN = 2
CAP = 2
PER_LIST = 2 * CAP
LANES = 128
GROUP = 16
ROWS = 16

two_pi = 2.0 * math.pi
f32 = jnp.float32
bf16 = jnp.bfloat16
i32 = jnp.int32


def iota(shape, dim):
    return lax.broadcasted_iota(i32, shape, dim)


def turns(index, window):
    return (two_pi / window) * jnp.bitwise_and(index, window - 1).astype(f32)


def bit_reversed(number, count):
    bits = count.bit_length() - 1
    return sum(((number >> b) & 1) << (bits - 1 - b) for b in range(bits))


def window_start(row, window, field_rows):
    start = jnp.right_shift(row, 2) - window // 2
    start = jnp.where(start < 0, start + field_rows, start)
    tile = jnp.right_shift(start, window.bit_length() - 1)
    return tile, jnp.bitwise_and(start, window - 1)


def times_i(pairs):
    return pltpu.roll(pairs, LANES // 2, pairs.ndim - 1)


def spectra_kernel(sizes, probes, smatrix, spectra, row_table, turn, column_table):
    window, kept, n_tile, n_beam = sizes
    share = kept // n_beam
    me_beam = lax.axis_index("beam")

    @pl.when(pl.program_id(0) == 0)
    def tables():
        shape = (2 * window, 2 * kept)
        x, part_in = iota(shape, 0) % window, iota(shape, 0) // window
        lane = iota(shape, 1)
        v, part_out = lane % kept - kept // 2, lane // kept
        angle = turns(x * v + (window // 4) * (part_out - part_in), window)
        column_table[...] = jnp.cos(angle).astype(bf16)

        shape = (2 * kept, 2 * window)
        line, turned = iota(shape, 0) % kept, iota(shape, 0) // kept
        r, part_in = iota(shape, 1) % window, iota(shape, 1) // window
        block = line // share
        owner = jnp.zeros_like(block)
        for pos in range(n_beam):
            owner = jnp.where(block == pos, jnp.bitwise_xor(me_beam, bit_reversed(pos, n_beam)), owner)
        u = owner * share + line % share - kept // 2
        angle = turns(u * r + (window // 4) * (turned - part_in), window)
        row_table[...] = jnp.cos(angle).astype(bf16)

        u = iota((share, LANES), 0) + me_beam * share - kept // 2
        lane = iota((share, LANES), 1)
        v = lane % kept - kept // 2
        for j in range(probes.shape[0]):
            _, offset = window_start(probes[j, 0], window, window * n_tile)
            shift = jnp.right_shift(probes[j, 1], 2) - window // 2
            angle = turns(u * offset + v * shift, window)
            turn[0, j] = jnp.cos(angle)
            turn[1, j] = jnp.where(lane < kept, -jnp.sin(angle), jnp.sin(angle))

    planes = smatrix.shape[1]
    flat = jnp.concatenate(
        [smatrix[0].reshape(planes * window, window), smatrix[1].reshape(planes * window, window)], axis=1
    )
    product = jnp.dot(flat, column_table[...], preferred_element_type=f32)
    spectra[...] = product.astype(bf16).reshape(spectra.shape)


def chosen(lists, me_tile, window, n_tile):
    before = jnp.where(me_tile == 0, n_tile - 1, me_tile - 1)
    rows, columns = [], []
    for probes in lists:
        picked = [[i32(0), i32(0)] for _ in range(PER_LIST)]
        seen = [i32(0), i32(0)]
        for j in range(probes.shape[0]):
            row, column = probes[j, 0], probes[j, 1]
            tile, _ = window_start(row, window, window * n_tile)
            for which, wanted in enumerate((me_tile, before)):
                match = tile == wanted
                for slot in range(CAP):
                    take = match & (seen[which] == slot)
                    held = picked[which * CAP + slot]
                    picked[which * CAP + slot] = [jnp.where(take, row, held[0]), jnp.where(take, column, held[1])]
                seen[which] = seen[which] + match.astype(i32)
        rows += [p[0] for p in picked]
        columns += [p[1] for p in picked]
    return rows, columns


def parts_kernel(sizes, *refs):
    window, kept, n_tile, n_beam = sizes
    lists = refs[:n_tile]
    beam_table, row_table, spectra, keep, send, coeff, waves = refs[n_tile:]
    share = kept // n_beam
    beams = spectra.shape[0]
    slots = n_tile * PER_LIST
    wide = beams * ROWS
    me_tile = lax.axis_index("tile")
    rows, columns = chosen(lists, me_tile, window, n_tile)
    offsets = [window_start(row, window, window * n_tile)[1] for row in rows]
    which = iota((slots, 1), 0)
    row_v = jnp.zeros((slots, 1), f32)
    column_v = jnp.zeros((slots, 1), f32)
    for s in range(slots):
        row_v = jnp.where(which == s, rows[s].astype(f32), row_v)
        column_v = jnp.where(which == s, columns[s].astype(f32), column_v)
    phase = beam_table[2:3, :] + two_pi / (window * IF) * (
        beam_table[0:1, :] * row_v + beam_table[1:2, :] * column_v
    )
    alpha = jnp.concatenate([jnp.cos(phase), -jnp.sin(phase)], axis=0).astype(bf16)
    spread = (iota((beams, wide), 1) // ROWS == iota((beams, wide), 0)).astype(f32).astype(bf16)
    alpha = jnp.dot(alpha, spread, preferred_element_type=f32)
    own_row = iota((ROWS, wide), 1) % ROWS == iota((ROWS, wide), 0)
    y_in = iota((ROWS, LANES), 0)
    lane = iota((kept, LANES), 1)
    sign = jnp.where(lane < kept, -1.0, 1.0)
    for first in range(0, slots, GROUP):
        for c in range(2):
            for p in range(GROUP):
                line = c * slots + first + p
                spot = (c * GROUP + p) * ROWS
                coeff[spot : spot + ROWS, :] = jnp.where(own_row, alpha[line : line + 1, :], 0.0).astype(bf16)
        for y in range(0, window, 2 * ROWS):
            pair = jnp.concatenate(
                [spectra[:, y + h : y + h + ROWS, :].reshape(wide, LANES) for h in (0, ROWS)], axis=1
            )
            made = jnp.dot(coeff[...], pair, preferred_element_type=f32)
            for h in range(2):
                y_here = y_in + (y + h * ROWS)
                for p in range(GROUP):
                    offset = offsets[first + p]
                    starts_here = p % PER_LIST < CAP
                    inside = y_here >= offset if starts_here else y_here < offset
                    for c in range(2):
                        spot = (c * GROUP + p) * ROWS
                        value = made[spot : spot + ROWS, h * LANES : (h + 1) * LANES]
                        waves[c, p, y + h * ROWS : y + (h + 1) * ROWS, :] = jnp.where(inside, value, 0.0).astype(bf16)
        for p in range(0, GROUP, PER_LIST):
            fields = []
            for q in range(p, p + PER_LIST, 2):
                pair = jnp.concatenate(
                    [waves[:, q + h].reshape(2 * window, LANES) for h in range(2)], axis=1
                )
                both = jnp.dot(row_table[...], pair, preferred_element_type=f32)
                for h in range(2):
                    value = both[:, h * LANES : (h + 1) * LANES]
                    fields.append(value[:kept] + times_i(value[kept:]) * sign)
            k = (first + p) // PER_LIST
            for pos in range(n_beam):
                block = jnp.concatenate([f[pos * share : (pos + 1) * share] for f in fields], axis=0).astype(bf16)
                half = n_beam // 2
                if pos < half:
                    keep[pos, k] = block
                else:
                    send[pos - half, k] = block


def result_kernel(sizes, all_beams, *refs):
    window, kept, n_tile, n_beam = sizes
    probes, turn = refs[:2]
    blocks = refs[2 : 2 + n_tile]
    out, staged, intensity = refs[2 + n_tile :]
    share = kept // n_beam
    count = probes.shape[0]
    me_tile = lax.axis_index("tile")
    for k in range(n_tile):
        block = blocks[k][...].astype(f32)
        for s in range(PER_LIST):
            staged[k * PER_LIST + s] = block[s * share : (s + 1) * share]
    tiles = [window_start(probes[j, 0], window, window * n_tile)[0] for j in range(count)]
    for j in range(count):
        slot = sum([(tiles[i] == tiles[j]).astype(i32) for i in range(j)], i32(0))
        following = jnp.where(tiles[j] == n_tile - 1, 0, tiles[j] + 1)
        field = (
            staged[jnp.bitwise_xor(tiles[j], me_tile) * PER_LIST + slot]
            + staged[jnp.bitwise_xor(following, me_tile) * PER_LIST + CAP + slot]
        )
        field = field * turn[0, j] + times_i(field) * turn[1, j]
        intensity[j * share : (j + 1) * share, :] = field * field
    height = count * share // BIN
    summed = intensity[pl.ds(0, height, stride=BIN), :]
    for b in range(1, BIN):
        summed = summed + intensity[pl.ds(b, height, stride=BIN), :]
    shape = (LANES, kept // BIN)
    bins = (iota(shape, 0) % kept // BIN == iota(shape, 1)).astype(f32)
    binned = jnp.dot(summed, bins, precision=lax.Precision.HIGHEST, preferred_element_type=f32)
    binned = binned * (1.0 / (BIN * BIN * window * window * all_beams))
    for j in range(count):
        out[j] = binned[j * (share // BIN) : (j + 1) * (share // BIN)]


VMEM = pl.BlockSpec(memory_space=pltpu.VMEM)
SMEM = pl.BlockSpec(memory_space=pltpu.SMEM)


def params(**more):
    return pltpu.CompilerParams(vmem_limit_bytes=48 * 1024 * 1024, **more)


def swapped(array, axis, by):
    return lax.ppermute(array, axis, [(i, i ^ by) for i in range(lax.axis_size(axis))])


def per_device(smatrix, beam_table, probes):
    _, beams, window, _ = smatrix.shape
    kept = window // 2
    n_tile = lax.axis_size("tile")
    n_beam = lax.axis_size("beam")
    sizes = (window, kept, n_tile, n_beam)
    share = kept // n_beam
    slots = n_tile * PER_LIST
    count = probes.shape[0]

    lists = [probes] + [swapped(probes, "tile", k) for k in range(1, n_tile)]

    step = 8
    spectra, row_table, turn = pl.pallas_call(
        functools.partial(spectra_kernel, sizes),
        grid=(beams // step,),
        in_specs=[SMEM, pl.BlockSpec((2, step, window, window), lambda i: (0, i, 0, 0))],
        out_specs=[
            pl.BlockSpec((step, window, 2 * kept), lambda i: (i, 0, 0)),
            pl.BlockSpec((2 * kept, 2 * window), lambda i: (0, 0)),
            pl.BlockSpec((2, count, share, LANES), lambda i: (0, 0, 0, 0)),
        ],
        out_shape=[
            jax.ShapeDtypeStruct((beams, window, 2 * kept), bf16),
            jax.ShapeDtypeStruct((2 * kept, 2 * window), bf16),
            jax.ShapeDtypeStruct((2, count, share, LANES), f32),
        ],
        scratch_shapes=[pltpu.VMEM((2 * window, 2 * kept), bf16)],
        compiler_params=params(),
        cost_estimate=pl.CostEstimate(
            flops=2 * beams * window * 4 * window * kept, bytes_accessed=smatrix.size * 3, transcendentals=0
        ),
        name="spectra",
    )(probes, smatrix)

    half = jax.ShapeDtypeStruct((n_beam // 2, n_tile, PER_LIST * share, LANES), bf16)
    keep, send = pl.pallas_call(
        functools.partial(parts_kernel, sizes),
        in_specs=[SMEM] * n_tile + [VMEM] * 3,
        out_specs=[VMEM] * 2,
        out_shape=[half, half],
        scratch_shapes=[
            pltpu.VMEM((2 * GROUP * ROWS, beams * ROWS), bf16),
            pltpu.VMEM((2, GROUP, window, LANES), bf16),
        ],
        compiler_params=params(),
        cost_estimate=pl.CostEstimate(
            flops=2 * slots * 2 * ROWS * beams * window * LANES, bytes_accessed=4 * 1024 * 1024, transcendentals=0
        ),
        name="parts",
    )(*lists, beam_table, row_table, spectra)

    by = 1
    while by < n_beam:
        arrived = swapped(send, "beam", by)
        total = (keep.astype(f32) + arrived.astype(f32)).astype(bf16)
        by *= 2
        middle = total.shape[0] // 2
        keep, send = total[:middle], total[middle:]
    mine = total[0]
    blocks = [mine[0]] + [swapped(mine[k], "tile", k) for k in range(1, n_tile)]

    return pl.pallas_call(
        functools.partial(result_kernel, sizes, beams * n_beam),
        in_specs=[SMEM] + [VMEM] * (1 + n_tile),
        out_specs=VMEM,
        out_shape=jax.ShapeDtypeStruct((count, share // BIN, kept // BIN), f32),
        scratch_shapes=[pltpu.VMEM((slots, share, LANES), f32), pltpu.VMEM((count * share, LANES), f32)],
        compiler_params=params(),
        name="result",
    )(probes, turn, *blocks)


def solution(mesh):
    in_specs = (
        P(None, ("groups", "beam"), "tile", None),
        P(None, "beam"),
        P(("groups", "tile"), None),
    )
    out_specs = P(("groups", "tile"), "beam", None)
    return jax.shard_map(
        per_device, mesh=mesh, in_specs=in_specs, out_specs=out_specs, check_vma=False
    )
```

time: 110 us -> 32.5 us (0.30)
  waiting for transfers between devices: 43.5 us -> 7.9 us
  local copies, waits for them, and re-layouts: 17.5 us -> 0.78 us
  matrix products: 14.6 us -> 0 us
  between operations: 13.6 us -> 0.08 us
  Pallas kernels: 0 us -> 11.4 us
  other arithmetic: 5.32 us -> 0.06 us
  starting transfers between devices: 15.2 us -> 12 us
    psum x1 -> x0, waiting for transfers between devices: 33 us -> none  [per_device(): lax.psum((own_part + returned).astype(jnp.bfloat16), 'beam')]
    dot_general x14 -> x0, matrix products: 14.6 us -> none  [the longest x2 2.35 us: local_terms(): jnp.einsum('pur,prv->upv', kern_im, wave_re, preferred_element_type=jnp.f...]
    pallas_call x0 -> x3, Pallas kernels: none -> 11.4 us  [the longest x1 7.09 us: per_device(): pl.pallas_call(functools.partial(spectra_kernel, sizes), grid=(beams // s...]
    all_to_all x2 -> x0, starting transfers between devices: 10.9 us -> none  [the longest x1 6.32 us: per_device(): lax.all_to_all(outgoing, 'tile', split_axis=0, concat_axis=0, tiled=True)]
    ppermute x2 -> x8, starting transfers between devices: 4.27 us -> 12 us  [swapped(): lax.ppermute(array, axis, [(i, i ^ by) for i in range(lax.axis_size(axis))])]
    convert_element_type x1 -> x0, local copies, waits for them, and re-layouts: 5.66 us -> none  [per_device(): jnp.stack([spec_re, spec_im]).astype(jnp.bfloat16)]
    all_to_all x2 -> x0, waiting for transfers between devices: 5.58 us -> none  [the longest x1 5.58 us: per_device(): lax.all_to_all(outgoing_results, 'tile', split_axis=0, concat_axis=0, til...]
    another operation x1 -> x0, local copies, waits for them, and re-layouts: 3.18 us -> none  [per_device(): jnp.stack([spec_re, spec_im]).astype(jnp.bfloat16)]
  transfers between devices with their start and end apart: 5 -> 8, of which waited for: 4 -> 4; matrix products, arithmetic and copies ran while one was open for 16% -> 0% of each run, Pallas kernels for 0% -> 22%
where the time goes in v1:
time: 32.5 us; the launch traced here: 32.2 us
  starting transfers between devices  12 us (37%)
  Pallas kernels  11.4 us (35%)
  waiting for transfers between devices  7.9 us (24%)
  local copies, waits for them, and re-layouts  0.78 us (2%)
    ppermute x8, starting transfers between devices, swapped(): lax.ppermute(array, axis, [(i, i ^ by) for i in range(lax.axis_size(axis))])  12 us
    ppermute x8, waiting for transfers between devices, swapped(): lax.ppermute(array, axis, [(i, i ^ by) for i in range(lax.axis_size(axis))])  7.9 us
    pallas_call x1, Pallas kernels, per_device(): pl.pallas_call(functools.partial(spectra_kernel, sizes), grid=(beams // s...  7.09 us
    pallas_call x1, Pallas kernels, per_device(): pl.pallas_call(functools.partial(parts_kernel, sizes), in_specs=[SMEM] *...  2.82 us
    pallas_call x1, Pallas kernels, per_device(): pl.pallas_call(functools.partial(result_kernel, sizes, beams * n_beam), i...  1.53 us
    unnamed x3, local copies, waits for them, and re-layouts  0.77 us
  transfers between devices with their start and end apart: 8, of which 4 were waited for; matrix products, arithmetic and copies ran while one was open for 0% of the time, Pallas kernels for 22%

profile of v1, /device:TPU:0, one launch (start us, length us, event | category | flops | bytes accessed | tf_op | source)
XLA Modules:
  0.0 32.2 jit_solution(15447349539178592457)
XLA Ops:
  0.0 0.0 copy-start
  0.0 0.8 %copy.9.probes.refs_0_ = s32[8,2]{1,0:T(8,128)S(1)} copy(s32[8,2]{0,1:T(2,128)} %param.5) | data formatting | bytes 128 | tf_op args[2]
  0.8 5.0 %collective-permute-start.2 = (s32[8,2]{1,0:T(8,128)S(1)}, s32[8,2]{1,0:T(8,128)S(1)}, u32[]{:S(2)}, u32[]{:S(2)}) collective-permute-start(s32[8,2]{1,0:T(8,128)S(1)} %copy.9.probes.refs_0_), channel_id=1, source_target_pairs={{0,3},{1,2},{2,1},{3,0},{4,7},{5,6},{6,5},{7,4},{8,11},{9,10},{10,... | collective-permute-start | bytes 200 | tf_op jit(solution)/shard_map/ppermute | solution.py:224
  5.8 0.0 collective-permute-start.1
  5.8 0.6 %collective-permute-start = (s32[8,2]{1,0:T(8,128)S(1)}, s32[8,2]{1,0:T(8,128)S(1)}, u32[]{:S(2)}, u32[]{:S(2)}) collective-permute-start(s32[8,2]{1,0:T(8,128)S(1)} %copy.9.probes.refs_0_), channel_id=1, source_target_pairs={{0,1},{1,0},{2,3},{3,2},{4,5},{5,4},{6,7},{7,6},{8,9},{9,8},{10,11... | collective-permute-start | bytes 200 | tf_op jit(solution)/shard_map/ppermute | solution.py:224
  6.4 7.1 %spectra.1 = (bf16[64,128,128]{2,1,0:T(8,128)(2,1)S(1)}, bf16[128,256]{1,0:T(8,128)(2,1)S(1)}, f32[2,8,16,128]{3,2,1,0:T(8,128)S(1)}) custom-call(s32[8,2]{1,0:T(8,128)S(1)} %copy.9.probes.refs_0_, bf16[2,64,128,128]{3,2,1,0:T(8,128)(2,1)} %smatrix.1), custom_call_target="tpu_custom_call" | custom-call | flops 536870912 | bytes 6291456 | tf_op jit(solution)/shard_map/spectra/pallas_call | solution.py:240
  13.5 0.0 collective-permute-done.2.refs_3_
  13.5 0.0 collective-permute-done.1.refs_2_
  13.5 0.0 collective-permute-done.refs_1_
  13.5 0.0 copy-done
  13.5 2.8 %parts.1 = (bf16[2,4,64,128]{3,2,1,0:T(8,128)(2,1)S(1)}, bf16[2,4,64,128]{3,2,1,0:T(8,128)(2,1)S(1)}) custom-call(s32[8,2]{1,0:T(8,128)S(1)} %copy.9.probes.refs_0_, s32[8,2]{1,0:T(8,128)S(1)} %collective-permute-done.refs_1_, s32[8,2]{1,0:T(8,128)S(1)} %collective-permute-done.1.refs_2_, s32[8,2]{1,0:T(8,128)S(1)} %collective-permute-done.2.refs_3_, ...), custom_call_target="tpu_custom_call" | custom-call | flops 1073741824 | bytes 4194304 | tf_op jit(solution)/shard_map/parts/pallas_call | solution.py:263
  16.3 0.1 collective-permute-start.3
  16.4 1.3 %collective-permute-done.3 = bf16[2,4,64,128]{3,2,1,0:T(8,128)(2,1)S(1)} collective-permute-done((bf16[2,4,64,128]{3,2,1,0:T(8,128)(2,1)S(1)}, bf16[2,4,64,128]{3,2,1,0:T(8,128)(2,1)S(1)}, u32[]{:S(2)}, u32[]{:S(2)}) %collective-permute-start.3) | collective-permute-done | bytes 131104 | tf_op jit(solution)/shard_map/ppermute | solution.py:224
  17.8 1.8 %collective-permute-start.4 = (bf16[1,4,64,128]{3,2,1,0:T(8,128)(2,1)S(1)}, bf16[1,4,64,128]{3,2,1,0:T(8,128)(2,1)S(1)}, u32[]{:S(2)}, u32[]{:S(2)}) collective-permute-start(bf16[1,4,64,128]{3,2,1,0:T(8,128)(2,1)S(1)} %slice.29), channel_id=1, source_target_pairs={{0,8},{4,12},{8,0},{12,4},{1,9},{5,13},{9,1},{13,5},{2,10},{6,14},... | collective-permute-start | bytes 196616 | tf_op jit(solution)/shard_map/ppermute | solution.py:224
  19.6 2.6 %collective-permute-done.4 = bf16[1,4,64,128]{3,2,1,0:T(8,128)(2,1)S(1)} collective-permute-done((bf16[1,4,64,128]{3,2,1,0:T(8,128)(2,1)S(1)}, bf16[1,4,64,128]{3,2,1,0:T(8,128)(2,1)S(1)}, u32[]{:S(2)}, u32[]{:S(2)}) %collective-permute-start.4) | collective-permute-done | bytes 65568 | tf_op jit(solution)/shard_map/ppermute | solution.py:224
  22.2 3.9 %collective-permute-start.7 = (bf16[64,128]{1,0:T(8,128)(2,1)S(1)}, bf16[64,128]{1,0:T(8,128)(2,1)S(1)}, u32[]{:S(2)}, u32[]{:S(2)}) collective-permute-start(bf16[64,128]{1,0:T(8,128)(2,1)S(1)} %get-tuple-element.15), channel_id=1, source_target_pairs={{0,3},{1,2},{2,1},{3,0},{4,7},{5,6},{6,5},{7,4},{8,11},{9,10},{10,... | collective-permute-start | bytes 49160 | tf_op jit(solution)/shard_map/ppermute | solution.py:224
  26.1 0.0 collective-permute-start.6
  26.1 0.6 %collective-permute-start.5 = (bf16[64,128]{1,0:T(8,128)(2,1)S(1)}, bf16[64,128]{1,0:T(8,128)(2,1)S(1)}, u32[]{:S(2)}, u32[]{:S(2)}) collective-permute-start(bf16[64,128]{1,0:T(8,128)(2,1)S(1)} %get-tuple-element.17), channel_id=1, source_target_pairs={{0,1},{1,0},{2,3},{3,2},{4,5},{5,4},{6,7},{7,6},{8,9},{9,8},{10,11... | collective-permute-start | bytes 49160 | tf_op jit(solution)/shard_map/ppermute | solution.py:224
  26.7 1.1 %collective-permute-done.7.refs_5_ = bf16[64,128]{1,0:T(8,128)(2,1)S(1)} collective-permute-done((bf16[64,128]{1,0:T(8,128)(2,1)S(1)}, bf16[64,128]{1,0:T(8,128)(2,1)S(1)}, u32[]{:S(2)}, u32[]{:S(2)}) %collective-permute-start.7) | collective-permute-done | bytes 16416 | tf_op jit(solution)/shard_map/ppermute | solution.py:224
  27.8 2.9 %collective-permute-done.6.refs_4_ = bf16[64,128]{1,0:T(8,128)(2,1)S(1)} collective-permute-done((bf16[64,128]{1,0:T(8,128)(2,1)S(1)}, bf16[64,128]{1,0:T(8,128)(2,1)S(1)}, u32[]{:S(2)}, u32[]{:S(2)}) %collective-permute-start.6) | collective-permute-done | bytes 16416 | tf_op jit(solution)/shard_map/ppermute | solution.py:224
  30.7 0.0 collective-permute-done.5.refs_3_
  30.7 1.5 %result.1 = f32[8,8,32]{2,1,0:T(8,128)} custom-call(s32[8,2]{1,0:T(8,128)S(1)} %copy.9.probes.refs_0_, f32[2,8,16,128]{3,2,1,0:T(8,128)S(1)} %get-tuple-element.10.refs_1_, bf16[64,128]{1,0:T(8,128)(2,1)S(1)} %get-tuple-element.18.refs_2_, bf16[64,128]{1,0:T(8,128)(2,1)S(1)} %collective-permute-done.5.refs_3_, ...), custom_call_target="tpu_custom_call" | custom-call | tf_op jit(solution)/shard_map/result/pallas_call | solution.py:289
  (4 shorter events, 0.1 us)
Async XLA Ops:
  0.0 13.5 %copy-start = (f32[3,64]{1,0:T(4,128)S(1)}, f32[3,64]{1,0:T(4,128)}, u32[]{:S(2)}) copy-start(f32[3,64]{1,0:T(4,128)} %refs_4_.1) | copy-start | bytes 2308
  0.8 12.7 %collective-permute-start.2 = (s32[8,2]{1,0:T(8,128)S(1)}, s32[8,2]{1,0:T(8,128)S(1)}, u32[]{:S(2)}, u32[]{:S(2)}) collective-permute-start(s32[8,2]{1,0:T(8,128)S(1)} %copy.9.probes.refs_0_), channel_id=1, source_target_pairs={{0,3},{1,2},{2,1},{3,0},{4,7},{5,6},{6,5},{7,4},{8,11},{9,10},{10,... | collective-permute-start | bytes 200 | tf_op jit(solution)/shard_map/ppermute | solution.py:224
  5.8 7.7 %collective-permute-start.1 = (s32[8,2]{1,0:T(8,128)S(1)}, s32[8,2]{1,0:T(8,128)S(1)}, u32[]{:S(2)}, u32[]{:S(2)}) collective-permute-start(s32[8,2]{1,0:T(8,128)S(1)} %copy.9.probes.refs_0_), channel_id=1, source_target_pairs={{0,2},{1,3},{2,0},{3,1},{4,6},{5,7},{6,4},{7,5},{8,10},{9,11},{10,... | collective-permute-start | bytes 200 | tf_op jit(solution)/shard_map/ppermute | solution.py:224
  5.8 7.7 %collective-permute-start = (s32[8,2]{1,0:T(8,128)S(1)}, s32[8,2]{1,0:T(8,128)S(1)}, u32[]{:S(2)}, u32[]{:S(2)}) collective-permute-start(s32[8,2]{1,0:T(8,128)S(1)} %copy.9.probes.refs_0_), channel_id=1, source_target_pairs={{0,1},{1,0},{2,3},{3,2},{4,5},{5,4},{6,7},{7,6},{8,9},{9,8},{10,11... | collective-permute-start | bytes 200 | tf_op jit(solution)/shard_map/ppermute | solution.py:224
  16.3 1.4 %collective-permute-start.3 = (bf16[2,4,64,128]{3,2,1,0:T(8,128)(2,1)S(1)}, bf16[2,4,64,128]{3,2,1,0:T(8,128)(2,1)S(1)}, u32[]{:S(2)}, u32[]{:S(2)}) collective-permute-start(bf16[2,4,64,128]{3,2,1,0:T(8,128)(2,1)S(1)} %get-tuple-element.14), channel_id=1, source_target_pairs={{0,4},{4,0},{8,12},{12,8},{1,5},{5,1},{9,13},{13,9},{2,6},{6,2},{1... | collective-permute-start | bytes 393224 | tf_op jit(solution)/shard_map/ppermute | solution.py:224
  17.8 4.3 %collective-permute-start.4 = (bf16[1,4,64,128]{3,2,1,0:T(8,128)(2,1)S(1)}, bf16[1,4,64,128]{3,2,1,0:T(8,128)(2,1)S(1)}, u32[]{:S(2)}, u32[]{:S(2)}) collective-permute-start(bf16[1,4,64,128]{3,2,1,0:T(8,128)(2,1)S(1)} %slice.29), channel_id=1, source_target_pairs={{0,8},{4,12},{8,0},{12,4},{1,9},{5,13},{9,1},{13,5},{2,10},{6,14},... | collective-permute-start | bytes 196616 | tf_op jit(solution)/shard_map/ppermute | solution.py:224
  22.2 5.6 %collective-permute-start.7 = (bf16[64,128]{1,0:T(8,128)(2,1)S(1)}, bf16[64,128]{1,0:T(8,128)(2,1)S(1)}, u32[]{:S(2)}, u32[]{:S(2)}) collective-permute-start(bf16[64,128]{1,0:T(8,128)(2,1)S(1)} %get-tuple-element.15), channel_id=1, source_target_pairs={{0,3},{1,2},{2,1},{3,0},{4,7},{5,6},{6,5},{7,4},{8,11},{9,10},{10,... | collective-permute-start | bytes 49160 | tf_op jit(solution)/shard_map/ppermute | solution.py:224
  26.1 4.6 %collective-permute-start.6 = (bf16[64,128]{1,0:T(8,128)(2,1)S(1)}, bf16[64,128]{1,0:T(8,128)(2,1)S(1)}, u32[]{:S(2)}, u32[]{:S(2)}) collective-permute-start(bf16[64,128]{1,0:T(8,128)(2,1)S(1)} %get-tuple-element.16), channel_id=1, source_target_pairs={{0,2},{1,3},{2,0},{3,1},{4,6},{5,7},{6,4},{7,5},{8,10},{9,11},{10,... | collective-permute-start | bytes 49160 | tf_op jit(solution)/shard_map/ppermute | solution.py:224
  26.1 4.6 %collective-permute-start.5 = (bf16[64,128]{1,0:T(8,128)(2,1)S(1)}, bf16[64,128]{1,0:T(8,128)(2,1)S(1)}, u32[]{:S(2)}, u32[]{:S(2)}) collective-permute-start(bf16[64,128]{1,0:T(8,128)(2,1)S(1)} %get-tuple-element.17), channel_id=1, source_target_pairs={{0,1},{1,0},{2,3},{3,2},{4,5},{5,4},{6,7},{7,6},{8,9},{9,8},{10,11... | collective-permute-start | bytes 49160 | tf_op jit(solution)/shard_map/ppermute | solution.py:224

commit v2 on v1

--- a/solution.py
+++ b/solution.py
@@ -14,6 +14,7 @@
 PER_LIST = 2 * CAP
 LANES = 128
 GROUP = 16
+CHUNKS = 1
 ROWS = 16
 
 two_pi = 2.0 * math.pi
@@ -46,47 +47,55 @@
     return pltpu.roll(pairs, LANES // 2, pairs.ndim - 1)
 
 
-def spectra_kernel(sizes, probes, smatrix, spectra, row_table, turn, column_table):
+def spectra_kernel(sizes, probes_hbm, smatrix_hbm, spectra, row_table, turn, column_table, smatrix, probes, sems):
     window, kept, n_tile, n_beam = sizes
     share = kept // n_beam
     me_beam = lax.axis_index("beam")
-
-    @pl.when(pl.program_id(0) == 0)
-    def tables():
-        shape = (2 * window, 2 * kept)
-        x, part_in = iota(shape, 0) % window, iota(shape, 0) // window
-        lane = iota(shape, 1)
-        v, part_out = lane % kept - kept // 2, lane // kept
-        angle = turns(x * v + (window // 4) * (part_out - part_in), window)
-        column_table[...] = jnp.cos(angle).astype(bf16)
-
-        shape = (2 * kept, 2 * window)
-        line, turned = iota(shape, 0) % kept, iota(shape, 0) // kept
-        r, part_in = iota(shape, 1) % window, iota(shape, 1) // window
-        block = line // share
-        owner = jnp.zeros_like(block)
-        for pos in range(n_beam):
-            owner = jnp.where(block == pos, jnp.bitwise_xor(me_beam, bit_reversed(pos, n_beam)), owner)
-        u = owner * share + line % share - kept // 2
-        angle = turns(u * r + (window // 4) * (turned - part_in), window)
-        row_table[...] = jnp.cos(angle).astype(bf16)
-
-        u = iota((share, LANES), 0) + me_beam * share - kept // 2
-        lane = iota((share, LANES), 1)
-        v = lane % kept - kept // 2
-        for j in range(probes.shape[0]):
-            _, offset = window_start(probes[j, 0], window, window * n_tile)
-            shift = jnp.right_shift(probes[j, 1], 2) - window // 2
-            angle = turns(u * offset + v * shift, window)
-            turn[0, j] = jnp.cos(angle)
-            turn[1, j] = jnp.where(lane < kept, -jnp.sin(angle), jnp.sin(angle))
-
-    planes = smatrix.shape[1]
-    flat = jnp.concatenate(
-        [smatrix[0].reshape(planes * window, window), smatrix[1].reshape(planes * window, window)], axis=1
-    )
-    product = jnp.dot(flat, column_table[...], preferred_element_type=f32)
-    spectra[...] = product.astype(bf16).reshape(spectra.shape)
+    planes = smatrix.shape[1] // CHUNKS
+    chunks = [pl.ds(i * planes, planes) for i in range(CHUNKS)]
+    copies = [
+        pltpu.make_async_copy(smatrix_hbm.at[:, chunk], smatrix.at[:, chunk], sems.at[i])
+        for i, chunk in enumerate(chunks)
+    ]
+    for copy in copies:
+        copy.start()
+    listed = pltpu.make_async_copy(probes_hbm, probes, sems.at[CHUNKS])
+    listed.start()
+
+    shape = (2 * window, 2 * kept)
+    x, part_in = iota(shape, 0) % window, iota(shape, 0) // window
+    lane = iota(shape, 1)
+    v, part_out = lane % kept - kept // 2, lane // kept
+    angle = turns(x * v + (window // 4) * (part_out - part_in), window)
+    column_table[...] = jnp.cos(angle).astype(bf16)
+
+    shape = (2 * kept, 2 * window)
+    line, turned = iota(shape, 0) % kept, iota(shape, 0) // kept
+    r, part_in = iota(shape, 1) % window, iota(shape, 1) // window
+    block = line // share
+    owner = jnp.zeros_like(block)
+    for pos in range(n_beam):
+        owner = jnp.where(block == pos, jnp.bitwise_xor(me_beam, bit_reversed(pos, n_beam)), owner)
+    u = owner * share + line % share - kept // 2
+    angle = turns(u * r + (window // 4) * (turned - part_in), window)
+    row_table[...] = jnp.cos(angle).astype(bf16)
+
+    u = iota((share, LANES), 0) + me_beam * share - kept // 2
+    lane = iota((share, LANES), 1)
+    v = lane % kept - kept // 2
+    listed.wait()
+    for j in range(probes.shape[1]):
+        _, offset = window_start(probes[0, j], window, window * n_tile)
+        shift = jnp.right_shift(probes[1, j], 2) - window // 2
+        angle = turns(u * offset + v * shift, window)
+        turn[0, j] = jnp.cos(angle)
+        turn[1, j] = jnp.where(lane < kept, -jnp.sin(angle), jnp.sin(angle))
+
+    for copy, chunk in zip(copies, chunks):
+        copy.wait()
+        flat = jnp.concatenate([smatrix[c, chunk].reshape(planes * window, window) for c in range(2)], axis=1)
+        product = jnp.dot(flat, column_table[...], preferred_element_type=f32)
+        spectra[chunk] = product.astype(bf16).reshape(planes, window, 2 * kept)
 
 
 def chosen(lists, me_tile, window, n_tile):
@@ -95,8 +104,8 @@
     for probes in lists:
         picked = [[i32(0), i32(0)] for _ in range(PER_LIST)]
         seen = [i32(0), i32(0)]
-        for j in range(probes.shape[0]):
-            row, column = probes[j, 0], probes[j, 1]
+        for j in range(probes.shape[1]):
+            row, column = probes[0, j], probes[1, j]
             tile, _ = window_start(row, window, window * n_tile)
             for which, wanted in enumerate((me_tile, before)):
                 match = tile == wanted
@@ -184,13 +193,13 @@
     blocks = refs[2 : 2 + n_tile]
     out, staged, intensity = refs[2 + n_tile :]
     share = kept // n_beam
-    count = probes.shape[0]
+    count = probes.shape[1]
     me_tile = lax.axis_index("tile")
     for k in range(n_tile):
         block = blocks[k][...].astype(f32)
         for s in range(PER_LIST):
             staged[k * PER_LIST + s] = block[s * share : (s + 1) * share]
-    tiles = [window_start(probes[j, 0], window, window * n_tile)[0] for j in range(count)]
+    tiles = [window_start(probes[0, j], window, window * n_tile)[0] for j in range(count)]
     for j in range(count):
         slot = sum([(tiles[i] == tiles[j]).astype(i32) for i in range(j)], i32(0))
         following = jnp.where(tiles[j] == n_tile - 1, 0, tiles[j] + 1)
@@ -213,11 +222,12 @@
 
 
 VMEM = pl.BlockSpec(memory_space=pltpu.VMEM)
+HBM = pl.BlockSpec(memory_space=pltpu.HBM)
 SMEM = pl.BlockSpec(memory_space=pltpu.SMEM)
 
 
-def params(**more):
-    return pltpu.CompilerParams(vmem_limit_bytes=48 * 1024 * 1024, **more)
+def params(mib=16):
+    return pltpu.CompilerParams(vmem_limit_bytes=mib * 1024 * 1024)
 
 
 def swapped(array, axis, by):
@@ -234,30 +244,30 @@
     slots = n_tile * PER_LIST
     count = probes.shape[0]
 
+    probes = probes.T
     lists = [probes] + [swapped(probes, "tile", k) for k in range(1, n_tile)]
 
-    step = 8
     spectra, row_table, turn = pl.pallas_call(
         functools.partial(spectra_kernel, sizes),
-        grid=(beams // step,),
-        in_specs=[SMEM, pl.BlockSpec((2, step, window, window), lambda i: (0, i, 0, 0))],
-        out_specs=[
-            pl.BlockSpec((step, window, 2 * kept), lambda i: (i, 0, 0)),
-            pl.BlockSpec((2 * kept, 2 * window), lambda i: (0, 0)),
-            pl.BlockSpec((2, count, share, LANES), lambda i: (0, 0, 0, 0)),
-        ],
+        in_specs=[HBM, HBM],
+        out_specs=[VMEM] * 3,
         out_shape=[
             jax.ShapeDtypeStruct((beams, window, 2 * kept), bf16),
             jax.ShapeDtypeStruct((2 * kept, 2 * window), bf16),
             jax.ShapeDtypeStruct((2, count, share, LANES), f32),
         ],
-        scratch_shapes=[pltpu.VMEM((2 * window, 2 * kept), bf16)],
-        compiler_params=params(),
+        scratch_shapes=[
+            pltpu.VMEM((2 * window, 2 * kept), bf16),
+            pltpu.VMEM(smatrix.shape, bf16),
+            pltpu.SMEM(probes.shape, i32),
+            pltpu.SemaphoreType.DMA((CHUNKS + 1,)),
+        ],
+        compiler_params=params(48),
         cost_estimate=pl.CostEstimate(
             flops=2 * beams * window * 4 * window * kept, bytes_accessed=smatrix.size * 3, transcendentals=0
         ),
         name="spectra",
-    )(probes, smatrix)
+    )(pltpu.with_memory_space_constraint(probes, pltpu.HBM), pltpu.with_memory_space_constraint(smatrix, pltpu.HBM))
 
     half = jax.ShapeDtypeStruct((n_beam // 2, n_tile, PER_LIST * share, LANES), bf16)
     keep, send = pl.pallas_call(

time: 32.5 us -> 27.8 us (0.86)
  Pallas kernels: 11.4 us -> 7.56 us
  local copies, waits for them, and re-layouts: 0.78 us -> 0.02 us
    pallas_call x1, Pallas kernels: 7.09 us -> 3.46 us  [per_device(): pl.pallas_call(functools.partial(spectra_kernel, sizes), in_specs=[HBM, H...]
    unnamed x3 -> x4, local copies, waits for them, and re-layouts: 0.77 us -> 0.01 us
  transfers between devices with their start and end apart: 8 -> 8, of which waited for: 4 -> 5; matrix products, arithmetic and copies ran while one was open for 0% -> 0% of each run, Pallas kernels for 22% -> 13%
where the time goes in v2:
time: 27.8 us; the launch traced here: 27.6 us
  starting transfers between devices  11.8 us (42%)
  waiting for transfers between devices  8.14 us (29%)
  Pallas kernels  7.56 us (27%)
    ppermute x8, starting transfers between devices, swapped(): lax.ppermute(array, axis, [(i, i ^ by) for i in range(lax.axis_size(axis))])  11.8 us
    ppermute x8, waiting for transfers between devices, swapped(): lax.ppermute(array, axis, [(i, i ^ by) for i in range(lax.axis_size(axis))])  8.14 us
    pallas_call x1, Pallas kernels, per_device(): pl.pallas_call(functools.partial(spectra_kernel, sizes), in_specs=[HBM, H...  3.46 us
    pallas_call x1, Pallas kernels, per_device(): pl.pallas_call(functools.partial(parts_kernel, sizes), in_specs=[SMEM] *...  2.61 us
    pallas_call x1, Pallas kernels, per_device(): pl.pallas_call(functools.partial(result_kernel, sizes, beams * n_beam), i...  1.49 us
  transfers between devices with their start and end apart: 8, of which 5 were waited for; matrix products, arithmetic and copies ran while one was open for 0% of the time, Pallas kernels for 13%

profile of v2, /device:TPU:0, one launch (start us, length us, event | category | flops | bytes accessed | tf_op | source)
XLA Modules:
  0.0 27.6 jit_solution(10164751205521739061)
XLA Ops:
  0.0 0.0 copy-start
  0.0 0.0 copy-start.1
  0.0 5.0 %collective-permute-start.2 = (s32[2,8]{1,0:T(2,128)}, s32[2,8]{1,0:T(2,128)S(1)}, u32[]{:S(2)}, u32[]{:S(2)}) collective-permute-start(s32[2,8]{1,0:T(2,128)} %bitcast.9), channel_id=1, source_target_pairs={{0,3},{1,2},{2,1},{3,0},{4,7},{5,6},{6,5},{7,4},{8,11},{9,10},{10,... | collective-permute-start | bytes 200 | tf_op jit(solution)/shard_map/ppermute | solution.py:234
  5.1 0.0 collective-permute-start.1
  5.1 0.6 %collective-permute-start = (s32[2,8]{1,0:T(2,128)}, s32[2,8]{1,0:T(2,128)S(1)}, u32[]{:S(2)}, u32[]{:S(2)}) collective-permute-start(s32[2,8]{1,0:T(2,128)} %bitcast.11), channel_id=1, source_target_pairs={{0,1},{1,0},{2,3},{3,2},{4,5},{5,4},{6,7},{7,6},{8,9},{9,8},{10,11... | collective-permute-start | bytes 200 | tf_op jit(solution)/shard_map/ppermute | solution.py:234
  5.7 3.5 %spectra.1 = (bf16[64,128,128]{2,1,0:T(8,128)(2,1)S(1)}, bf16[128,256]{1,0:T(8,128)(2,1)S(1)}, f32[2,8,16,128]{3,2,1,0:T(8,128)S(1)}) custom-call(s32[2,8]{1,0:T(2,128)} %bitcast.12, bf16[2,64,128,128]{3,2,1,0:T(8,128)(2,1)} %smatrix_hbm.1), custom_call_target="tpu_custom_call" | custom-call | flops 536870912 | bytes 6291456 | tf_op jit(solution)/shard_map/spectra/pallas_call | solution.py:250
  9.2 0.0 collective-permute-done.2.refs_3_
  9.2 0.6 %collective-permute-done.1.refs_2_ = s32[2,8]{1,0:T(2,128)S(1)} collective-permute-done((s32[2,8]{1,0:T(2,128)}, s32[2,8]{1,0:T(2,128)S(1)}, u32[]{:S(2)}, u32[]{:S(2)}) %collective-permute-start.1) | collective-permute-done | bytes 96 | tf_op jit(solution)/shard_map/ppermute | solution.py:234
  9.7 0.0 collective-permute-done.refs_1_
  9.7 0.0 copy-done
  9.7 0.0 copy-done.1
  9.7 2.6 %parts.1 = (bf16[2,4,64,128]{3,2,1,0:T(8,128)(2,1)S(1)}, bf16[2,4,64,128]{3,2,1,0:T(8,128)(2,1)S(1)}) custom-call(s32[2,8]{1,0:T(2,128)S(1)} %bitcast.13, s32[2,8]{1,0:T(2,128)S(1)} %collective-permute-done.refs_1_, s32[2,8]{1,0:T(2,128)S(1)} %collective-permute-done.1.refs_2_, s32[2,8]{1,0:T(2,128)S(1)} %collective-permute-done.2.refs_3_, ...), custom_call_target="tpu_custom_call" | custom-call | flops 1073741824 | bytes 4194304 | tf_op jit(solution)/shard_map/parts/pallas_call | solution.py:273
  12.4 0.1 collective-permute-start.3
  12.4 1.3 %collective-permute-done.3 = bf16[2,4,64,128]{3,2,1,0:T(8,128)(2,1)S(1)} collective-permute-done((bf16[2,4,64,128]{3,2,1,0:T(8,128)(2,1)S(1)}, bf16[2,4,64,128]{3,2,1,0:T(8,128)(2,1)S(1)}, u32[]{:S(2)}, u32[]{:S(2)}) %collective-permute-start.3) | collective-permute-done | bytes 131104 | tf_op jit(solution)/shard_map/ppermute | solution.py:234
  13.8 1.6 %collective-permute-start.4 = (bf16[1,4,64,128]{3,2,1,0:T(8,128)(2,1)S(1)}, bf16[1,4,64,128]{3,2,1,0:T(8,128)(2,1)S(1)}, u32[]{:S(2)}, u32[]{:S(2)}) collective-permute-start(bf16[1,4,64,128]{3,2,1,0:T(8,128)(2,1)S(1)} %slice.29), channel_id=1, source_target_pairs={{0,8},{4,12},{8,0},{12,4},{1,9},{5,13},{9,1},{13,5},{2,10},{6,14},... | collective-permute-start | bytes 196616 | tf_op jit(solution)/shard_map/ppermute | solution.py:234
  15.4 2.8 %collective-permute-done.4 = bf16[1,4,64,128]{3,2,1,0:T(8,128)(2,1)S(1)} collective-permute-done((bf16[1,4,64,128]{3,2,1,0:T(8,128)(2,1)S(1)}, bf16[1,4,64,128]{3,2,1,0:T(8,128)(2,1)S(1)}, u32[]{:S(2)}, u32[]{:S(2)}) %collective-permute-start.4) | collective-permute-done | bytes 65568 | tf_op jit(solution)/shard_map/ppermute | solution.py:234
  18.2 3.3 %collective-permute-start.7 = (bf16[64,128]{1,0:T(8,128)(2,1)S(1)}, bf16[64,128]{1,0:T(8,128)(2,1)S(1)}, u32[]{:S(2)}, u32[]{:S(2)}) collective-permute-start(bf16[64,128]{1,0:T(8,128)(2,1)S(1)} %get-tuple-element.15), channel_id=1, source_target_pairs={{0,3},{1,2},{2,1},{3,0},{4,7},{5,6},{6,5},{7,4},{8,11},{9,10},{10,... | collective-permute-start | bytes 49160 | tf_op jit(solution)/shard_map/ppermute | solution.py:234
  21.5 0.0 collective-permute-start.6
  21.5 1.2 %collective-permute-start.5 = (bf16[64,128]{1,0:T(8,128)(2,1)S(1)}, bf16[64,128]{1,0:T(8,128)(2,1)S(1)}, u32[]{:S(2)}, u32[]{:S(2)}) collective-permute-start(bf16[64,128]{1,0:T(8,128)(2,1)S(1)} %get-tuple-element.17), channel_id=1, source_target_pairs={{0,1},{1,0},{2,3},{3,2},{4,5},{5,4},{6,7},{7,6},{8,9},{9,8},{10,11... | collective-permute-start | bytes 49160 | tf_op jit(solution)/shard_map/ppermute | solution.py:234
  22.7 1.2 %collective-permute-done.7.refs_5_ = bf16[64,128]{1,0:T(8,128)(2,1)S(1)} collective-permute-done((bf16[64,128]{1,0:T(8,128)(2,1)S(1)}, bf16[64,128]{1,0:T(8,128)(2,1)S(1)}, u32[]{:S(2)}, u32[]{:S(2)}) %collective-permute-start.7) | collective-permute-done | bytes 16416 | tf_op jit(solution)/shard_map/ppermute | solution.py:234
  23.8 2.3 %collective-permute-done.6.refs_4_ = bf16[64,128]{1,0:T(8,128)(2,1)S(1)} collective-permute-done((bf16[64,128]{1,0:T(8,128)(2,1)S(1)}, bf16[64,128]{1,0:T(8,128)(2,1)S(1)}, u32[]{:S(2)}, u32[]{:S(2)}) %collective-permute-start.6) | collective-permute-done | bytes 16416 | tf_op jit(solution)/shard_map/ppermute | solution.py:234
  26.1 0.0 collective-permute-done.5.refs_3_
  26.1 1.5 %result.1 = f32[8,8,32]{2,1,0:T(8,128)} custom-call(s32[2,8]{1,0:T(2,128)S(1)} %bitcast.14, f32[2,8,16,128]{3,2,1,0:T(8,128)S(1)} %get-tuple-element.10.refs_1_, bf16[64,128]{1,0:T(8,128)(2,1)S(1)} %get-tuple-element.18.refs_2_, bf16[64,128]{1,0:T(8,128)(2,1)S(1)} %collective-permute-done.5.refs_3_, bf16[64,128]{1,0:T(8,128)(2,1)S(1)} %collective-permute-done.6.refs_4_, ...), custom_call_target="tpu_custom_call" | custom-call | tf_op jit(solution)/shard_map/result/pallas_call | solution.py:299
  (4 shorter events, 0.1 us)
Async XLA Ops:
  0.0 9.7 %copy-start = (s32[8,2]{0,1:T(2,128)S(1)}, s32[8,2]{0,1:T(2,128)}, u32[]{:S(2)}) copy-start(s32[8,2]{0,1:T(2,128)} %param.5) | copy-start | bytes 196
  0.0 9.7 %copy-start.1 = (f32[3,64]{1,0:T(4,128)S(1)}, f32[3,64]{1,0:T(4,128)}, u32[]{:S(2)}) copy-start(f32[3,64]{1,0:T(4,128)} %refs_4_.1) | copy-start | bytes 2308
  0.0 9.2 %collective-permute-start.2 = (s32[2,8]{1,0:T(2,128)}, s32[2,8]{1,0:T(2,128)S(1)}, u32[]{:S(2)}, u32[]{:S(2)}) collective-permute-start(s32[2,8]{1,0:T(2,128)} %bitcast.9), channel_id=1, source_target_pairs={{0,3},{1,2},{2,1},{3,0},{4,7},{5,6},{6,5},{7,4},{8,11},{9,10},{10,... | collective-permute-start | bytes 200 | tf_op jit(solution)/shard_map/ppermute | solution.py:234
  5.1 4.7 %collective-permute-start.1 = (s32[2,8]{1,0:T(2,128)}, s32[2,8]{1,0:T(2,128)S(1)}, u32[]{:S(2)}, u32[]{:S(2)}) collective-permute-start(s32[2,8]{1,0:T(2,128)} %bitcast.10), channel_id=1, source_target_pairs={{0,2},{1,3},{2,0},{3,1},{4,6},{5,7},{6,4},{7,5},{8,10},{9,11},{10,... | collective-permute-start | bytes 200 | tf_op jit(solution)/shard_map/ppermute | solution.py:234
  5.1 4.7 %collective-permute-start = (s32[2,8]{1,0:T(2,128)}, s32[2,8]{1,0:T(2,128)S(1)}, u32[]{:S(2)}, u32[]{:S(2)}) collective-permute-start(s32[2,8]{1,0:T(2,128)} %bitcast.11), channel_id=1, source_target_pairs={{0,1},{1,0},{2,3},{3,2},{4,5},{5,4},{6,7},{7,6},{8,9},{9,8},{10,11... | collective-permute-start | bytes 200 | tf_op jit(solution)/shard_map/ppermute | solution.py:234
  12.4 1.4 %collective-permute-start.3 = (bf16[2,4,64,128]{3,2,1,0:T(8,128)(2,1)S(1)}, bf16[2,4,64,128]{3,2,1,0:T(8,128)(2,1)S(1)}, u32[]{:S(2)}, u32[]{:S(2)}) collective-permute-start(bf16[2,4,64,128]{3,2,1,0:T(8,128)(2,1)S(1)} %get-tuple-element.14), channel_id=1, source_target_pairs={{0,4},{4,0},{8,12},{12,8},{1,5},{5,1},{9,13},{13,9},{2,6},{6,2},{1... | collective-permute-start | bytes 393224 | tf_op jit(solution)/shard_map/ppermute | solution.py:234
  13.8 4.3 %collective-permute-start.4 = (bf16[1,4,64,128]{3,2,1,0:T(8,128)(2,1)S(1)}, bf16[1,4,64,128]{3,2,1,0:T(8,128)(2,1)S(1)}, u32[]{:S(2)}, u32[]{:S(2)}) collective-permute-start(bf16[1,4,64,128]{3,2,1,0:T(8,128)(2,1)S(1)} %slice.29), channel_id=1, source_target_pairs={{0,8},{4,12},{8,0},{12,4},{1,9},{5,13},{9,1},{13,5},{2,10},{6,14},... | collective-permute-start | bytes 196616 | tf_op jit(solution)/shard_map/ppermute | solution.py:234
  18.2 5.6 %collective-permute-start.7 = (bf16[64,128]{1,0:T(8,128)(2,1)S(1)}, bf16[64,128]{1,0:T(8,128)(2,1)S(1)}, u32[]{:S(2)}, u32[]{:S(2)}) collective-permute-start(bf16[64,128]{1,0:T(8,128)(2,1)S(1)} %get-tuple-element.15), channel_id=1, source_target_pairs={{0,3},{1,2},{2,1},{3,0},{4,7},{5,6},{6,5},{7,4},{8,11},{9,10},{10,... | collective-permute-start | bytes 49160 | tf_op jit(solution)/shard_map/ppermute | solution.py:234
  21.5 4.6 %collective-permute-start.6 = (bf16[64,128]{1,0:T(8,128)(2,1)S(1)}, bf16[64,128]{1,0:T(8,128)(2,1)S(1)}, u32[]{:S(2)}, u32[]{:S(2)}) collective-permute-start(bf16[64,128]{1,0:T(8,128)(2,1)S(1)} %get-tuple-element.16), channel_id=1, source_target_pairs={{0,2},{1,3},{2,0},{3,1},{4,6},{5,7},{6,4},{7,5},{8,10},{9,11},{10,... | collective-permute-start | bytes 49160 | tf_op jit(solution)/shard_map/ppermute | solution.py:234
  21.5 4.6 %collective-permute-start.5 = (bf16[64,128]{1,0:T(8,128)(2,1)S(1)}, bf16[64,128]{1,0:T(8,128)(2,1)S(1)}, u32[]{:S(2)}, u32[]{:S(2)}) collective-permute-start(bf16[64,128]{1,0:T(8,128)(2,1)S(1)} %get-tuple-element.17), channel_id=1, source_target_pairs={{0,1},{1,0},{2,3},{3,2},{4,5},{5,4},{6,7},{7,6},{8,9},{9,8},{10,11... | collective-permute-start | bytes 49160 | tf_op jit(solution)/shard_map/ppermute | solution.py:234

commit v3 on v2

--- a/solution.py
+++ b/solution.py
@@ -16,6 +16,16 @@
 GROUP = 16
 CHUNKS = 1
 ROWS = 16
+
+LISTS_ORDER = (0, 2, 3, 1)
+RESULTS_ORDER = (0, 1, 2, 3)
+
+
+def orders(n_tile):
+    if n_tile == 4:
+        return LISTS_ORDER, RESULTS_ORDER
+    return tuple(range(n_tile)), tuple(range(n_tile))
+
 
 two_pi = 2.0 * math.pi
 f32 = jnp.float32
@@ -121,7 +131,7 @@
 
 def parts_kernel(sizes, *refs):
     window, kept, n_tile, n_beam = sizes
-    lists = refs[:n_tile]
+    lists = in_order(refs[:n_tile], orders(n_tile)[0])
     beam_table, row_table, spectra, keep, send, coeff, waves = refs[n_tile:]
     share = kept // n_beam
     beams = spectra.shape[0]
@@ -190,7 +200,7 @@
 def result_kernel(sizes, all_beams, *refs):
     window, kept, n_tile, n_beam = sizes
     probes, turn = refs[:2]
-    blocks = refs[2 : 2 + n_tile]
+    blocks = in_order(refs[2 : 2 + n_tile], orders(n_tile)[1])
     out, staged, intensity = refs[2 + n_tile :]
     share = kept // n_beam
     count = probes.shape[1]
@@ -199,13 +209,16 @@
         block = blocks[k][...].astype(f32)
         for s in range(PER_LIST):
             staged[k * PER_LIST + s] = block[s * share : (s + 1) * share]
+    def place(tile):
+        return jnp.where(tile < me_tile, tile + n_tile, tile) - me_tile
+
     tiles = [window_start(probes[0, j], window, window * n_tile)[0] for j in range(count)]
     for j in range(count):
         slot = sum([(tiles[i] == tiles[j]).astype(i32) for i in range(j)], i32(0))
         following = jnp.where(tiles[j] == n_tile - 1, 0, tiles[j] + 1)
         field = (
-            staged[jnp.bitwise_xor(tiles[j], me_tile) * PER_LIST + slot]
-            + staged[jnp.bitwise_xor(following, me_tile) * PER_LIST + CAP + slot]
+            staged[place(tiles[j]) * PER_LIST + slot]
+            + staged[place(following) * PER_LIST + CAP + slot]
         )
         field = field * turn[0, j] + times_i(field) * turn[1, j]
         intensity[j * share : (j + 1) * share, :] = field * field
@@ -234,6 +247,18 @@
     return lax.ppermute(array, axis, [(i, i ^ by) for i in range(lax.axis_size(axis))])
 
 
+def shifted(arrays, way, order):
+    size = lax.axis_size("tile")
+    return [
+        lax.ppermute(arrays[k], "tile", [(i, (i + way * k) % size) for i in range(size)]) if k else arrays[0]
+        for k in order
+    ]
+
+
+def in_order(refs, order):
+    return [refs[order.index(k)] for k in range(len(order))]
+
+
 def per_device(smatrix, beam_table, probes):
     _, beams, window, _ = smatrix.shape
     kept = window // 2
@@ -245,7 +270,8 @@
     count = probes.shape[0]
 
     probes = probes.T
-    lists = [probes] + [swapped(probes, "tile", k) for k in range(1, n_tile)]
+    lists_order, results_order = orders(n_tile)
+    lists = shifted([probes] * n_tile, 1, lists_order)
 
     spectra, row_table, turn = pl.pallas_call(
         functools.partial(spectra_kernel, sizes),
@@ -294,7 +320,7 @@
         middle = total.shape[0] // 2
         keep, send = total[:middle], total[middle:]
     mine = total[0]
-    blocks = [mine[0]] + [swapped(mine[k], "tile", k) for k in range(1, n_tile)]
+    blocks = shifted(mine, -1, results_order)
 
     return pl.pallas_call(
         functools.partial(result_kernel, sizes, beams * n_beam),

time: 27.8 us -> 26.2 us (0.942)
  waiting for transfers between devices: 8.14 us -> 5.77 us
  starting transfers between devices: 11.8 us -> 12.6 us
    ppermute x0 -> x6, starting transfers between devices: none -> 10.8 us  [shifted(): lax.ppermute(arrays[k], 'tile', [(i, (i + way * k) % size) for i in range...]
    ppermute x8 -> x2, starting transfers between devices: 11.8 us -> 1.8 us  [swapped(): lax.ppermute(array, axis, [(i, i ^ by) for i in range(lax.axis_size(axis))])]
    ppermute x8 -> x2, waiting for transfers between devices: 8.14 us -> 3.94 us  [swapped(): lax.ppermute(array, axis, [(i, i ^ by) for i in range(lax.axis_size(axis))])]
    ppermute x0 -> x6, waiting for transfers between devices: none -> 1.83 us  [shifted(): lax.ppermute(arrays[k], 'tile', [(i, (i + way * k) % size) for i in range...]
  transfers between devices with their start and end apart: 8 -> 8, of which waited for: 5 -> 6; matrix products, arithmetic and copies ran while one was open for 0% -> 0% of each run, Pallas kernels for 13% -> 13%
where the time goes in v3:
time: 26.2 us; the launch traced here: 26.1 us
  starting transfers between devices  12.6 us (48%)
  Pallas kernels  7.57 us (29%)
  waiting for transfers between devices  5.77 us (22%)
    ppermute x6, starting transfers between devices, shifted(): lax.ppermute(arrays[k], 'tile', [(i, (i + way * k) % size) for i in range...  10.8 us
    ppermute x2, waiting for transfers between devices, swapped(): lax.ppermute(array, axis, [(i, i ^ by) for i in range(lax.axis_size(axis))])  3.94 us
    pallas_call x1, Pallas kernels, per_device(): pl.pallas_call(functools.partial(spectra_kernel, sizes), in_specs=[HBM, H...  3.46 us
    pallas_call x1, Pallas kernels, per_device(): pl.pallas_call(functools.partial(parts_kernel, sizes), in_specs=[SMEM] *...  2.61 us
    ppermute x6, waiting for transfers between devices, shifted(): lax.ppermute(arrays[k], 'tile', [(i, (i + way * k) % size) for i in range...  1.83 us
    ppermute x2, starting transfers between devices, swapped(): lax.ppermute(array, axis, [(i, i ^ by) for i in range(lax.axis_size(axis))])  1.8 us
    pallas_call x1, Pallas kernels, per_device(): pl.pallas_call(functools.partial(result_kernel, sizes, beams * n_beam), i...  1.5 us
  transfers between devices with their start and end apart: 8, of which 6 were waited for; matrix products, arithmetic and copies ran while one was open for 0% of the time, Pallas kernels for 13%

profile of v3, /device:TPU:0, one launch (start us, length us, event | category | flops | bytes accessed | tf_op | source)
XLA Modules:
  0.0 26.1 jit_solution(3945298383419655214)
XLA Ops:
  0.0 0.0 copy-start
  0.0 0.0 copy-start.1
  0.0 3.0 %collective-permute-start.2 = (s32[2,8]{1,0:T(2,128)}, s32[2,8]{1,0:T(2,128)S(1)}, u32[]{:S(2)}, u32[]{:S(2)}) collective-permute-start(s32[2,8]{1,0:T(2,128)} %bitcast.9), channel_id=1, source_target_pairs={{0,1},{1,2},{2,3},{3,0},{4,5},{5,6},{6,7},{7,4},{8,9},{9,10},{10,1... | collective-permute-start | bytes 200 | tf_op jit(solution)/shard_map/ppermute | solution.py:253
  3.0 2.1 %collective-permute-start.1 = (s32[2,8]{1,0:T(2,128)}, s32[2,8]{1,0:T(2,128)S(1)}, u32[]{:S(2)}, u32[]{:S(2)}) collective-permute-start(s32[2,8]{1,0:T(2,128)} %bitcast.10), channel_id=1, source_target_pairs={{0,3},{1,0},{2,1},{3,2},{4,7},{5,4},{6,5},{7,6},{8,11},{9,8},{10,9... | collective-permute-start | bytes 200 | tf_op jit(solution)/shard_map/ppermute | solution.py:253
  5.1 1.0 %collective-permute-start = (s32[2,8]{1,0:T(2,128)}, s32[2,8]{1,0:T(2,128)S(1)}, u32[]{:S(2)}, u32[]{:S(2)}) collective-permute-start(s32[2,8]{1,0:T(2,128)} %bitcast.11), channel_id=1, source_target_pairs={{0,2},{1,3},{2,0},{3,1},{4,6},{5,7},{6,4},{7,5},{8,10},{9,11},{10,... | collective-permute-start | bytes 200 | tf_op jit(solution)/shard_map/ppermute | solution.py:253
  6.1 3.5 %spectra.1 = (bf16[64,128,128]{2,1,0:T(8,128)(2,1)S(1)}, bf16[128,256]{1,0:T(8,128)(2,1)S(1)}, f32[2,8,16,128]{3,2,1,0:T(8,128)S(1)}) custom-call(s32[2,8]{1,0:T(2,128)} %bitcast.12, bf16[2,64,128,128]{3,2,1,0:T(8,128)(2,1)} %smatrix_hbm.1), custom_call_target="tpu_custom_call" | custom-call | flops 536870912 | bytes 6291456 | tf_op jit(solution)/shard_map/spectra/pallas_call | solution.py:276
  9.5 0.0 collective-permute-done.2.refs_3_
  9.5 0.0 collective-permute-done.1.refs_2_
  9.6 0.2 collective-permute-done.refs_1_
  9.8 0.0 copy-done
  9.8 0.0 copy-done.1
  9.8 2.6 %parts.1 = (bf16[2,4,64,128]{3,2,1,0:T(8,128)(2,1)S(1)}, bf16[2,4,64,128]{3,2,1,0:T(8,128)(2,1)S(1)}) custom-call(s32[2,8]{1,0:T(2,128)S(1)} %bitcast.13, s32[2,8]{1,0:T(2,128)S(1)} %collective-permute-done.refs_1_, s32[2,8]{1,0:T(2,128)S(1)} %collective-permute-done.1.refs_2_, s32[2,8]{1,0:T(2,128)S(1)} %collective-permute-done.2.refs_3_, ...), custom_call_target="tpu_custom_call" | custom-call | flops 1073741824 | bytes 4194304 | tf_op jit(solution)/shard_map/parts/pallas_call | solution.py:299
  12.4 0.1 collective-permute-start.3
  12.5 1.3 %collective-permute-done.3 = bf16[2,4,64,128]{3,2,1,0:T(8,128)(2,1)S(1)} collective-permute-done((bf16[2,4,64,128]{3,2,1,0:T(8,128)(2,1)S(1)}, bf16[2,4,64,128]{3,2,1,0:T(8,128)(2,1)S(1)}, u32[]{:S(2)}, u32[]{:S(2)}) %collective-permute-start.3) | collective-permute-done | bytes 131104 | tf_op jit(solution)/shard_map/ppermute | solution.py:247
  13.9 1.7 %collective-permute-start.4 = (bf16[1,4,64,128]{3,2,1,0:T(8,128)(2,1)S(1)}, bf16[1,4,64,128]{3,2,1,0:T(8,128)(2,1)S(1)}, u32[]{:S(2)}, u32[]{:S(2)}) collective-permute-start(bf16[1,4,64,128]{3,2,1,0:T(8,128)(2,1)S(1)} %slice.29), channel_id=1, source_target_pairs={{0,8},{4,12},{8,0},{12,4},{1,9},{5,13},{9,1},{13,5},{2,10},{6,14},... | collective-permute-start | bytes 196616 | tf_op jit(solution)/shard_map/ppermute | solution.py:247
  15.6 2.6 %collective-permute-done.4 = bf16[1,4,64,128]{3,2,1,0:T(8,128)(2,1)S(1)} collective-permute-done((bf16[1,4,64,128]{3,2,1,0:T(8,128)(2,1)S(1)}, bf16[1,4,64,128]{3,2,1,0:T(8,128)(2,1)S(1)}, u32[]{:S(2)}, u32[]{:S(2)}) %collective-permute-start.4) | collective-permute-done | bytes 65568 | tf_op jit(solution)/shard_map/ppermute | solution.py:247
  18.3 1.4 %collective-permute-start.7 = (bf16[64,128]{1,0:T(8,128)(2,1)S(1)}, bf16[64,128]{1,0:T(8,128)(2,1)S(1)}, u32[]{:S(2)}, u32[]{:S(2)}) collective-permute-start(bf16[64,128]{1,0:T(8,128)(2,1)S(1)} %get-tuple-element.15), channel_id=1, source_target_pairs={{0,1},{1,2},{2,3},{3,0},{4,5},{5,6},{6,7},{7,4},{8,9},{9,10},{10,1... | collective-permute-start | bytes 49160 | tf_op jit(solution)/shard_map/ppermute | solution.py:253
  19.7 1.2 %collective-permute-start.6 = (bf16[64,128]{1,0:T(8,128)(2,1)S(1)}, bf16[64,128]{1,0:T(8,128)(2,1)S(1)}, u32[]{:S(2)}, u32[]{:S(2)}) collective-permute-start(bf16[64,128]{1,0:T(8,128)(2,1)S(1)} %get-tuple-element.16), channel_id=1, source_target_pairs={{0,2},{1,3},{2,0},{3,1},{4,6},{5,7},{6,4},{7,5},{8,10},{9,11},{10,... | collective-permute-start | bytes 49160 | tf_op jit(solution)/shard_map/ppermute | solution.py:253
  20.8 2.1 %collective-permute-start.5 = (bf16[64,128]{1,0:T(8,128)(2,1)S(1)}, bf16[64,128]{1,0:T(8,128)(2,1)S(1)}, u32[]{:S(2)}, u32[]{:S(2)}) collective-permute-start(bf16[64,128]{1,0:T(8,128)(2,1)S(1)} %get-tuple-element.17), channel_id=1, source_target_pairs={{0,3},{1,0},{2,1},{3,2},{4,7},{5,4},{6,5},{7,6},{8,11},{9,8},{10,9... | collective-permute-start | bytes 49160 | tf_op jit(solution)/shard_map/ppermute | solution.py:253
  23.0 0.9 %collective-permute-done.7.refs_5_ = bf16[64,128]{1,0:T(8,128)(2,1)S(1)} collective-permute-done((bf16[64,128]{1,0:T(8,128)(2,1)S(1)}, bf16[64,128]{1,0:T(8,128)(2,1)S(1)}, u32[]{:S(2)}, u32[]{:S(2)}) %collective-permute-start.7) | collective-permute-done | bytes 16416 | tf_op jit(solution)/shard_map/ppermute | solution.py:253
  23.8 0.5 %collective-permute-done.6.refs_4_ = bf16[64,128]{1,0:T(8,128)(2,1)S(1)} collective-permute-done((bf16[64,128]{1,0:T(8,128)(2,1)S(1)}, bf16[64,128]{1,0:T(8,128)(2,1)S(1)}, u32[]{:S(2)}, u32[]{:S(2)}) %collective-permute-start.6) | collective-permute-done | bytes 16416 | tf_op jit(solution)/shard_map/ppermute | solution.py:253
  24.3 0.3 %collective-permute-done.5.refs_3_ = bf16[64,128]{1,0:T(8,128)(2,1)S(1)} collective-permute-done((bf16[64,128]{1,0:T(8,128)(2,1)S(1)}, bf16[64,128]{1,0:T(8,128)(2,1)S(1)}, u32[]{:S(2)}, u32[]{:S(2)}) %collective-permute-start.5) | collective-permute-done | bytes 16416 | tf_op jit(solution)/shard_map/ppermute | solution.py:253
  24.6 1.5 %result.1 = f32[8,8,32]{2,1,0:T(8,128)} custom-call(s32[2,8]{1,0:T(2,128)S(1)} %bitcast.14, f32[2,8,16,128]{3,2,1,0:T(8,128)S(1)} %get-tuple-element.10.refs_1_, bf16[64,128]{1,0:T(8,128)(2,1)S(1)} %get-tuple-element.18.refs_2_, bf16[64,128]{1,0:T(8,128)(2,1)S(1)} %collective-permute-done.5.refs_3_, bf16[64,128]{1,0:T(8,128)(2,1)S(1)} %collective-permute-done.6.refs_4_, ...), custom_call_target="tpu_custom_call" | custom-call | tf_op jit(solution)/shard_map/result/pallas_call | solution.py:325
  (4 shorter events, 0.1 us)
Async XLA Ops:
  0.0 9.8 %copy-start = (s32[8,2]{0,1:T(2,128)S(1)}, s32[8,2]{0,1:T(2,128)}, u32[]{:S(2)}) copy-start(s32[8,2]{0,1:T(2,128)} %param.5) | copy-start | bytes 196
  0.0 9.8 %copy-start.1 = (f32[3,64]{1,0:T(4,128)S(1)}, f32[3,64]{1,0:T(4,128)}, u32[]{:S(2)}) copy-start(f32[3,64]{1,0:T(4,128)} %refs_4_.1) | copy-start | bytes 2308
  0.0 9.5 %collective-permute-start.2 = (s32[2,8]{1,0:T(2,128)}, s32[2,8]{1,0:T(2,128)S(1)}, u32[]{:S(2)}, u32[]{:S(2)}) collective-permute-start(s32[2,8]{1,0:T(2,128)} %bitcast.9), channel_id=1, source_target_pairs={{0,1},{1,2},{2,3},{3,0},{4,5},{5,6},{6,7},{7,4},{8,9},{9,10},{10,1... | collective-permute-start | bytes 200 | tf_op jit(solution)/shard_map/ppermute | solution.py:253
  3.0 6.5 %collective-permute-start.1 = (s32[2,8]{1,0:T(2,128)}, s32[2,8]{1,0:T(2,128)S(1)}, u32[]{:S(2)}, u32[]{:S(2)}) collective-permute-start(s32[2,8]{1,0:T(2,128)} %bitcast.10), channel_id=1, source_target_pairs={{0,3},{1,0},{2,1},{3,2},{4,7},{5,4},{6,5},{7,6},{8,11},{9,8},{10,9... | collective-permute-start | bytes 200 | tf_op jit(solution)/shard_map/ppermute | solution.py:253
  5.1 4.7 %collective-permute-start = (s32[2,8]{1,0:T(2,128)}, s32[2,8]{1,0:T(2,128)S(1)}, u32[]{:S(2)}, u32[]{:S(2)}) collective-permute-start(s32[2,8]{1,0:T(2,128)} %bitcast.11), channel_id=1, source_target_pairs={{0,2},{1,3},{2,0},{3,1},{4,6},{5,7},{6,4},{7,5},{8,10},{9,11},{10,... | collective-permute-start | bytes 200 | tf_op jit(solution)/shard_map/ppermute | solution.py:253
  12.4 1.4 %collective-permute-start.3 = (bf16[2,4,64,128]{3,2,1,0:T(8,128)(2,1)S(1)}, bf16[2,4,64,128]{3,2,1,0:T(8,128)(2,1)S(1)}, u32[]{:S(2)}, u32[]{:S(2)}) collective-permute-start(bf16[2,4,64,128]{3,2,1,0:T(8,128)(2,1)S(1)} %get-tuple-element.14), channel_id=1, source_target_pairs={{0,4},{4,0},{8,12},{12,8},{1,5},{5,1},{9,13},{13,9},{2,6},{6,2},{1... | collective-permute-start | bytes 393224 | tf_op jit(solution)/shard_map/ppermute | solution.py:247
  13.9 4.3 %collective-permute-start.4 = (bf16[1,4,64,128]{3,2,1,0:T(8,128)(2,1)S(1)}, bf16[1,4,64,128]{3,2,1,0:T(8,128)(2,1)S(1)}, u32[]{:S(2)}, u32[]{:S(2)}) collective-permute-start(bf16[1,4,64,128]{3,2,1,0:T(8,128)(2,1)S(1)} %slice.29), channel_id=1, source_target_pairs={{0,8},{4,12},{8,0},{12,4},{1,9},{5,13},{9,1},{13,5},{2,10},{6,14},... | collective-permute-start | bytes 196616 | tf_op jit(solution)/shard_map/ppermute | solution.py:247
  18.3 5.6 %collective-permute-start.7 = (bf16[64,128]{1,0:T(8,128)(2,1)S(1)}, bf16[64,128]{1,0:T(8,128)(2,1)S(1)}, u32[]{:S(2)}, u32[]{:S(2)}) collective-permute-start(bf16[64,128]{1,0:T(8,128)(2,1)S(1)} %get-tuple-element.15), channel_id=1, source_target_pairs={{0,1},{1,2},{2,3},{3,0},{4,5},{5,6},{6,7},{7,4},{8,9},{9,10},{10,1... | collective-permute-start | bytes 49160 | tf_op jit(solution)/shard_map/ppermute | solution.py:253
  19.7 4.6 %collective-permute-start.6 = (bf16[64,128]{1,0:T(8,128)(2,1)S(1)}, bf16[64,128]{1,0:T(8,128)(2,1)S(1)}, u32[]{:S(2)}, u32[]{:S(2)}) collective-permute-start(bf16[64,128]{1,0:T(8,128)(2,1)S(1)} %get-tuple-element.16), channel_id=1, source_target_pairs={{0,2},{1,3},{2,0},{3,1},{4,6},{5,7},{6,4},{7,5},{8,10},{9,11},{10,... | collective-permute-start | bytes 49160 | tf_op jit(solution)/shard_map/ppermute | solution.py:253
  20.8 3.7 %collective-permute-start.5 = (bf16[64,128]{1,0:T(8,128)(2,1)S(1)}, bf16[64,128]{1,0:T(8,128)(2,1)S(1)}, u32[]{:S(2)}, u32[]{:S(2)}) collective-permute-start(bf16[64,128]{1,0:T(8,128)(2,1)S(1)} %get-tuple-element.17), channel_id=1, source_target_pairs={{0,3},{1,0},{2,1},{3,2},{4,7},{5,4},{6,5},{7,6},{8,11},{9,8},{10,9... | collective-permute-start | bytes 49160 | tf_op jit(solution)/shard_map/ppermute | solution.py:253

commit v4 on v3

--- a/solution.py
+++ b/solution.py
@@ -57,10 +57,11 @@
     return pltpu.roll(pairs, LANES // 2, pairs.ndim - 1)
 
 
-def spectra_kernel(sizes, probes_hbm, smatrix_hbm, spectra, row_table, turn, column_table, smatrix, probes, sems):
+def spectra_kernel(sizes, probes_hbm, smatrix_hbm, spectra, row_table, turn, select, column_table, smatrix, probes, sems):
     window, kept, n_tile, n_beam = sizes
     share = kept // n_beam
     me_beam = lax.axis_index("beam")
+    me_tile = lax.axis_index("tile")
     planes = smatrix.shape[1] // CHUNKS
     chunks = [pl.ds(i * planes, planes) for i in range(CHUNKS)]
     copies = [
@@ -94,12 +95,26 @@
     lane = iota((share, LANES), 1)
     v = lane % kept - kept // 2
     listed.wait()
+    shape = (select.shape[0], select.shape[1])
+    window_of, slot_of = iota(shape, 0) // share, iota(shape, 1) // share
+    wanted = (slot_of == -1, slot_of == -1)
+    tiles = []
     for j in range(probes.shape[1]):
-        _, offset = window_start(probes[0, j], window, window * n_tile)
+        tile, offset = window_start(probes[0, j], window, window * n_tile)
+        following = jnp.where(tile == n_tile - 1, 0, tile + 1)
+        rank = sum([(t == tile).astype(i32) for t in tiles], i32(0))
+        tiles.append(tile)
+        spots = [
+            (jnp.where(t < me_tile, t + n_tile, t) - me_tile) * PER_LIST + base + rank
+            for t, base in ((tile, 0), (following, CAP))
+        ]
+        wanted = [w | ((window_of == j) & (slot_of == spot)) for w, spot in zip(wanted, spots)]
         shift = jnp.right_shift(probes[1, j], 2) - window // 2
         angle = turns(u * offset + v * shift, window)
-        turn[0, j] = jnp.cos(angle)
-        turn[1, j] = jnp.where(lane < kept, -jnp.sin(angle), jnp.sin(angle))
+        turn[0, j * share : (j + 1) * share, :] = jnp.cos(angle)
+        turn[1, j * share : (j + 1) * share, :] = jnp.where(lane < kept, -jnp.sin(angle), jnp.sin(angle))
+    same_line = iota(shape, 0) % share == iota(shape, 1) % share
+    select[...] = jnp.where((wanted[0] | wanted[1]) & same_line, 1.0, 0.0).astype(bf16)
 
     for copy, chunk in zip(copies, chunks):
         copy.wait()
@@ -109,24 +124,26 @@
 
 
 def chosen(lists, me_tile, window, n_tile):
+    shape = (n_tile * PER_LIST, lists[0].shape[1])
+    slot, item = iota(shape, 0), iota(shape, 1)
+    rows = jnp.zeros(shape, i32)
+    columns = jnp.zeros(shape, i32)
+    for n, probes in enumerate(lists):
+        here = slot // PER_LIST == n
+        rows = jnp.where(here, probes[0:1, :], rows)
+        columns = jnp.where(here, probes[1:2, :], columns)
+    tile, _ = window_start(rows, window, window * n_tile)
     before = jnp.where(me_tile == 0, n_tile - 1, me_tile - 1)
-    rows, columns = [], []
-    for probes in lists:
-        picked = [[i32(0), i32(0)] for _ in range(PER_LIST)]
-        seen = [i32(0), i32(0)]
-        for j in range(probes.shape[1]):
-            row, column = probes[0, j], probes[1, j]
-            tile, _ = window_start(row, window, window * n_tile)
-            for which, wanted in enumerate((me_tile, before)):
-                match = tile == wanted
-                for slot in range(CAP):
-                    take = match & (seen[which] == slot)
-                    held = picked[which * CAP + slot]
-                    picked[which * CAP + slot] = [jnp.where(take, row, held[0]), jnp.where(take, column, held[1])]
-                seen[which] = seen[which] + match.astype(i32)
-        rows += [p[0] for p in picked]
-        columns += [p[1] for p in picked]
-    return rows, columns
+    match = tile == jnp.where(slot % PER_LIST < CAP, me_tile, before)
+    item = item.astype(f32)
+    nothing = float(shape[1])
+    left = jnp.where(match, item, nothing)
+    picked = jnp.min(left, axis=1, keepdims=True)
+    for n in range(1, CAP):
+        left = jnp.where(left == picked, nothing, left)
+        picked = jnp.where(slot[:, :1] % CAP >= n, jnp.min(left, axis=1, keepdims=True), picked)
+    hit = item == picked
+    return [jnp.sum(jnp.where(hit, x.astype(f32), 0.0), axis=1, keepdims=True) for x in (rows, columns)]
 
 
 def parts_kernel(sizes, *refs):
@@ -138,14 +155,9 @@
     slots = n_tile * PER_LIST
     wide = beams * ROWS
     me_tile = lax.axis_index("tile")
-    rows, columns = chosen(lists, me_tile, window, n_tile)
-    offsets = [window_start(row, window, window * n_tile)[1] for row in rows]
-    which = iota((slots, 1), 0)
-    row_v = jnp.zeros((slots, 1), f32)
-    column_v = jnp.zeros((slots, 1), f32)
-    for s in range(slots):
-        row_v = jnp.where(which == s, rows[s].astype(f32), row_v)
-        column_v = jnp.where(which == s, columns[s].astype(f32), column_v)
+    row_v, column_v = chosen(lists, me_tile, window, n_tile)
+    offsets = jnp.bitwise_and(jnp.right_shift(row_v.astype(i32), 2) - window // 2, window - 1)
+    offsets = jnp.broadcast_to(offsets, (slots, LANES))
     phase = beam_table[2:3, :] + two_pi / (window * IF) * (
         beam_table[0:1, :] * row_v + beam_table[1:2, :] * column_v
     )
@@ -170,7 +182,7 @@
             for h in range(2):
                 y_here = y_in + (y + h * ROWS)
                 for p in range(GROUP):
-                    offset = offsets[first + p]
+                    offset = offsets[first + p : first + p + 1, :]
                     starts_here = p % PER_LIST < CAP
                     inside = y_here >= offset if starts_here else y_here < offset
                     for c in range(2):
@@ -199,44 +211,30 @@
 
 def result_kernel(sizes, all_beams, *refs):
     window, kept, n_tile, n_beam = sizes
-    probes, turn = refs[:2]
+    turn, select = refs[:2]
     blocks = in_order(refs[2 : 2 + n_tile], orders(n_tile)[1])
-    out, staged, intensity = refs[2 + n_tile :]
-    share = kept // n_beam
-    count = probes.shape[1]
-    me_tile = lax.axis_index("tile")
-    for k in range(n_tile):
-        block = blocks[k][...].astype(f32)
-        for s in range(PER_LIST):
-            staged[k * PER_LIST + s] = block[s * share : (s + 1) * share]
-    def place(tile):
-        return jnp.where(tile < me_tile, tile + n_tile, tile) - me_tile
-
-    tiles = [window_start(probes[0, j], window, window * n_tile)[0] for j in range(count)]
-    for j in range(count):
-        slot = sum([(tiles[i] == tiles[j]).astype(i32) for i in range(j)], i32(0))
-        following = jnp.where(tiles[j] == n_tile - 1, 0, tiles[j] + 1)
-        field = (
-            staged[place(tiles[j]) * PER_LIST + slot]
-            + staged[place(following) * PER_LIST + CAP + slot]
-        )
-        field = field * turn[0, j] + times_i(field) * turn[1, j]
-        intensity[j * share : (j + 1) * share, :] = field * field
-    height = count * share // BIN
+    out, intensity = refs[2 + n_tile :]
+    height = select.shape[0] // BIN
+    shape = (2 * LANES, kept // BIN)
+    bins = (iota(shape, 0) % kept // BIN == iota(shape, 1)).astype(f32).astype(bf16)
+    arrived = jnp.concatenate([block[...] for block in blocks], axis=0)
+    field = jnp.dot(select[...], arrived, preferred_element_type=f32)
+    field = field * turn[0] + times_i(field) * turn[1]
+    intensity[...] = field * field
     summed = intensity[pl.ds(0, height, stride=BIN), :]
     for b in range(1, BIN):
         summed = summed + intensity[pl.ds(b, height, stride=BIN), :]
-    shape = (LANES, kept // BIN)
-    bins = (iota(shape, 0) % kept // BIN == iota(shape, 1)).astype(f32)
-    binned = jnp.dot(summed, bins, precision=lax.Precision.HIGHEST, preferred_element_type=f32)
+    high = summed.astype(bf16)
+    low = (summed - high.astype(f32)).astype(bf16)
+    binned = jnp.dot(jnp.concatenate([high, low], axis=1), bins, preferred_element_type=f32)
     binned = binned * (1.0 / (BIN * BIN * window * window * all_beams))
-    for j in range(count):
-        out[j] = binned[j * (share // BIN) : (j + 1) * (share // BIN)]
+    each = height // out.shape[0]
+    for j in range(out.shape[0]):
+        out[j] = binned[j * each : (j + 1) * each]
 
 
 VMEM = pl.BlockSpec(memory_space=pltpu.VMEM)
 HBM = pl.BlockSpec(memory_space=pltpu.HBM)
-SMEM = pl.BlockSpec(memory_space=pltpu.SMEM)
 
 
 def params(mib=16):
@@ -273,14 +271,15 @@
     lists_order, results_order = orders(n_tile)
     lists = shifted([probes] * n_tile, 1, lists_order)
 
-    spectra, row_table, turn = pl.pallas_call(
+    spectra, row_table, turn, select = pl.pallas_call(
         functools.partial(spectra_kernel, sizes),
         in_specs=[HBM, HBM],
-        out_specs=[VMEM] * 3,
+        out_specs=[VMEM] * 4,
         out_shape=[
             jax.ShapeDtypeStruct((beams, window, 2 * kept), bf16),
             jax.ShapeDtypeStruct((2 * kept, 2 * window), bf16),
-            jax.ShapeDtypeStruct((2, count, share, LANES), f32),
+            jax.ShapeDtypeStruct((2, count * share, LANES), f32),
+            jax.ShapeDtypeStruct((count * share, slots * share), bf16),
         ],
         scratch_shapes=[
             pltpu.VMEM((2 * window, 2 * kept), bf16),
@@ -298,7 +297,7 @@
     half = jax.ShapeDtypeStruct((n_beam // 2, n_tile, PER_LIST * share, LANES), bf16)
     keep, send = pl.pallas_call(
         functools.partial(parts_kernel, sizes),
-        in_specs=[SMEM] * n_tile + [VMEM] * 3,
+        in_specs=[VMEM] * (n_tile + 3),
         out_specs=[VMEM] * 2,
         out_shape=[half, half],
         scratch_shapes=[
@@ -324,13 +323,13 @@
 
     return pl.pallas_call(
         functools.partial(result_kernel, sizes, beams * n_beam),
-        in_specs=[SMEM] + [VMEM] * (1 + n_tile),
+        in_specs=[VMEM] * (2 + n_tile),
         out_specs=VMEM,
         out_shape=jax.ShapeDtypeStruct((count, share // BIN, kept // BIN), f32),
-        scratch_shapes=[pltpu.VMEM((slots, share, LANES), f32), pltpu.VMEM((count * share, LANES), f32)],
+        scratch_shapes=[pltpu.VMEM((count * share, LANES), f32)],
         compiler_params=params(),
         name="result",
-    )(probes, turn, *blocks)
+    )(turn, select, *blocks)
 
 
 def solution(mesh):

time: 26.2 us -> 25.1 us (0.958)
  Pallas kernels: 7.57 us -> 6.42 us
    pallas_call x1, Pallas kernels: 2.61 us -> 1.97 us  [per_device(): pl.pallas_call(functools.partial(parts_kernel, sizes), in_specs=[VMEM] *...]
    pallas_call x1, Pallas kernels: 1.5 us -> 0.99 us  [per_device(): pl.pallas_call(functools.partial(result_kernel, sizes, beams * n_beam), i...]
  transfers between devices with their start and end apart: 8 -> 8, of which waited for: 6 -> 6; matrix products, arithmetic and copies ran while one was open for 0% -> 0% of each run, Pallas kernels for 13% -> 14%
where the time goes in v4:
time: 25.1 us; the launch traced here: 24.9 us
  starting transfers between devices  12.6 us (50%)
  Pallas kernels  6.42 us (26%)
  waiting for transfers between devices  5.77 us (23%)
    ppermute x6, starting transfers between devices, shifted(): lax.ppermute(arrays[k], 'tile', [(i, (i + way * k) % size) for i in range...  10.8 us
    ppermute x2, waiting for transfers between devices, swapped(): lax.ppermute(array, axis, [(i, i ^ by) for i in range(lax.axis_size(axis))])  3.95 us
    pallas_call x1, Pallas kernels, per_device(): pl.pallas_call(functools.partial(spectra_kernel, sizes), in_specs=[HBM, H...  3.46 us
    pallas_call x1, Pallas kernels, per_device(): pl.pallas_call(functools.partial(parts_kernel, sizes), in_specs=[VMEM] *...  1.97 us
    ppermute x6, waiting for transfers between devices, shifted(): lax.ppermute(arrays[k], 'tile', [(i, (i + way * k) % size) for i in range...  1.82 us
    ppermute x2, starting transfers between devices, swapped(): lax.ppermute(array, axis, [(i, i ^ by) for i in range(lax.axis_size(axis))])  1.79 us
    pallas_call x1, Pallas kernels, per_device(): pl.pallas_call(functools.partial(result_kernel, sizes, beams * n_beam), i...  0.99 us
  transfers between devices with their start and end apart: 8, of which 6 were waited for; matrix products, arithmetic and copies ran while one was open for 0% of the time, Pallas kernels for 14%

profile of v4, /device:TPU:0, one launch (start us, length us, event | category | flops | bytes accessed | tf_op | source)
XLA Modules:
  0.0 24.9 jit_solution(7199201200999082945)
XLA Ops:
  0.0 0.0 copy-start
  0.0 0.0 copy-start.1
  0.0 3.0 %collective-permute-start.2 = (s32[2,8]{1,0:T(2,128)}, s32[2,8]{1,0:T(2,128)S(1)}, u32[]{:S(2)}, u32[]{:S(2)}) collective-permute-start(s32[2,8]{1,0:T(2,128)} %bitcast.9), channel_id=1, source_target_pairs={{0,1},{1,2},{2,3},{3,0},{4,5},{5,6},{6,7},{7,4},{8,9},{9,10},{10,1... | collective-permute-start | bytes 200 | tf_op jit(solution)/shard_map/ppermute | solution.py:251
  3.0 2.1 %collective-permute-start.1 = (s32[2,8]{1,0:T(2,128)}, s32[2,8]{1,0:T(2,128)S(1)}, u32[]{:S(2)}, u32[]{:S(2)}) collective-permute-start(s32[2,8]{1,0:T(2,128)} %bitcast.10), channel_id=1, source_target_pairs={{0,3},{1,0},{2,1},{3,2},{4,7},{5,4},{6,5},{7,6},{8,11},{9,8},{10,9... | collective-permute-start | bytes 200 | tf_op jit(solution)/shard_map/ppermute | solution.py:251
  5.1 1.0 %collective-permute-start = (s32[2,8]{1,0:T(2,128)}, s32[2,8]{1,0:T(2,128)S(1)}, u32[]{:S(2)}, u32[]{:S(2)}) collective-permute-start(s32[2,8]{1,0:T(2,128)} %bitcast.11), channel_id=1, source_target_pairs={{0,2},{1,3},{2,0},{3,1},{4,6},{5,7},{6,4},{7,5},{8,10},{9,11},{10,... | collective-permute-start | bytes 200 | tf_op jit(solution)/shard_map/ppermute | solution.py:251
  6.1 3.5 %spectra.1 = (bf16[64,128,128]{2,1,0:T(8,128)(2,1)S(1)}, bf16[128,256]{1,0:T(8,128)(2,1)S(1)}, f32[2,128,128]{2,1,0:T(8,128)S(1)}, bf16[128,256]{1,0:T(8,128)(2,1)S(1)}) custom-call(s32[2,8]{1,0:T(2,128)} %bitcast.12, bf16[2,64,128,128]{3,2,1,0:T(8,128)(2,1)} %smatrix_hbm.1), custom_call_target="tpu_custom_call" | custom-call | flops 536870912 | bytes 6291456 | tf_op jit(solution)/shard_map/spectra/pallas_call | solution.py:274
  9.5 0.0 collective-permute-done.2.refs_3_
  9.6 0.0 collective-permute-done.1.refs_2_
  9.6 0.2 collective-permute-done.refs_1_
  9.8 0.0 copy-done
  9.8 0.0 copy-done.1
  9.8 2.0 %parts.1 = (bf16[2,4,64,128]{3,2,1,0:T(8,128)(2,1)S(1)}, bf16[2,4,64,128]{3,2,1,0:T(8,128)(2,1)S(1)}) custom-call(s32[2,8]{1,0:T(2,128)S(1)} %bitcast.13, s32[2,8]{1,0:T(2,128)S(1)} %collective-permute-done.refs_1_, s32[2,8]{1,0:T(2,128)S(1)} %collective-permute-done.1.refs_2_, s32[2,8]{1,0:T(2,128)S(1)} %collective-permute-done.2.refs_3_, ...), custom_call_target="tpu_custom_call" | custom-call | flops 1073741824 | bytes 4194304 | tf_op jit(solution)/shard_map/parts/pallas_call | solution.py:298
  11.8 0.1 collective-permute-start.3
  11.9 1.3 %collective-permute-done.3 = bf16[2,4,64,128]{3,2,1,0:T(8,128)(2,1)S(1)} collective-permute-done((bf16[2,4,64,128]{3,2,1,0:T(8,128)(2,1)S(1)}, bf16[2,4,64,128]{3,2,1,0:T(8,128)(2,1)S(1)}, u32[]{:S(2)}, u32[]{:S(2)}) %collective-permute-start.3) | collective-permute-done | bytes 131104 | tf_op jit(solution)/shard_map/ppermute | solution.py:245
  13.2 1.7 %collective-permute-start.4 = (bf16[1,4,64,128]{3,2,1,0:T(8,128)(2,1)S(1)}, bf16[1,4,64,128]{3,2,1,0:T(8,128)(2,1)S(1)}, u32[]{:S(2)}, u32[]{:S(2)}) collective-permute-start(bf16[1,4,64,128]{3,2,1,0:T(8,128)(2,1)S(1)} %slice.29), channel_id=1, source_target_pairs={{0,8},{4,12},{8,0},{12,4},{1,9},{5,13},{9,1},{13,5},{2,10},{6,14},... | collective-permute-start | bytes 196616 | tf_op jit(solution)/shard_map/ppermute | solution.py:245
  15.0 2.6 %collective-permute-done.4 = bf16[1,4,64,128]{3,2,1,0:T(8,128)(2,1)S(1)} collective-permute-done((bf16[1,4,64,128]{3,2,1,0:T(8,128)(2,1)S(1)}, bf16[1,4,64,128]{3,2,1,0:T(8,128)(2,1)S(1)}, u32[]{:S(2)}, u32[]{:S(2)}) %collective-permute-start.4) | collective-permute-done | bytes 65568 | tf_op jit(solution)/shard_map/ppermute | solution.py:245
  17.6 1.4 %collective-permute-start.7 = (bf16[64,128]{1,0:T(8,128)(2,1)S(1)}, bf16[64,128]{1,0:T(8,128)(2,1)S(1)}, u32[]{:S(2)}, u32[]{:S(2)}) collective-permute-start(bf16[64,128]{1,0:T(8,128)(2,1)S(1)} %get-tuple-element.17), channel_id=1, source_target_pairs={{0,1},{1,2},{2,3},{3,0},{4,5},{5,6},{6,7},{7,4},{8,9},{9,10},{10,1... | collective-permute-start | bytes 49160 | tf_op jit(solution)/shard_map/ppermute | solution.py:251
  19.0 1.2 %collective-permute-start.6 = (bf16[64,128]{1,0:T(8,128)(2,1)S(1)}, bf16[64,128]{1,0:T(8,128)(2,1)S(1)}, u32[]{:S(2)}, u32[]{:S(2)}) collective-permute-start(bf16[64,128]{1,0:T(8,128)(2,1)S(1)} %get-tuple-element.18), channel_id=1, source_target_pairs={{0,2},{1,3},{2,0},{3,1},{4,6},{5,7},{6,4},{7,5},{8,10},{9,11},{10,... | collective-permute-start | bytes 49160 | tf_op jit(solution)/shard_map/ppermute | solution.py:251
  20.2 2.2 %collective-permute-start.5 = (bf16[64,128]{1,0:T(8,128)(2,1)S(1)}, bf16[64,128]{1,0:T(8,128)(2,1)S(1)}, u32[]{:S(2)}, u32[]{:S(2)}) collective-permute-start(bf16[64,128]{1,0:T(8,128)(2,1)S(1)} %get-tuple-element.19), channel_id=1, source_target_pairs={{0,3},{1,0},{2,1},{3,2},{4,7},{5,4},{6,5},{7,6},{8,11},{9,8},{10,9... | collective-permute-start | bytes 49160 | tf_op jit(solution)/shard_map/ppermute | solution.py:251
  22.4 0.9 %collective-permute-done.7.refs_5_ = bf16[64,128]{1,0:T(8,128)(2,1)S(1)} collective-permute-done((bf16[64,128]{1,0:T(8,128)(2,1)S(1)}, bf16[64,128]{1,0:T(8,128)(2,1)S(1)}, u32[]{:S(2)}, u32[]{:S(2)}) %collective-permute-start.7) | collective-permute-done | bytes 16416 | tf_op jit(solution)/shard_map/ppermute | solution.py:251
  23.2 0.5 %collective-permute-done.6.refs_4_ = bf16[64,128]{1,0:T(8,128)(2,1)S(1)} collective-permute-done((bf16[64,128]{1,0:T(8,128)(2,1)S(1)}, bf16[64,128]{1,0:T(8,128)(2,1)S(1)}, u32[]{:S(2)}, u32[]{:S(2)}) %collective-permute-start.6) | collective-permute-done | bytes 16416 | tf_op jit(solution)/shard_map/ppermute | solution.py:251
  23.7 0.3 %collective-permute-done.5.refs_3_ = bf16[64,128]{1,0:T(8,128)(2,1)S(1)} collective-permute-done((bf16[64,128]{1,0:T(8,128)(2,1)S(1)}, bf16[64,128]{1,0:T(8,128)(2,1)S(1)}, u32[]{:S(2)}, u32[]{:S(2)}) %collective-permute-start.5) | collective-permute-done | bytes 16416 | tf_op jit(solution)/shard_map/ppermute | solution.py:251
  23.9 1.0 %result.1 = f32[8,8,32]{2,1,0:T(8,128)} custom-call(f32[2,128,128]{2,1,0:T(8,128)S(1)} %get-tuple-element.11.refs_0_, bf16[128,256]{1,0:T(8,128)(2,1)S(1)} %get-tuple-element.12.refs_1_, bf16[64,128]{1,0:T(8,128)(2,1)S(1)} %get-tuple-element.20.refs_2_, bf16[64,128]{1,0:T(8,128)(2,1)S(1)} %collective-permute-done.5.refs_3_, ...), custom_call_target="tpu_custom_call" | custom-call | tf_op jit(solution)/shard_map/result/pallas_call | solution.py:324
  (4 shorter events, 0.1 us)
Async XLA Ops:
  0.0 9.8 %copy-start = (s32[8,2]{0,1:T(2,128)S(1)}, s32[8,2]{0,1:T(2,128)}, u32[]{:S(2)}) copy-start(s32[8,2]{0,1:T(2,128)} %param.5) | copy-start | bytes 196
  0.0 9.8 %copy-start.1 = (f32[3,64]{1,0:T(4,128)S(1)}, f32[3,64]{1,0:T(4,128)}, u32[]{:S(2)}) copy-start(f32[3,64]{1,0:T(4,128)} %refs_4_.1) | copy-start | bytes 2308
  0.0 9.5 %collective-permute-start.2 = (s32[2,8]{1,0:T(2,128)}, s32[2,8]{1,0:T(2,128)S(1)}, u32[]{:S(2)}, u32[]{:S(2)}) collective-permute-start(s32[2,8]{1,0:T(2,128)} %bitcast.9), channel_id=1, source_target_pairs={{0,1},{1,2},{2,3},{3,0},{4,5},{5,6},{6,7},{7,4},{8,9},{9,10},{10,1... | collective-permute-start | bytes 200 | tf_op jit(solution)/shard_map/ppermute | solution.py:251
  3.0 6.5 %collective-permute-start.1 = (s32[2,8]{1,0:T(2,128)}, s32[2,8]{1,0:T(2,128)S(1)}, u32[]{:S(2)}, u32[]{:S(2)}) collective-permute-start(s32[2,8]{1,0:T(2,128)} %bitcast.10), channel_id=1, source_target_pairs={{0,3},{1,0},{2,1},{3,2},{4,7},{5,4},{6,5},{7,6},{8,11},{9,8},{10,9... | collective-permute-start | bytes 200 | tf_op jit(solution)/shard_map/ppermute | solution.py:251
  5.1 4.7 %collective-permute-start = (s32[2,8]{1,0:T(2,128)}, s32[2,8]{1,0:T(2,128)S(1)}, u32[]{:S(2)}, u32[]{:S(2)}) collective-permute-start(s32[2,8]{1,0:T(2,128)} %bitcast.11), channel_id=1, source_target_pairs={{0,2},{1,3},{2,0},{3,1},{4,6},{5,7},{6,4},{7,5},{8,10},{9,11},{10,... | collective-permute-start | bytes 200 | tf_op jit(solution)/shard_map/ppermute | solution.py:251
  11.8 1.4 %collective-permute-start.3 = (bf16[2,4,64,128]{3,2,1,0:T(8,128)(2,1)S(1)}, bf16[2,4,64,128]{3,2,1,0:T(8,128)(2,1)S(1)}, u32[]{:S(2)}, u32[]{:S(2)}) collective-permute-start(bf16[2,4,64,128]{3,2,1,0:T(8,128)(2,1)S(1)} %get-tuple-element.16), channel_id=1, source_target_pairs={{0,4},{4,0},{8,12},{12,8},{1,5},{5,1},{9,13},{13,9},{2,6},{6,2},{1... | collective-permute-start | bytes 393224 | tf_op jit(solution)/shard_map/ppermute | solution.py:245
  13.2 4.3 %collective-permute-start.4 = (bf16[1,4,64,128]{3,2,1,0:T(8,128)(2,1)S(1)}, bf16[1,4,64,128]{3,2,1,0:T(8,128)(2,1)S(1)}, u32[]{:S(2)}, u32[]{:S(2)}) collective-permute-start(bf16[1,4,64,128]{3,2,1,0:T(8,128)(2,1)S(1)} %slice.29), channel_id=1, source_target_pairs={{0,8},{4,12},{8,0},{12,4},{1,9},{5,13},{9,1},{13,5},{2,10},{6,14},... | collective-permute-start | bytes 196616 | tf_op jit(solution)/shard_map/ppermute | solution.py:245
  17.6 5.6 %collective-permute-start.7 = (bf16[64,128]{1,0:T(8,128)(2,1)S(1)}, bf16[64,128]{1,0:T(8,128)(2,1)S(1)}, u32[]{:S(2)}, u32[]{:S(2)}) collective-permute-start(bf16[64,128]{1,0:T(8,128)(2,1)S(1)} %get-tuple-element.17), channel_id=1, source_target_pairs={{0,1},{1,2},{2,3},{3,0},{4,5},{5,6},{6,7},{7,4},{8,9},{9,10},{10,1... | collective-permute-start | bytes 49160 | tf_op jit(solution)/shard_map/ppermute | solution.py:251
  19.0 4.6 %collective-permute-start.6 = (bf16[64,128]{1,0:T(8,128)(2,1)S(1)}, bf16[64,128]{1,0:T(8,128)(2,1)S(1)}, u32[]{:S(2)}, u32[]{:S(2)}) collective-permute-start(bf16[64,128]{1,0:T(8,128)(2,1)S(1)} %get-tuple-element.18), channel_id=1, source_target_pairs={{0,2},{1,3},{2,0},{3,1},{4,6},{5,7},{6,4},{7,5},{8,10},{9,11},{10,... | collective-permute-start | bytes 49160 | tf_op jit(solution)/shard_map/ppermute | solution.py:251
  20.2 3.7 %collective-permute-start.5 = (bf16[64,128]{1,0:T(8,128)(2,1)S(1)}, bf16[64,128]{1,0:T(8,128)(2,1)S(1)}, u32[]{:S(2)}, u32[]{:S(2)}) collective-permute-start(bf16[64,128]{1,0:T(8,128)(2,1)S(1)} %get-tuple-element.19), channel_id=1, source_target_pairs={{0,3},{1,0},{2,1},{3,2},{4,7},{5,4},{6,5},{7,6},{8,11},{9,8},{10,9... | collective-permute-start | bytes 49160 | tf_op jit(solution)/shard_map/ppermute | solution.py:251

commit v5 on v4

--- a/solution.py
+++ b/solution.py
@@ -13,12 +13,12 @@
 CAP = 2
 PER_LIST = 2 * CAP
 LANES = 128
-GROUP = 16
+GROUP = 8
 CHUNKS = 1
 ROWS = 16
 
-LISTS_ORDER = (0, 2, 3, 1)
-RESULTS_ORDER = (0, 1, 2, 3)
+LISTS_ORDER = (0, 1, 3, 2)
+RESULTS_ORDER = (0, 1, 3, 2)
 
 
 def orders(n_tile):
@@ -37,8 +37,27 @@
     return lax.broadcasted_iota(i32, shape, dim)
 
 
-def turns(index, window):
-    return (two_pi / window) * jnp.bitwise_and(index, window - 1).astype(f32)
+def series(square, last):
+    total = jnp.full_like(square, (-1.0) ** (last // 2) / math.factorial(last))
+    for n in range(last - 2, -1, -2):
+        total = total * square + (-1.0) ** (n // 2) / math.factorial(n)
+    return total
+
+
+def cos_sin(turn):
+    x = (turn - jnp.floor(turn + 0.5)) * two_pi
+    square = x * x
+    return series(square, 18), series(square, 19) * x
+
+
+def angle_of(index, window):
+    half = window // 2
+    return (two_pi / window) * (jnp.bitwise_and(index + half, window - 1) - half).astype(f32)
+
+
+def cosine_of(index, window):
+    angle = angle_of(index, window)
+    return series(angle * angle, 18)
 
 
 def bit_reversed(number, count):
@@ -57,11 +76,14 @@
     return pltpu.roll(pairs, LANES // 2, pairs.ndim - 1)
 
 
-def spectra_kernel(sizes, probes_hbm, smatrix_hbm, spectra, row_table, turn, select, column_table, smatrix, probes, sems):
+def spectra_kernel(
+    sizes, probes_hbm, smatrix_hbm, table_hbm, spectra, row_table, turn, select, beam_turns, *scratch
+):
     window, kept, n_tile, n_beam = sizes
     share = kept // n_beam
     me_beam = lax.axis_index("beam")
     me_tile = lax.axis_index("tile")
+    column_table, smatrix, probes, beam_table, sems = scratch
     planes = smatrix.shape[1] // CHUNKS
     chunks = [pl.ds(i * planes, planes) for i in range(CHUNKS)]
     copies = [
@@ -72,13 +94,15 @@
         copy.start()
     listed = pltpu.make_async_copy(probes_hbm, probes, sems.at[CHUNKS])
     listed.start()
+    tabled = pltpu.make_async_copy(table_hbm, beam_table, sems.at[CHUNKS + 1])
+    tabled.start()
 
     shape = (2 * window, 2 * kept)
     x, part_in = iota(shape, 0) % window, iota(shape, 0) // window
     lane = iota(shape, 1)
     v, part_out = lane % kept - kept // 2, lane // kept
-    angle = turns(x * v + (window // 4) * (part_out - part_in), window)
-    column_table[...] = jnp.cos(angle).astype(bf16)
+    index = x * v + (window // 4) * (part_out - part_in)
+    column_table[...] = cosine_of(index, window).astype(bf16)
 
     shape = (2 * kept, 2 * window)
     line, turned = iota(shape, 0) % kept, iota(shape, 0) // kept
@@ -88,12 +112,21 @@
     for pos in range(n_beam):
         owner = jnp.where(block == pos, jnp.bitwise_xor(me_beam, bit_reversed(pos, n_beam)), owner)
     u = owner * share + line % share - kept // 2
-    angle = turns(u * r + (window // 4) * (turned - part_in), window)
-    row_table[...] = jnp.cos(angle).astype(bf16)
+    index = u * r + (window // 4) * (turned - part_in)
+    row_table[...] = cosine_of(index, window).astype(bf16)
 
     u = iota((share, LANES), 0) + me_beam * share - kept // 2
     lane = iota((share, LANES), 1)
     v = lane % kept - kept // 2
+    tabled.wait()
+    beams, wide = beam_table.shape[1], beam_turns.shape[1]
+    spread = (iota((beams, wide), 1) // ROWS == iota((beams, wide), 0)).astype(f32)
+    wave_numbers = beam_table[...]
+    scale = jnp.where(iota(wave_numbers.shape, 0) < 2, 1.0 / (window * IF), 1.0 / two_pi)
+    beam_turns[...] = jnp.dot(
+        wave_numbers * scale, spread, precision=lax.Precision.HIGHEST, preferred_element_type=f32
+    )
+
     listed.wait()
     shape = (select.shape[0], select.shape[1])
     window_of, slot_of = iota(shape, 0) // share, iota(shape, 1) // share
@@ -110,9 +143,10 @@
         ]
         wanted = [w | ((window_of == j) & (slot_of == spot)) for w, spot in zip(wanted, spots)]
         shift = jnp.right_shift(probes[1, j], 2) - window // 2
-        angle = turns(u * offset + v * shift, window)
-        turn[0, j * share : (j + 1) * share, :] = jnp.cos(angle)
-        turn[1, j * share : (j + 1) * share, :] = jnp.where(lane < kept, -jnp.sin(angle), jnp.sin(angle))
+        angle = angle_of(u * offset + v * shift, window)
+        square = angle * angle
+        turn[0, j * share : (j + 1) * share, :] = series(square, 18)
+        turn[1, j * share : (j + 1) * share, :] = series(square, 19) * jnp.where(lane < kept, -angle, angle)
     same_line = iota(shape, 0) % share == iota(shape, 1) % share
     select[...] = jnp.where((wanted[0] | wanted[1]) & same_line, 1.0, 0.0).astype(bf16)
 
@@ -124,7 +158,7 @@
 
 
 def chosen(lists, me_tile, window, n_tile):
-    shape = (n_tile * PER_LIST, lists[0].shape[1])
+    shape = (len(lists) * PER_LIST, lists[0].shape[1])
     slot, item = iota(shape, 0), iota(shape, 1)
     rows = jnp.zeros(shape, i32)
     columns = jnp.zeros(shape, i32)
@@ -146,39 +180,50 @@
     return [jnp.sum(jnp.where(hit, x.astype(f32), 0.0), axis=1, keepdims=True) for x in (rows, columns)]
 
 
-def parts_kernel(sizes, *refs):
+def coefficients_kernel(sizes, *refs):
     window, kept, n_tile, n_beam = sizes
-    lists = in_order(refs[:n_tile], orders(n_tile)[0])
-    beam_table, row_table, spectra, keep, send, coeff, waves = refs[n_tile:]
-    share = kept // n_beam
-    beams = spectra.shape[0]
-    slots = n_tile * PER_LIST
-    wide = beams * ROWS
+    lists, (beam_turns, row_table, spectra, keep, send, later, later_offsets, coeff, waves) = refs[:-9], refs[-9:]
+    slots = len(lists) * PER_LIST
+    wide = beam_turns.shape[1]
+    now = keep.shape[1] * PER_LIST
     me_tile = lax.axis_index("tile")
     row_v, column_v = chosen(lists, me_tile, window, n_tile)
     offsets = jnp.bitwise_and(jnp.right_shift(row_v.astype(i32), 2) - window // 2, window - 1)
     offsets = jnp.broadcast_to(offsets, (slots, LANES))
-    phase = beam_table[2:3, :] + two_pi / (window * IF) * (
-        beam_table[0:1, :] * row_v + beam_table[1:2, :] * column_v
-    )
-    alpha = jnp.concatenate([jnp.cos(phase), -jnp.sin(phase)], axis=0).astype(bf16)
-    spread = (iota((beams, wide), 1) // ROWS == iota((beams, wide), 0)).astype(f32).astype(bf16)
-    alpha = jnp.dot(alpha, spread, preferred_element_type=f32)
+    later_offsets[...] = offsets[now:]
+    alpha_re, alpha_im = cos_sin(
+        beam_turns[2:3, :] + (beam_turns[0:1, :] * row_v + beam_turns[1:2, :] * column_v)
+    )
     own_row = iota((ROWS, wide), 1) % ROWS == iota((ROWS, wide), 0)
+    for c, alpha in enumerate((alpha_re, -alpha_im)):
+        for p in range(slots):
+            line = jnp.where(own_row, alpha[p : p + 1, :], 0.0).astype(bf16)
+            if p < now:
+                coeff[p // GROUP, c, p % GROUP] = line
+            else:
+                later[(p - now) // GROUP, c, (p - now) % GROUP] = line
+    make_parts(sizes, coeff, offsets[:now], row_table, spectra, keep, send, waves)
+
+
+def parts_kernel(sizes, coeff, offsets, row_table, spectra, keep, send, waves):
+    make_parts(sizes, coeff, offsets[...], row_table, spectra, keep, send, waves)
+
+
+def make_parts(sizes, coeff, offsets, row_table, spectra, keep, send, waves):
+    window, kept, n_tile, n_beam = sizes
+    share = kept // n_beam
+    wide = spectra.shape[0] * ROWS
     y_in = iota((ROWS, LANES), 0)
     lane = iota((kept, LANES), 1)
     sign = jnp.where(lane < kept, -1.0, 1.0)
-    for first in range(0, slots, GROUP):
-        for c in range(2):
-            for p in range(GROUP):
-                line = c * slots + first + p
-                spot = (c * GROUP + p) * ROWS
-                coeff[spot : spot + ROWS, :] = jnp.where(own_row, alpha[line : line + 1, :], 0.0).astype(bf16)
+    for group in range(coeff.shape[0]):
+        first = group * GROUP
+        matrix = coeff[group].reshape(2 * GROUP * ROWS, wide)
         for y in range(0, window, 2 * ROWS):
             pair = jnp.concatenate(
                 [spectra[:, y + h : y + h + ROWS, :].reshape(wide, LANES) for h in (0, ROWS)], axis=1
             )
-            made = jnp.dot(coeff[...], pair, preferred_element_type=f32)
+            made = jnp.dot(matrix, pair, preferred_element_type=f32)
             for h in range(2):
                 y_here = y_in + (y + h * ROWS)
                 for p in range(GROUP):
@@ -253,6 +298,11 @@
     ]
 
 
+def halves(n_tile):
+    numbers = list(range(n_tile))[::-1]
+    return numbers[: n_tile // 2], numbers[n_tile // 2 :]
+
+
 def in_order(refs, order):
     return [refs[order.index(k)] for k in range(len(order))]
 
@@ -269,57 +319,85 @@
 
     probes = probes.T
     lists_order, results_order = orders(n_tile)
-    lists = shifted([probes] * n_tile, 1, lists_order)
-
-    spectra, row_table, turn, select = pl.pallas_call(
+    lists = lax.optimization_barrier(shifted([probes] * n_tile, 1, lists_order))
+    lists = dict(zip(lists_order, lists))
+
+    spectra, row_table, turn, select, beam_turns = pl.pallas_call(
         functools.partial(spectra_kernel, sizes),
-        in_specs=[HBM, HBM],
-        out_specs=[VMEM] * 4,
+        in_specs=[HBM, HBM, HBM],
+        out_specs=[VMEM] * 5,
         out_shape=[
             jax.ShapeDtypeStruct((beams, window, 2 * kept), bf16),
             jax.ShapeDtypeStruct((2 * kept, 2 * window), bf16),
             jax.ShapeDtypeStruct((2, count * share, LANES), f32),
             jax.ShapeDtypeStruct((count * share, slots * share), bf16),
+            jax.ShapeDtypeStruct((3, beams * ROWS), f32),
         ],
         scratch_shapes=[
             pltpu.VMEM((2 * window, 2 * kept), bf16),
             pltpu.VMEM(smatrix.shape, bf16),
             pltpu.SMEM(probes.shape, i32),
-            pltpu.SemaphoreType.DMA((CHUNKS + 1,)),
+            pltpu.VMEM(beam_table.shape, f32),
+            pltpu.SemaphoreType.DMA((CHUNKS + 2,)),
         ],
         compiler_params=params(48),
         cost_estimate=pl.CostEstimate(
             flops=2 * beams * window * 4 * window * kept, bytes_accessed=smatrix.size * 3, transcendentals=0
         ),
         name="spectra",
-    )(pltpu.with_memory_space_constraint(probes, pltpu.HBM), pltpu.with_memory_space_constraint(smatrix, pltpu.HBM))
-
-    half = jax.ShapeDtypeStruct((n_beam // 2, n_tile, PER_LIST * share, LANES), bf16)
-    keep, send = pl.pallas_call(
-        functools.partial(parts_kernel, sizes),
-        in_specs=[VMEM] * (n_tile + 3),
-        out_specs=[VMEM] * 2,
-        out_shape=[half, half],
-        scratch_shapes=[
-            pltpu.VMEM((2 * GROUP * ROWS, beams * ROWS), bf16),
-            pltpu.VMEM((2, GROUP, window, LANES), bf16),
+    )(
+        pltpu.with_memory_space_constraint(probes, pltpu.HBM),
+        pltpu.with_memory_space_constraint(smatrix, pltpu.HBM),
+        pltpu.with_memory_space_constraint(beam_table, pltpu.HBM),
+    )
+
+    earlier, later = halves(n_tile)
+
+    def parts_call(kernel, numbers, operands, more, scratch, name):
+        half = jax.ShapeDtypeStruct((n_beam // 2, len(numbers), PER_LIST * share, LANES), bf16)
+        return pl.pallas_call(
+            functools.partial(kernel, sizes),
+            in_specs=[VMEM] * len(operands),
+            out_specs=[VMEM] * (2 + len(more)),
+            out_shape=[half, half, *more],
+            scratch_shapes=[*scratch, pltpu.VMEM((2, GROUP, window, LANES), bf16)],
+            compiler_params=params(),
+            cost_estimate=pl.CostEstimate(
+                flops=2 * len(numbers) * PER_LIST * 2 * ROWS * beams * window * LANES,
+                bytes_accessed=4 * 1024 * 1024,
+                transcendentals=0,
+            ),
+            name=name,
+        )(*operands)
+
+    coeff_shape = (len(earlier) * PER_LIST // GROUP, 2, GROUP, ROWS, beams * ROWS)
+    keep, send, coeff, offsets = parts_call(
+        coefficients_kernel,
+        earlier,
+        [lists[n] for n in earlier + later] + [beam_turns, row_table, spectra],
+        [
+            jax.ShapeDtypeStruct(coeff_shape, bf16),
+            jax.ShapeDtypeStruct((len(later) * PER_LIST, LANES), i32),
         ],
-        compiler_params=params(),
-        cost_estimate=pl.CostEstimate(
-            flops=2 * slots * 2 * ROWS * beams * window * LANES, bytes_accessed=4 * 1024 * 1024, transcendentals=0
-        ),
-        name="parts",
-    )(*lists, beam_table, row_table, spectra)
-
-    by = 1
-    while by < n_beam:
-        arrived = swapped(send, "beam", by)
-        total = (keep.astype(f32) + arrived.astype(f32)).astype(bf16)
-        by *= 2
-        middle = total.shape[0] // 2
-        keep, send = total[:middle], total[middle:]
-    mine = total[0]
-    blocks = shifted(mine, -1, results_order)
+        [pltpu.VMEM(coeff_shape, bf16)],
+        "coefficients",
+    )
+    halves_made = [
+        (earlier, keep, send),
+        (later, *parts_call(parts_kernel, later, [coeff, offsets, row_table, spectra], [], [], "parts")),
+    ]
+
+    results = {}
+    for numbers, keep, send in halves_made:
+        by = 1
+        while by < n_beam:
+            arrived = swapped(send, "beam", by)
+            total = (keep.astype(f32) + arrived.astype(f32)).astype(bf16)
+            by *= 2
+            middle = total.shape[0] // 2
+            keep, send = total[:middle], total[middle:]
+        results |= {n: total[0, i] for i, n in enumerate(numbers)}
+    blocks = shifted(results, -1, results_order)
 
     return pl.pallas_call(
         functools.partial(result_kernel, sizes, beams * n_beam),

time: 25.1 us -> 24.3 us (0.968)
  waiting for transfers between devices: 5.77 us -> 2.83 us
  starting transfers between devices: 12.6 us -> 14.3 us
  Pallas kernels: 6.42 us -> 6.91 us
    ppermute x2 -> x4, waiting for transfers between devices: 3.95 us -> 1.36 us  [swapped(): lax.ppermute(array, axis, [(i, i ^ by) for i in range(lax.axis_size(axis))])]
    ppermute x2 -> x4, starting transfers between devices: 1.79 us -> 3.22 us  [swapped(): lax.ppermute(array, axis, [(i, i ^ by) for i in range(lax.axis_size(axis))])]
    ppermute x6, waiting for transfers between devices: 1.82 us -> 1.47 us  [shifted(): lax.ppermute(arrays[k], 'tile', [(i, (i + way * k) % size) for i in range...]
    pallas_call x1 -> x2, Pallas kernels: 1.97 us -> 2.26 us  [parts_call(): pl.pallas_call(functools.partial(kernel, sizes), in_specs=[VMEM] * len(op...]
  transfers between devices with their start and end apart: 8 -> 10, of which waited for: 6 -> 4; matrix products, arithmetic and copies ran while one was open for 0% -> 0% of each run, Pallas kernels for 14% -> 19%
where the time goes in v5:
time: 24.3 us; the launch traced here: 24.2 us
  starting transfers between devices  14.3 us (59%)
  Pallas kernels  6.91 us (28%)
  waiting for transfers between devices  2.83 us (12%)
    ppermute x6, starting transfers between devices, shifted(): lax.ppermute(arrays[k], 'tile', [(i, (i + way * k) % size) for i in range...  11 us
    pallas_call x1, Pallas kernels, per_device(): pl.pallas_call(functools.partial(spectra_kernel, sizes), in_specs=[HBM, H...  3.66 us
    ppermute x4, starting transfers between devices, swapped(): lax.ppermute(array, axis, [(i, i ^ by) for i in range(lax.axis_size(axis))])  3.22 us
    pallas_call x2, Pallas kernels, parts_call(): pl.pallas_call(functools.partial(kernel, sizes), in_specs=[VMEM] * len(op...  2.26 us
    ppermute x6, waiting for transfers between devices, shifted(): lax.ppermute(arrays[k], 'tile', [(i, (i + way * k) % size) for i in range...  1.47 us
    ppermute x4, waiting for transfers between devices, swapped(): lax.ppermute(array, axis, [(i, i ^ by) for i in range(lax.axis_size(axis))])  1.36 us
    pallas_call x1, Pallas kernels, per_device(): pl.pallas_call(functools.partial(result_kernel, sizes, beams * n_beam), i...  0.99 us
  transfers between devices with their start and end apart: 10, of which 4 were waited for; matrix products, arithmetic and copies ran while one was open for 0% of the time, Pallas kernels for 19%

profile of v5, /device:TPU:0, one launch (start us, length us, event | category | flops | bytes accessed | tf_op | source)
XLA Modules:
  0.0 24.2 jit_solution(16300528084083444144)
XLA Ops:
  0.0 0.0 copy-start
  0.0 3.0 %collective-permute-start = (s32[2,8]{1,0:T(2,128)}, s32[2,8]{1,0:T(2,128)S(1)}, u32[]{:S(2)}, u32[]{:S(2)}) collective-permute-start(s32[2,8]{1,0:T(2,128)} %bitcast.9), channel_id=1, source_target_pairs={{0,1},{1,2},{2,3},{3,0},{4,5},{5,6},{6,7},{7,4},{8,9},{9,10},{10,1... | collective-permute-start | bytes 200 | tf_op jit(solution)/shard_map/ppermute | solution.py:296
  3.0 2.1 %collective-permute-start.1 = (s32[2,8]{1,0:T(2,128)}, s32[2,8]{1,0:T(2,128)S(1)}, u32[]{:S(2)}, u32[]{:S(2)}) collective-permute-start(s32[2,8]{1,0:T(2,128)} %bitcast.10), channel_id=1, source_target_pairs={{0,3},{1,0},{2,1},{3,2},{4,7},{5,4},{6,5},{7,6},{8,11},{9,8},{10,9... | collective-permute-start | bytes 200 | tf_op jit(solution)/shard_map/ppermute | solution.py:296
  5.1 1.0 %collective-permute-start.2 = (s32[2,8]{1,0:T(2,128)}, s32[2,8]{1,0:T(2,128)S(1)}, u32[]{:S(2)}, u32[]{:S(2)}) collective-permute-start(s32[2,8]{1,0:T(2,128)} %bitcast.11), channel_id=1, source_target_pairs={{0,2},{1,3},{2,0},{3,1},{4,6},{5,7},{6,4},{7,5},{8,10},{9,11},{10,... | collective-permute-start | bytes 200 | tf_op jit(solution)/shard_map/ppermute | solution.py:296
  6.1 3.7 %spectra.1 = (bf16[64,128,128]{2,1,0:T(8,128)(2,1)S(1)}, bf16[128,256]{1,0:T(8,128)(2,1)S(1)}, f32[2,128,128]{2,1,0:T(8,128)S(1)}, bf16[128,256]{1,0:T(8,128)(2,1)S(1)}, f32[3,1024]{1,0:T(4,128)S(1)}) custom-call(s32[2,8]{1,0:T(2,128)} %bitcast.12, bf16[2,64,128,128]{3,2,1,0:T(8,128)(2,1)} %smatrix_hbm.1, f32[3,64]{1,0:T(4,128)} %table_hbm.1), custom_call_target="tpu_custom_call" | custom-call | flops 536870912 | bytes 6291456 | tf_op jit(solution)/shard_map/spectra/pallas_call | solution.py:325
  9.7 0.0 collective-permute-done.refs_2_
  9.7 0.0 collective-permute-done.1.refs_0_
  9.8 0.0 collective-permute-done.2.refs_1_
  9.8 0.0 copy-done
  9.8 1.3 %coefficients.1 = (bf16[2,2,64,128]{3,2,1,0:T(8,128)(2,1)S(1)}, bf16[2,2,64,128]{3,2,1,0:T(8,128)(2,1)S(1)}, bf16[1,2,8,16,1024]{4,3,2,1,0:T(8,128)(2,1)S(1)}, s32[8,128]{1,0:T(8,128)S(1)}) custom-call(s32[2,8]{1,0:T(2,128)S(1)} %collective-permute-done.1.refs_0_, s32[2,8]{1,0:T(2,128)S(1)} %collective-permute-done.2.refs_1_, ...), custom_call_target="tpu_custom_call" | custom-call | flops 536870912 | bytes 4194304 | tf_op jit(solution)/shard_map/coefficients/pallas_call | solution.py:358
  11.0 0.1 collective-permute-start.6
  11.1 1.0 %parts.1 = (bf16[2,2,64,128]{3,2,1,0:T(8,128)(2,1)S(1)}, bf16[2,2,64,128]{3,2,1,0:T(8,128)(2,1)S(1)}) custom-call(bf16[1,2,8,16,1024]{4,3,2,1,0:T(8,128)(2,1)S(1)} %get-tuple-element.29.coeff, s32[8,128]{1,0:T(8,128)S(1)} %get-tuple-element.30.offsets, bf16[128,256]{1,0:T(8,128)(2,1)S(1)} %get-tuple-element.27.refs_5_.row_table, ...), custom_call_target="tpu_custom_call" | custom-call | flops 536870912 | bytes 4194304 | tf_op jit(solution)/shard_map/parts/pallas_call | solution.py:358
  12.1 0.6 %collective-permute-start.3 = (bf16[2,2,64,128]{3,2,1,0:T(8,128)(2,1)S(1)}, bf16[2,2,64,128]{3,2,1,0:T(8,128)(2,1)S(1)}, u32[]{:S(2)}, u32[]{:S(2)}) collective-permute-start(bf16[2,2,64,128]{3,2,1,0:T(8,128)(2,1)S(1)} %get-tuple-element.32), channel_id=1, source_target_pairs={{0,4},{4,0},{8,12},{12,8},{1,5},{5,1},{9,13},{13,9},{2,6},{6,2},{1... | collective-permute-start | bytes 196616 | tf_op jit(solution)/shard_map/ppermute | solution.py:290
  12.7 0.0 collective-permute-done.6
  12.7 1.7 %collective-permute-start.7 = (bf16[1,2,64,128]{3,2,1,0:T(8,128)(2,1)S(1)}, bf16[1,2,64,128]{3,2,1,0:T(8,128)(2,1)S(1)}, u32[]{:S(2)}, u32[]{:S(2)}) collective-permute-start(bf16[1,2,64,128]{3,2,1,0:T(8,128)(2,1)S(1)} %slice.37), channel_id=1, source_target_pairs={{0,8},{4,12},{8,0},{12,4},{1,9},{5,13},{9,1},{13,5},{2,10},{6,14},... | collective-permute-start | bytes 98312 | tf_op jit(solution)/shard_map/ppermute | solution.py:290
  14.5 0.0 collective-permute-done.3
  14.5 0.9 %collective-permute-start.4 = (bf16[1,2,64,128]{3,2,1,0:T(8,128)(2,1)S(1)}, bf16[1,2,64,128]{3,2,1,0:T(8,128)(2,1)S(1)}, u32[]{:S(2)}, u32[]{:S(2)}) collective-permute-start(bf16[1,2,64,128]{3,2,1,0:T(8,128)(2,1)S(1)} %slice.33), channel_id=1, source_target_pairs={{0,8},{4,12},{8,0},{12,4},{1,9},{5,13},{9,1},{13,5},{2,10},{6,14},... | collective-permute-start | bytes 98312 | tf_op jit(solution)/shard_map/ppermute | solution.py:290
  15.4 1.4 %collective-permute-done.7 = bf16[1,2,64,128]{3,2,1,0:T(8,128)(2,1)S(1)} collective-permute-done((bf16[1,2,64,128]{3,2,1,0:T(8,128)(2,1)S(1)}, bf16[1,2,64,128]{3,2,1,0:T(8,128)(2,1)S(1)}, u32[]{:S(2)}, u32[]{:S(2)}) %collective-permute-start.7) | collective-permute-done | bytes 32800 | tf_op jit(solution)/shard_map/ppermute | solution.py:290
  16.7 1.6 %collective-permute-start.8 = (bf16[64,128]{1,0:T(8,128)(2,1)S(1)}, bf16[64,128]{1,0:T(8,128)(2,1)S(1)}, u32[]{:S(2)}, u32[]{:S(2)}) collective-permute-start(bf16[64,128]{1,0:T(8,128)(2,1)S(1)} %get-tuple-element.36), channel_id=1, source_target_pairs={{0,1},{1,2},{2,3},{3,0},{4,5},{5,6},{6,7},{7,4},{8,9},{9,10},{10,1... | collective-permute-start | bytes 49160 | tf_op jit(solution)/shard_map/ppermute | solution.py:296
  18.4 1.0 %collective-permute-start.9 = (bf16[64,128]{1,0:T(8,128)(2,1)S(1)}, bf16[64,128]{1,0:T(8,128)(2,1)S(1)}, u32[]{:S(2)}, u32[]{:S(2)}) collective-permute-start(bf16[64,128]{1,0:T(8,128)(2,1)S(1)} %get-tuple-element.35), channel_id=1, source_target_pairs={{0,2},{1,3},{2,0},{3,1},{4,6},{5,7},{6,4},{7,5},{8,10},{9,11},{10,... | collective-permute-start | bytes 49160 | tf_op jit(solution)/shard_map/ppermute | solution.py:296
  19.3 0.0 collective-permute-done.4
  19.4 2.4 %collective-permute-start.5 = (bf16[64,128]{1,0:T(8,128)(2,1)S(1)}, bf16[64,128]{1,0:T(8,128)(2,1)S(1)}, u32[]{:S(2)}, u32[]{:S(2)}) collective-permute-start(bf16[64,128]{1,0:T(8,128)(2,1)S(1)} %get-tuple-element.37), channel_id=1, source_target_pairs={{0,3},{1,0},{2,1},{3,2},{4,7},{5,4},{6,5},{7,6},{8,11},{9,8},{10,9... | collective-permute-start | bytes 49160 | tf_op jit(solution)/shard_map/ppermute | solution.py:296
  21.8 0.6 %collective-permute-done.8.refs_4_ = bf16[64,128]{1,0:T(8,128)(2,1)S(1)} collective-permute-done((bf16[64,128]{1,0:T(8,128)(2,1)S(1)}, bf16[64,128]{1,0:T(8,128)(2,1)S(1)}, u32[]{:S(2)}, u32[]{:S(2)}) %collective-permute-start.8) | collective-permute-done | bytes 16416 | tf_op jit(solution)/shard_map/ppermute | solution.py:296
  22.3 0.7 %collective-permute-done.9.refs_5_ = bf16[64,128]{1,0:T(8,128)(2,1)S(1)} collective-permute-done((bf16[64,128]{1,0:T(8,128)(2,1)S(1)}, bf16[64,128]{1,0:T(8,128)(2,1)S(1)}, u32[]{:S(2)}, u32[]{:S(2)}) %collective-permute-start.9) | collective-permute-done | bytes 16416 | tf_op jit(solution)/shard_map/ppermute | solution.py:296
  23.0 0.2 collective-permute-done.5.refs_3_
  23.2 1.0 %result.1 = f32[8,8,32]{2,1,0:T(8,128)} custom-call(f32[2,128,128]{2,1,0:T(8,128)S(1)} %get-tuple-element.20.refs_0_, bf16[128,256]{1,0:T(8,128)(2,1)S(1)} %get-tuple-element.21.refs_1_, bf16[64,128]{1,0:T(8,128)(2,1)S(1)} %get-tuple-element.38.refs_2_, bf16[64,128]{1,0:T(8,128)(2,1)S(1)} %collective-permute-done.5.refs_3_, ...), custom_call_target="tpu_custom_call" | custom-call | tf_op jit(solution)/shard_map/result/pallas_call | solution.py:402
  (8 shorter events, 0.1 us)
Async XLA Ops:
  0.0 9.8 %copy-start = (s32[8,2]{0,1:T(2,128)S(1)}, s32[8,2]{0,1:T(2,128)}, u32[]{:S(2)}) copy-start(s32[8,2]{0,1:T(2,128)} %param.5) | copy-start | bytes 196
  0.0 9.7 %collective-permute-start = (s32[2,8]{1,0:T(2,128)}, s32[2,8]{1,0:T(2,128)S(1)}, u32[]{:S(2)}, u32[]{:S(2)}) collective-permute-start(s32[2,8]{1,0:T(2,128)} %bitcast.9), channel_id=1, source_target_pairs={{0,1},{1,2},{2,3},{3,0},{4,5},{5,6},{6,7},{7,4},{8,9},{9,10},{10,1... | collective-permute-start | bytes 200 | tf_op jit(solution)/shard_map/ppermute | solution.py:296
  3.0 6.7 %collective-permute-start.1 = (s32[2,8]{1,0:T(2,128)}, s32[2,8]{1,0:T(2,128)S(1)}, u32[]{:S(2)}, u32[]{:S(2)}) collective-permute-start(s32[2,8]{1,0:T(2,128)} %bitcast.10), channel_id=1, source_target_pairs={{0,3},{1,0},{2,1},{3,2},{4,7},{5,4},{6,5},{7,6},{8,11},{9,8},{10,9... | collective-permute-start | bytes 200 | tf_op jit(solution)/shard_map/ppermute | solution.py:296
  5.1 4.7 %collective-permute-start.2 = (s32[2,8]{1,0:T(2,128)}, s32[2,8]{1,0:T(2,128)S(1)}, u32[]{:S(2)}, u32[]{:S(2)}) collective-permute-start(s32[2,8]{1,0:T(2,128)} %bitcast.11), channel_id=1, source_target_pairs={{0,2},{1,3},{2,0},{3,1},{4,6},{5,7},{6,4},{7,5},{8,10},{9,11},{10,... | collective-permute-start | bytes 200 | tf_op jit(solution)/shard_map/ppermute | solution.py:296
  11.0 1.7 %collective-permute-start.6 = (bf16[2,2,64,128]{3,2,1,0:T(8,128)(2,1)S(1)}, bf16[2,2,64,128]{3,2,1,0:T(8,128)(2,1)S(1)}, u32[]{:S(2)}, u32[]{:S(2)}) collective-permute-start(bf16[2,2,64,128]{3,2,1,0:T(8,128)(2,1)S(1)} %get-tuple-element.34), channel_id=1, source_target_pairs={{0,4},{4,0},{8,12},{12,8},{1,5},{5,1},{9,13},{13,9},{2,6},{6,2},{1... | collective-permute-start | bytes 196616 | tf_op jit(solution)/shard_map/ppermute | solution.py:290
  12.1 2.3 %collective-permute-start.3 = (bf16[2,2,64,128]{3,2,1,0:T(8,128)(2,1)S(1)}, bf16[2,2,64,128]{3,2,1,0:T(8,128)(2,1)S(1)}, u32[]{:S(2)}, u32[]{:S(2)}) collective-permute-start(bf16[2,2,64,128]{3,2,1,0:T(8,128)(2,1)S(1)} %get-tuple-element.32), channel_id=1, source_target_pairs={{0,4},{4,0},{8,12},{12,8},{1,5},{5,1},{9,13},{13,9},{2,6},{6,2},{1... | collective-permute-start | bytes 196616 | tf_op jit(solution)/shard_map/ppermute | solution.py:290
  12.7 4.0 %collective-permute-start.7 = (bf16[1,2,64,128]{3,2,1,0:T(8,128)(2,1)S(1)}, bf16[1,2,64,128]{3,2,1,0:T(8,128)(2,1)S(1)}, u32[]{:S(2)}, u32[]{:S(2)}) collective-permute-start(bf16[1,2,64,128]{3,2,1,0:T(8,128)(2,1)S(1)} %slice.37), channel_id=1, source_target_pairs={{0,8},{4,12},{8,0},{12,4},{1,9},{5,13},{9,1},{13,5},{2,10},{6,14},... | collective-permute-start | bytes 98312 | tf_op jit(solution)/shard_map/ppermute | solution.py:290
  14.5 4.8 %collective-permute-start.4 = (bf16[1,2,64,128]{3,2,1,0:T(8,128)(2,1)S(1)}, bf16[1,2,64,128]{3,2,1,0:T(8,128)(2,1)S(1)}, u32[]{:S(2)}, u32[]{:S(2)}) collective-permute-start(bf16[1,2,64,128]{3,2,1,0:T(8,128)(2,1)S(1)} %slice.33), channel_id=1, source_target_pairs={{0,8},{4,12},{8,0},{12,4},{1,9},{5,13},{9,1},{13,5},{2,10},{6,14},... | collective-permute-start | bytes 98312 | tf_op jit(solution)/shard_map/ppermute | solution.py:290
  16.7 5.6 %collective-permute-start.8 = (bf16[64,128]{1,0:T(8,128)(2,1)S(1)}, bf16[64,128]{1,0:T(8,128)(2,1)S(1)}, u32[]{:S(2)}, u32[]{:S(2)}) collective-permute-start(bf16[64,128]{1,0:T(8,128)(2,1)S(1)} %get-tuple-element.36), channel_id=1, source_target_pairs={{0,1},{1,2},{2,3},{3,0},{4,5},{5,6},{6,7},{7,4},{8,9},{9,10},{10,1... | collective-permute-start | bytes 49160 | tf_op jit(solution)/shard_map/ppermute | solution.py:296
  18.4 4.6 %collective-permute-start.9 = (bf16[64,128]{1,0:T(8,128)(2,1)S(1)}, bf16[64,128]{1,0:T(8,128)(2,1)S(1)}, u32[]{:S(2)}, u32[]{:S(2)}) collective-permute-start(bf16[64,128]{1,0:T(8,128)(2,1)S(1)} %get-tuple-element.35), channel_id=1, source_target_pairs={{0,2},{1,3},{2,0},{3,1},{4,6},{5,7},{6,4},{7,5},{8,10},{9,11},{10,... | collective-permute-start | bytes 49160 | tf_op jit(solution)/shard_map/ppermute | solution.py:296
  19.4 3.8 %collective-permute-start.5 = (bf16[64,128]{1,0:T(8,128)(2,1)S(1)}, bf16[64,128]{1,0:T(8,128)(2,1)S(1)}, u32[]{:S(2)}, u32[]{:S(2)}) collective-permute-start(bf16[64,128]{1,0:T(8,128)(2,1)S(1)} %get-tuple-element.37), channel_id=1, source_target_pairs={{0,3},{1,0},{2,1},{3,2},{4,7},{5,4},{6,5},{7,6},{8,11},{9,8},{10,9... | collective-permute-start | bytes 49160 | tf_op jit(solution)/shard_map/ppermute | solution.py:296

commit v6 on v5

--- a/solution.py
+++ b/solution.py
@@ -15,7 +15,7 @@
 LANES = 128
 GROUP = 8
 CHUNKS = 1
-ROWS = 16
+ROWS = 8
 
 LISTS_ORDER = (0, 1, 3, 2)
 RESULTS_ORDER = (0, 1, 3, 2)
@@ -150,11 +150,14 @@
     same_line = iota(shape, 0) % share == iota(shape, 1) % share
     select[...] = jnp.where((wanted[0] | wanted[1]) & same_line, 1.0, 0.0).astype(bf16)
 
-    for copy, chunk in zip(copies, chunks):
+    for i, (copy, chunk) in enumerate(zip(copies, chunks)):
         copy.wait()
         flat = jnp.concatenate([smatrix[c, chunk].reshape(planes * window, window) for c in range(2)], axis=1)
         product = jnp.dot(flat, column_table[...], preferred_element_type=f32)
-        spectra[chunk] = product.astype(bf16).reshape(planes, window, 2 * kept)
+        product = product.reshape(planes, window // ROWS, ROWS, 2 * kept)
+        for t in range(window // ROWS):
+            rows = slice(i * planes * ROWS, (i + 1) * planes * ROWS)
+            spectra[t, rows, :] = product[:, t].reshape(planes * ROWS, 2 * kept).astype(bf16)
 
 
 def chosen(lists, me_tile, window, n_tile):
@@ -194,14 +197,16 @@
     alpha_re, alpha_im = cos_sin(
         beam_turns[2:3, :] + (beam_turns[0:1, :] * row_v + beam_turns[1:2, :] * column_v)
     )
-    own_row = iota((ROWS, wide), 1) % ROWS == iota((ROWS, wide), 0)
+    pair = iota((2 * ROWS, wide), 0)
+    own_row = iota((2 * ROWS, wide), 1) % ROWS == pair % ROWS
     for c, alpha in enumerate((alpha_re, -alpha_im)):
-        for p in range(slots):
-            line = jnp.where(own_row, alpha[p : p + 1, :], 0.0).astype(bf16)
+        for p in range(0, slots, 2):
+            lines = jnp.where(pair < ROWS, alpha[p : p + 1, :], alpha[p + 1 : p + 2, :])
+            lines = jnp.where(own_row, lines, 0.0).astype(bf16)
             if p < now:
-                coeff[p // GROUP, c, p % GROUP] = line
+                coeff[p // GROUP, c, p % GROUP // 2] = lines
             else:
-                later[(p - now) // GROUP, c, (p - now) % GROUP] = line
+                later[(p - now) // GROUP, c, (p - now) % GROUP // 2] = lines
     make_parts(sizes, coeff, offsets[:now], row_table, spectra, keep, send, waves)
 
 
@@ -212,28 +217,25 @@
 def make_parts(sizes, coeff, offsets, row_table, spectra, keep, send, waves):
     window, kept, n_tile, n_beam = sizes
     share = kept // n_beam
-    wide = spectra.shape[0] * ROWS
-    y_in = iota((ROWS, LANES), 0)
+    y_in = iota((2 * ROWS, LANES), 0)
     lane = iota((kept, LANES), 1)
     sign = jnp.where(lane < kept, -1.0, 1.0)
     for group in range(coeff.shape[0]):
         first = group * GROUP
-        matrix = coeff[group].reshape(2 * GROUP * ROWS, wide)
-        for y in range(0, window, 2 * ROWS):
-            pair = jnp.concatenate(
-                [spectra[:, y + h : y + h + ROWS, :].reshape(wide, LANES) for h in (0, ROWS)], axis=1
-            )
+        matrix = coeff[group].reshape(2 * GROUP * ROWS, spectra.shape[1])
+        for t in range(0, spectra.shape[0], 2):
+            pair = jnp.concatenate([spectra[t], spectra[t + 1]], axis=1)
             made = jnp.dot(matrix, pair, preferred_element_type=f32)
-            for h in range(2):
-                y_here = y_in + (y + h * ROWS)
-                for p in range(GROUP):
-                    offset = offsets[first + p : first + p + 1, :]
-                    starts_here = p % PER_LIST < CAP
-                    inside = y_here >= offset if starts_here else y_here < offset
-                    for c in range(2):
-                        spot = (c * GROUP + p) * ROWS
-                        value = made[spot : spot + ROWS, h * LANES : (h + 1) * LANES]
-                        waves[c, p, y + h * ROWS : y + (h + 1) * ROWS, :] = jnp.where(inside, value, 0.0).astype(bf16)
+            y = t * ROWS
+            for p in range(GROUP):
+                offset = offsets[first + p : first + p + 1, :]
+                starts_here = p % PER_LIST < CAP
+                inside = y_in + y >= offset if starts_here else y_in + y < offset
+                for c in range(2):
+                    spot = (c * GROUP + p) * ROWS
+                    value = made[spot : spot + ROWS, :]
+                    value = jnp.concatenate([value[:, :LANES], value[:, LANES:]], axis=0)
+                    waves[c, p, y : y + 2 * ROWS, :] = jnp.where(inside, value, 0.0).astype(bf16)
         for p in range(0, GROUP, PER_LIST):
             fields = []
             for q in range(p, p + PER_LIST, 2):
@@ -327,7 +329,7 @@
         in_specs=[HBM, HBM, HBM],
         out_specs=[VMEM] * 5,
         out_shape=[
-            jax.ShapeDtypeStruct((beams, window, 2 * kept), bf16),
+            jax.ShapeDtypeStruct((window // ROWS, beams * ROWS, 2 * kept), bf16),
             jax.ShapeDtypeStruct((2 * kept, 2 * window), bf16),
             jax.ShapeDtypeStruct((2, count * share, LANES), f32),
             jax.ShapeDtypeStruct((count * share, slots * share), bf16),
@@ -370,7 +372,7 @@
             name=name,
         )(*operands)
 
-    coeff_shape = (len(earlier) * PER_LIST // GROUP, 2, GROUP, ROWS, beams * ROWS)
+    coeff_shape = (len(earlier) * PER_LIST // GROUP, 2, GROUP // 2, 2 * ROWS, beams * ROWS)
     keep, send, coeff, offsets = parts_call(
         coefficients_kernel,
         earlier,

time: 24.3 us -> 23.8 us (0.979)
  Pallas kernels: 6.91 us -> 6.31 us
    pallas_call x2, Pallas kernels: 2.26 us -> 1.74 us  [parts_call(): pl.pallas_call(functools.partial(kernel, sizes), in_specs=[VMEM] * len(op...]
  transfers between devices with their start and end apart: 10 -> 10, of which waited for: 4 -> 5; matrix products, arithmetic and copies ran while one was open for 0% -> 0% of each run, Pallas kernels for 19% -> 18%
where the time goes in v6:
time: 23.8 us; the launch traced here: 23.6 us
  starting transfers between devices  14.2 us (60%)
  Pallas kernels  6.31 us (27%)
  waiting for transfers between devices  2.95 us (12%)
    ppermute x6, starting transfers between devices, shifted(): lax.ppermute(arrays[k], 'tile', [(i, (i + way * k) % size) for i in range...  11 us
    pallas_call x1, Pallas kernels, per_device(): pl.pallas_call(functools.partial(spectra_kernel, sizes), in_specs=[HBM, H...  3.58 us
    ppermute x4, starting transfers between devices, swapped(): lax.ppermute(array, axis, [(i, i ^ by) for i in range(lax.axis_size(axis))])  3.22 us
    pallas_call x2, Pallas kernels, parts_call(): pl.pallas_call(functools.partial(kernel, sizes), in_specs=[VMEM] * len(op...  1.74 us
    ppermute x6, waiting for transfers between devices, shifted(): lax.ppermute(arrays[k], 'tile', [(i, (i + way * k) % size) for i in range...  1.59 us
    ppermute x4, waiting for transfers between devices, swapped(): lax.ppermute(array, axis, [(i, i ^ by) for i in range(lax.axis_size(axis))])  1.36 us
    pallas_call x1, Pallas kernels, per_device(): pl.pallas_call(functools.partial(result_kernel, sizes, beams * n_beam), i...  0.99 us
  transfers between devices with their start and end apart: 10, of which 5 were waited for; matrix products, arithmetic and copies ran while one was open for 0% of the time, Pallas kernels for 18%

profile of v6, /device:TPU:0, one launch (start us, length us, event | category | flops | bytes accessed | tf_op | source)
XLA Modules:
  0.0 23.6 jit_solution(11529544613307599468)
XLA Ops:
  0.0 0.0 copy-start
  0.0 3.0 %collective-permute-start = (s32[2,8]{1,0:T(2,128)}, s32[2,8]{1,0:T(2,128)S(1)}, u32[]{:S(2)}, u32[]{:S(2)}) collective-permute-start(s32[2,8]{1,0:T(2,128)} %bitcast.9), channel_id=1, source_target_pairs={{0,1},{1,2},{2,3},{3,0},{4,5},{5,6},{6,7},{7,4},{8,9},{9,10},{10,1... | collective-permute-start | bytes 200 | tf_op jit(solution)/shard_map/ppermute | solution.py:298
  3.0 2.1 %collective-permute-start.1 = (s32[2,8]{1,0:T(2,128)}, s32[2,8]{1,0:T(2,128)S(1)}, u32[]{:S(2)}, u32[]{:S(2)}) collective-permute-start(s32[2,8]{1,0:T(2,128)} %bitcast.10), channel_id=1, source_target_pairs={{0,3},{1,0},{2,1},{3,2},{4,7},{5,4},{6,5},{7,6},{8,11},{9,8},{10,9... | collective-permute-start | bytes 200 | tf_op jit(solution)/shard_map/ppermute | solution.py:298
  5.1 1.0 %collective-permute-start.2 = (s32[2,8]{1,0:T(2,128)}, s32[2,8]{1,0:T(2,128)S(1)}, u32[]{:S(2)}, u32[]{:S(2)}) collective-permute-start(s32[2,8]{1,0:T(2,128)} %bitcast.11), channel_id=1, source_target_pairs={{0,2},{1,3},{2,0},{3,1},{4,6},{5,7},{6,4},{7,5},{8,10},{9,11},{10,... | collective-permute-start | bytes 200 | tf_op jit(solution)/shard_map/ppermute | solution.py:298
  6.1 3.6 %spectra.1 = (bf16[16,512,128]{2,1,0:T(8,128)(2,1)S(1)}, bf16[128,256]{1,0:T(8,128)(2,1)S(1)}, f32[2,128,128]{2,1,0:T(8,128)S(1)}, bf16[128,256]{1,0:T(8,128)(2,1)S(1)}, f32[3,512]{1,0:T(4,128)S(1)}) custom-call(s32[2,8]{1,0:T(2,128)} %bitcast.12, bf16[2,64,128,128]{3,2,1,0:T(8,128)(2,1)} %smatrix_hbm.1, f32[3,64]{1,0:T(4,128)} %table_hbm.1), custom_call_target="tpu_custom_call" | custom-call | flops 536870912 | bytes 6291456 | tf_op jit(solution)/shard_map/spectra/pallas_call | solution.py:327
  9.7 0.0 collective-permute-done.refs_2_
  9.7 0.0 collective-permute-done.1.refs_0_
  9.7 0.1 collective-permute-done.2.refs_1_
  9.8 0.0 copy-done
  9.8 1.0 %coefficients.1 = (bf16[2,2,64,128]{3,2,1,0:T(8,128)(2,1)S(1)}, bf16[2,2,64,128]{3,2,1,0:T(8,128)(2,1)S(1)}, bf16[1,2,4,16,512]{4,3,2,1,0:T(8,128)(2,1)S(1)}, s32[8,128]{1,0:T(8,128)S(1)}) custom-call(s32[2,8]{1,0:T(2,128)S(1)} %collective-permute-done.1.refs_0_, s32[2,8]{1,0:T(2,128)S(1)} %collective-permute-done.2.refs_1_, ...), custom_call_target="tpu_custom_call" | custom-call | flops 268435456 | bytes 4194304 | tf_op jit(solution)/shard_map/coefficients/pallas_call | solution.py:360
  10.8 0.1 collective-permute-start.6
  10.9 0.7 %parts.1 = (bf16[2,2,64,128]{3,2,1,0:T(8,128)(2,1)S(1)}, bf16[2,2,64,128]{3,2,1,0:T(8,128)(2,1)S(1)}) custom-call(bf16[1,2,4,16,512]{4,3,2,1,0:T(8,128)(2,1)S(1)} %get-tuple-element.29.coeff, s32[8,128]{1,0:T(8,128)S(1)} %get-tuple-element.30.offsets, bf16[128,256]{1,0:T(8,128)(2,1)S(1)} %get-tuple-element.27.refs_5_.row_table, ...), custom_call_target="tpu_custom_call" | custom-call | flops 268435456 | bytes 4194304 | tf_op jit(solution)/shard_map/parts/pallas_call | solution.py:360
  11.6 0.6 %collective-permute-start.3 = (bf16[2,2,64,128]{3,2,1,0:T(8,128)(2,1)S(1)}, bf16[2,2,64,128]{3,2,1,0:T(8,128)(2,1)S(1)}, u32[]{:S(2)}, u32[]{:S(2)}) collective-permute-start(bf16[2,2,64,128]{3,2,1,0:T(8,128)(2,1)S(1)} %get-tuple-element.32), channel_id=1, source_target_pairs={{0,4},{4,0},{8,12},{12,8},{1,5},{5,1},{9,13},{13,9},{2,6},{6,2},{1... | collective-permute-start | bytes 196616 | tf_op jit(solution)/shard_map/ppermute | solution.py:292
  12.2 0.0 collective-permute-done.6
  12.2 1.7 %collective-permute-start.7 = (bf16[1,2,64,128]{3,2,1,0:T(8,128)(2,1)S(1)}, bf16[1,2,64,128]{3,2,1,0:T(8,128)(2,1)S(1)}, u32[]{:S(2)}, u32[]{:S(2)}) collective-permute-start(bf16[1,2,64,128]{3,2,1,0:T(8,128)(2,1)S(1)} %slice.37), channel_id=1, source_target_pairs={{0,8},{4,12},{8,0},{12,4},{1,9},{5,13},{9,1},{13,5},{2,10},{6,14},... | collective-permute-start | bytes 98312 | tf_op jit(solution)/shard_map/ppermute | solution.py:292
  13.9 0.0 collective-permute-done.3
  14.0 0.9 %collective-permute-start.4 = (bf16[1,2,64,128]{3,2,1,0:T(8,128)(2,1)S(1)}, bf16[1,2,64,128]{3,2,1,0:T(8,128)(2,1)S(1)}, u32[]{:S(2)}, u32[]{:S(2)}) collective-permute-start(bf16[1,2,64,128]{3,2,1,0:T(8,128)(2,1)S(1)} %slice.33), channel_id=1, source_target_pairs={{0,8},{4,12},{8,0},{12,4},{1,9},{5,13},{9,1},{13,5},{2,10},{6,14},... | collective-permute-start | bytes 98312 | tf_op jit(solution)/shard_map/ppermute | solution.py:292
  14.8 1.3 %collective-permute-done.7 = bf16[1,2,64,128]{3,2,1,0:T(8,128)(2,1)S(1)} collective-permute-done((bf16[1,2,64,128]{3,2,1,0:T(8,128)(2,1)S(1)}, bf16[1,2,64,128]{3,2,1,0:T(8,128)(2,1)S(1)}, u32[]{:S(2)}, u32[]{:S(2)}) %collective-permute-start.7) | collective-permute-done | bytes 32800 | tf_op jit(solution)/shard_map/ppermute | solution.py:292
  16.2 1.5 %collective-permute-start.8 = (bf16[64,128]{1,0:T(8,128)(2,1)S(1)}, bf16[64,128]{1,0:T(8,128)(2,1)S(1)}, u32[]{:S(2)}, u32[]{:S(2)}) collective-permute-start(bf16[64,128]{1,0:T(8,128)(2,1)S(1)} %get-tuple-element.36), channel_id=1, source_target_pairs={{0,1},{1,2},{2,3},{3,0},{4,5},{5,6},{6,7},{7,4},{8,9},{9,10},{10,1... | collective-permute-start | bytes 49160 | tf_op jit(solution)/shard_map/ppermute | solution.py:298
  17.8 1.1 %collective-permute-start.9 = (bf16[64,128]{1,0:T(8,128)(2,1)S(1)}, bf16[64,128]{1,0:T(8,128)(2,1)S(1)}, u32[]{:S(2)}, u32[]{:S(2)}) collective-permute-start(bf16[64,128]{1,0:T(8,128)(2,1)S(1)} %get-tuple-element.35), channel_id=1, source_target_pairs={{0,2},{1,3},{2,0},{3,1},{4,6},{5,7},{6,4},{7,5},{8,10},{9,11},{10,... | collective-permute-start | bytes 49160 | tf_op jit(solution)/shard_map/ppermute | solution.py:298
  18.8 0.0 collective-permute-done.4
  18.9 2.3 %collective-permute-start.5 = (bf16[64,128]{1,0:T(8,128)(2,1)S(1)}, bf16[64,128]{1,0:T(8,128)(2,1)S(1)}, u32[]{:S(2)}, u32[]{:S(2)}) collective-permute-start(bf16[64,128]{1,0:T(8,128)(2,1)S(1)} %get-tuple-element.37), channel_id=1, source_target_pairs={{0,3},{1,0},{2,1},{3,2},{4,7},{5,4},{6,5},{7,6},{8,11},{9,8},{10,9... | collective-permute-start | bytes 49160 | tf_op jit(solution)/shard_map/ppermute | solution.py:298
  21.2 0.7 %collective-permute-done.8.refs_4_ = bf16[64,128]{1,0:T(8,128)(2,1)S(1)} collective-permute-done((bf16[64,128]{1,0:T(8,128)(2,1)S(1)}, bf16[64,128]{1,0:T(8,128)(2,1)S(1)}, u32[]{:S(2)}, u32[]{:S(2)}) %collective-permute-start.8) | collective-permute-done | bytes 16416 | tf_op jit(solution)/shard_map/ppermute | solution.py:298
  21.8 0.6 %collective-permute-done.9.refs_5_ = bf16[64,128]{1,0:T(8,128)(2,1)S(1)} collective-permute-done((bf16[64,128]{1,0:T(8,128)(2,1)S(1)}, bf16[64,128]{1,0:T(8,128)(2,1)S(1)}, u32[]{:S(2)}, u32[]{:S(2)}) %collective-permute-start.9) | collective-permute-done | bytes 16416 | tf_op jit(solution)/shard_map/ppermute | solution.py:298
  22.4 0.2 %collective-permute-done.5.refs_3_ = bf16[64,128]{1,0:T(8,128)(2,1)S(1)} collective-permute-done((bf16[64,128]{1,0:T(8,128)(2,1)S(1)}, bf16[64,128]{1,0:T(8,128)(2,1)S(1)}, u32[]{:S(2)}, u32[]{:S(2)}) %collective-permute-start.5) | collective-permute-done | bytes 16416 | tf_op jit(solution)/shard_map/ppermute | solution.py:298
  22.6 1.0 %result.1 = f32[8,8,32]{2,1,0:T(8,128)} custom-call(f32[2,128,128]{2,1,0:T(8,128)S(1)} %get-tuple-element.20.refs_0_, bf16[128,256]{1,0:T(8,128)(2,1)S(1)} %get-tuple-element.21.refs_1_, bf16[64,128]{1,0:T(8,128)(2,1)S(1)} %get-tuple-element.38.refs_2_, bf16[64,128]{1,0:T(8,128)(2,1)S(1)} %collective-permute-done.5.refs_3_, ...), custom_call_target="tpu_custom_call" | custom-call | tf_op jit(solution)/shard_map/result/pallas_call | solution.py:404
  (8 shorter events, 0.1 us)
Async XLA Ops:
  0.0 9.8 %copy-start = (s32[8,2]{0,1:T(2,128)S(1)}, s32[8,2]{0,1:T(2,128)}, u32[]{:S(2)}) copy-start(s32[8,2]{0,1:T(2,128)} %param.5) | copy-start | bytes 196
  0.0 9.7 %collective-permute-start = (s32[2,8]{1,0:T(2,128)}, s32[2,8]{1,0:T(2,128)S(1)}, u32[]{:S(2)}, u32[]{:S(2)}) collective-permute-start(s32[2,8]{1,0:T(2,128)} %bitcast.9), channel_id=1, source_target_pairs={{0,1},{1,2},{2,3},{3,0},{4,5},{5,6},{6,7},{7,4},{8,9},{9,10},{10,1... | collective-permute-start | bytes 200 | tf_op jit(solution)/shard_map/ppermute | solution.py:298
  3.0 6.6 %collective-permute-start.1 = (s32[2,8]{1,0:T(2,128)}, s32[2,8]{1,0:T(2,128)S(1)}, u32[]{:S(2)}, u32[]{:S(2)}) collective-permute-start(s32[2,8]{1,0:T(2,128)} %bitcast.10), channel_id=1, source_target_pairs={{0,3},{1,0},{2,1},{3,2},{4,7},{5,4},{6,5},{7,6},{8,11},{9,8},{10,9... | collective-permute-start | bytes 200 | tf_op jit(solution)/shard_map/ppermute | solution.py:298
  5.1 4.7 %collective-permute-start.2 = (s32[2,8]{1,0:T(2,128)}, s32[2,8]{1,0:T(2,128)S(1)}, u32[]{:S(2)}, u32[]{:S(2)}) collective-permute-start(s32[2,8]{1,0:T(2,128)} %bitcast.11), channel_id=1, source_target_pairs={{0,2},{1,3},{2,0},{3,1},{4,6},{5,7},{6,4},{7,5},{8,10},{9,11},{10,... | collective-permute-start | bytes 200 | tf_op jit(solution)/shard_map/ppermute | solution.py:298
  10.8 1.4 %collective-permute-start.6 = (bf16[2,2,64,128]{3,2,1,0:T(8,128)(2,1)S(1)}, bf16[2,2,64,128]{3,2,1,0:T(8,128)(2,1)S(1)}, u32[]{:S(2)}, u32[]{:S(2)}) collective-permute-start(bf16[2,2,64,128]{3,2,1,0:T(8,128)(2,1)S(1)} %get-tuple-element.34), channel_id=1, source_target_pairs={{0,4},{4,0},{8,12},{12,8},{1,5},{5,1},{9,13},{13,9},{2,6},{6,2},{1... | collective-permute-start | bytes 196616 | tf_op jit(solution)/shard_map/ppermute | solution.py:292
  11.6 2.3 %collective-permute-start.3 = (bf16[2,2,64,128]{3,2,1,0:T(8,128)(2,1)S(1)}, bf16[2,2,64,128]{3,2,1,0:T(8,128)(2,1)S(1)}, u32[]{:S(2)}, u32[]{:S(2)}) collective-permute-start(bf16[2,2,64,128]{3,2,1,0:T(8,128)(2,1)S(1)} %get-tuple-element.32), channel_id=1, source_target_pairs={{0,4},{4,0},{8,12},{12,8},{1,5},{5,1},{9,13},{13,9},{2,6},{6,2},{1... | collective-permute-start | bytes 196616 | tf_op jit(solution)/shard_map/ppermute | solution.py:292
  12.2 4.0 %collective-permute-start.7 = (bf16[1,2,64,128]{3,2,1,0:T(8,128)(2,1)S(1)}, bf16[1,2,64,128]{3,2,1,0:T(8,128)(2,1)S(1)}, u32[]{:S(2)}, u32[]{:S(2)}) collective-permute-start(bf16[1,2,64,128]{3,2,1,0:T(8,128)(2,1)S(1)} %slice.37), channel_id=1, source_target_pairs={{0,8},{4,12},{8,0},{12,4},{1,9},{5,13},{9,1},{13,5},{2,10},{6,14},... | collective-permute-start | bytes 98312 | tf_op jit(solution)/shard_map/ppermute | solution.py:292
  14.0 4.8 %collective-permute-start.4 = (bf16[1,2,64,128]{3,2,1,0:T(8,128)(2,1)S(1)}, bf16[1,2,64,128]{3,2,1,0:T(8,128)(2,1)S(1)}, u32[]{:S(2)}, u32[]{:S(2)}) collective-permute-start(bf16[1,2,64,128]{3,2,1,0:T(8,128)(2,1)S(1)} %slice.33), channel_id=1, source_target_pairs={{0,8},{4,12},{8,0},{12,4},{1,9},{5,13},{9,1},{13,5},{2,10},{6,14},... | collective-permute-start | bytes 98312 | tf_op jit(solution)/shard_map/ppermute | solution.py:292
  16.2 5.6 %collective-permute-start.8 = (bf16[64,128]{1,0:T(8,128)(2,1)S(1)}, bf16[64,128]{1,0:T(8,128)(2,1)S(1)}, u32[]{:S(2)}, u32[]{:S(2)}) collective-permute-start(bf16[64,128]{1,0:T(8,128)(2,1)S(1)} %get-tuple-element.36), channel_id=1, source_target_pairs={{0,1},{1,2},{2,3},{3,0},{4,5},{5,6},{6,7},{7,4},{8,9},{9,10},{10,1... | collective-permute-start | bytes 49160 | tf_op jit(solution)/shard_map/ppermute | solution.py:298
  17.8 4.6 %collective-permute-start.9 = (bf16[64,128]{1,0:T(8,128)(2,1)S(1)}, bf16[64,128]{1,0:T(8,128)(2,1)S(1)}, u32[]{:S(2)}, u32[]{:S(2)}) collective-permute-start(bf16[64,128]{1,0:T(8,128)(2,1)S(1)} %get-tuple-element.35), channel_id=1, source_target_pairs={{0,2},{1,3},{2,0},{3,1},{4,6},{5,7},{6,4},{7,5},{8,10},{9,11},{10,... | collective-permute-start | bytes 49160 | tf_op jit(solution)/shard_map/ppermute | solution.py:298
  18.9 3.8 %collective-permute-start.5 = (bf16[64,128]{1,0:T(8,128)(2,1)S(1)}, bf16[64,128]{1,0:T(8,128)(2,1)S(1)}, u32[]{:S(2)}, u32[]{:S(2)}) collective-permute-start(bf16[64,128]{1,0:T(8,128)(2,1)S(1)} %get-tuple-element.37), channel_id=1, source_target_pairs={{0,3},{1,0},{2,1},{3,2},{4,7},{5,4},{6,5},{7,6},{8,11},{9,8},{10,9... | collective-permute-start | bytes 49160 | tf_op jit(solution)/shard_map/ppermute | solution.py:298

commit v7 on v6

--- a/solution.py
+++ b/solution.py
@@ -172,15 +172,14 @@
     tile, _ = window_start(rows, window, window * n_tile)
     before = jnp.where(me_tile == 0, n_tile - 1, me_tile - 1)
     match = tile == jnp.where(slot % PER_LIST < CAP, me_tile, before)
-    item = item.astype(f32)
-    nothing = float(shape[1])
-    left = jnp.where(match, item, nothing)
-    picked = jnp.min(left, axis=1, keepdims=True)
-    for n in range(1, CAP):
-        left = jnp.where(left == picked, nothing, left)
-        picked = jnp.where(slot[:, :1] % CAP >= n, jnp.min(left, axis=1, keepdims=True), picked)
-    hit = item == picked
-    return [jnp.sum(jnp.where(hit, x.astype(f32), 0.0), axis=1, keepdims=True) for x in (rows, columns)]
+    sign = jnp.where(slot % CAP == 0, 1, -1)
+    nothing = float(1 << 23)
+    found = []
+    for values, limit in ((rows, window * n_tile * IF), (columns, window * IF)):
+        keys = (sign * (item * limit + values)).astype(f32)
+        key = jnp.abs(jnp.min(jnp.where(match, keys, nothing), axis=1, keepdims=True))
+        found.append(jnp.bitwise_and(key.astype(i32), limit - 1))
+    return found
 
 
 def coefficients_kernel(sizes, *refs):
@@ -191,11 +190,11 @@
     now = keep.shape[1] * PER_LIST
     me_tile = lax.axis_index("tile")
     row_v, column_v = chosen(lists, me_tile, window, n_tile)
-    offsets = jnp.bitwise_and(jnp.right_shift(row_v.astype(i32), 2) - window // 2, window - 1)
+    offsets = jnp.bitwise_and(jnp.right_shift(row_v, 2) - window // 2, window - 1)
     offsets = jnp.broadcast_to(offsets, (slots, LANES))
     later_offsets[...] = offsets[now:]
     alpha_re, alpha_im = cos_sin(
-        beam_turns[2:3, :] + (beam_turns[0:1, :] * row_v + beam_turns[1:2, :] * column_v)
+        beam_turns[2:3, :] + (beam_turns[0:1, :] * row_v.astype(f32) + beam_turns[1:2, :] * column_v.astype(f32))
     )
     pair = iota((2 * ROWS, wide), 0)
     own_row = iota((2 * ROWS, wide), 1) % ROWS == pair % ROWS

time: 23.8 us -> 23.6 us (level)
  no operation moved by 1% of the time
where the time goes in v7:
time: 23.6 us; the launch traced here: 23.5 us
  starting transfers between devices  14.2 us (60%)
  Pallas kernels  6.15 us (26%)
  waiting for transfers between devices  2.95 us (12%)
    ppermute x6, starting transfers between devices, shifted(): lax.ppermute(arrays[k], 'tile', [(i, (i + way * k) % size) for i in range...  11 us
    pallas_call x1, Pallas kernels, per_device(): pl.pallas_call(functools.partial(spectra_kernel, sizes), in_specs=[HBM, H...  3.58 us
    ppermute x4, starting transfers between devices, swapped(): lax.ppermute(array, axis, [(i, i ^ by) for i in range(lax.axis_size(axis))])  3.22 us
    ppermute x6, waiting for transfers between devices, shifted(): lax.ppermute(arrays[k], 'tile', [(i, (i + way * k) % size) for i in range...  1.59 us
    pallas_call x2, Pallas kernels, parts_call(): pl.pallas_call(functools.partial(kernel, sizes), in_specs=[VMEM] * len(op...  1.58 us
    ppermute x4, waiting for transfers between devices, swapped(): lax.ppermute(array, axis, [(i, i ^ by) for i in range(lax.axis_size(axis))])  1.36 us
    pallas_call x1, Pallas kernels, per_device(): pl.pallas_call(functools.partial(result_kernel, sizes, beams * n_beam), i...  0.99 us
  transfers between devices with their start and end apart: 10, of which 5 were waited for; matrix products, arithmetic and copies ran while one was open for 0% of the time, Pallas kernels for 18%

profile of v7, /device:TPU:0, one launch (start us, length us, event | category | flops | bytes accessed | tf_op | source)
XLA Modules:
  0.0 23.5 jit_solution(14751315087083889179)
XLA Ops:
  0.0 0.0 copy-start
  0.0 3.0 %collective-permute-start = (s32[2,8]{1,0:T(2,128)}, s32[2,8]{1,0:T(2,128)S(1)}, u32[]{:S(2)}, u32[]{:S(2)}) collective-permute-start(s32[2,8]{1,0:T(2,128)} %bitcast.9), channel_id=1, source_target_pairs={{0,1},{1,2},{2,3},{3,0},{4,5},{5,6},{6,7},{7,4},{8,9},{9,10},{10,1... | collective-permute-start | bytes 200 | tf_op jit(solution)/shard_map/ppermute | solution.py:297
  3.0 2.1 %collective-permute-start.1 = (s32[2,8]{1,0:T(2,128)}, s32[2,8]{1,0:T(2,128)S(1)}, u32[]{:S(2)}, u32[]{:S(2)}) collective-permute-start(s32[2,8]{1,0:T(2,128)} %bitcast.10), channel_id=1, source_target_pairs={{0,3},{1,0},{2,1},{3,2},{4,7},{5,4},{6,5},{7,6},{8,11},{9,8},{10,9... | collective-permute-start | bytes 200 | tf_op jit(solution)/shard_map/ppermute | solution.py:297
  5.1 1.0 %collective-permute-start.2 = (s32[2,8]{1,0:T(2,128)}, s32[2,8]{1,0:T(2,128)S(1)}, u32[]{:S(2)}, u32[]{:S(2)}) collective-permute-start(s32[2,8]{1,0:T(2,128)} %bitcast.11), channel_id=1, source_target_pairs={{0,2},{1,3},{2,0},{3,1},{4,6},{5,7},{6,4},{7,5},{8,10},{9,11},{10,... | collective-permute-start | bytes 200 | tf_op jit(solution)/shard_map/ppermute | solution.py:297
  6.1 3.6 %spectra.1 = (bf16[16,512,128]{2,1,0:T(8,128)(2,1)S(1)}, bf16[128,256]{1,0:T(8,128)(2,1)S(1)}, f32[2,128,128]{2,1,0:T(8,128)S(1)}, bf16[128,256]{1,0:T(8,128)(2,1)S(1)}, f32[3,512]{1,0:T(4,128)S(1)}) custom-call(s32[2,8]{1,0:T(2,128)} %bitcast.12, bf16[2,64,128,128]{3,2,1,0:T(8,128)(2,1)} %smatrix_hbm.1, f32[3,64]{1,0:T(4,128)} %table_hbm.1), custom_call_target="tpu_custom_call" | custom-call | flops 536870912 | bytes 6291456 | tf_op jit(solution)/shard_map/spectra/pallas_call | solution.py:326
  9.7 0.0 collective-permute-done.refs_2_
  9.7 0.0 collective-permute-done.1.refs_0_
  9.7 0.1 collective-permute-done.2.refs_1_
  9.8 0.0 copy-done
  9.8 0.8 %coefficients.1 = (bf16[2,2,64,128]{3,2,1,0:T(8,128)(2,1)S(1)}, bf16[2,2,64,128]{3,2,1,0:T(8,128)(2,1)S(1)}, bf16[1,2,4,16,512]{4,3,2,1,0:T(8,128)(2,1)S(1)}, s32[8,128]{1,0:T(8,128)S(1)}) custom-call(s32[2,8]{1,0:T(2,128)S(1)} %collective-permute-done.1.refs_0_, s32[2,8]{1,0:T(2,128)S(1)} %collective-permute-done.2.refs_1_, ...), custom_call_target="tpu_custom_call" | custom-call | flops 268435456 | bytes 4194304 | tf_op jit(solution)/shard_map/coefficients/pallas_call | solution.py:359
  10.6 0.1 collective-permute-start.6
  10.7 0.7 %parts.1 = (bf16[2,2,64,128]{3,2,1,0:T(8,128)(2,1)S(1)}, bf16[2,2,64,128]{3,2,1,0:T(8,128)(2,1)S(1)}) custom-call(bf16[1,2,4,16,512]{4,3,2,1,0:T(8,128)(2,1)S(1)} %get-tuple-element.29.coeff, s32[8,128]{1,0:T(8,128)S(1)} %get-tuple-element.30.offsets, bf16[128,256]{1,0:T(8,128)(2,1)S(1)} %get-tuple-element.27.refs_5_.row_table, ...), custom_call_target="tpu_custom_call" | custom-call | flops 268435456 | bytes 4194304 | tf_op jit(solution)/shard_map/parts/pallas_call | solution.py:359
  11.5 0.6 %collective-permute-start.3 = (bf16[2,2,64,128]{3,2,1,0:T(8,128)(2,1)S(1)}, bf16[2,2,64,128]{3,2,1,0:T(8,128)(2,1)S(1)}, u32[]{:S(2)}, u32[]{:S(2)}) collective-permute-start(bf16[2,2,64,128]{3,2,1,0:T(8,128)(2,1)S(1)} %get-tuple-element.32), channel_id=1, source_target_pairs={{0,4},{4,0},{8,12},{12,8},{1,5},{5,1},{9,13},{13,9},{2,6},{6,2},{1... | collective-permute-start | bytes 196616 | tf_op jit(solution)/shard_map/ppermute | solution.py:291
  12.0 0.0 collective-permute-done.6
  12.1 1.7 %collective-permute-start.7 = (bf16[1,2,64,128]{3,2,1,0:T(8,128)(2,1)S(1)}, bf16[1,2,64,128]{3,2,1,0:T(8,128)(2,1)S(1)}, u32[]{:S(2)}, u32[]{:S(2)}) collective-permute-start(bf16[1,2,64,128]{3,2,1,0:T(8,128)(2,1)S(1)} %slice.37), channel_id=1, source_target_pairs={{0,8},{4,12},{8,0},{12,4},{1,9},{5,13},{9,1},{13,5},{2,10},{6,14},... | collective-permute-start | bytes 98312 | tf_op jit(solution)/shard_map/ppermute | solution.py:291
  13.8 0.0 collective-permute-done.3
  13.8 0.9 %collective-permute-start.4 = (bf16[1,2,64,128]{3,2,1,0:T(8,128)(2,1)S(1)}, bf16[1,2,64,128]{3,2,1,0:T(8,128)(2,1)S(1)}, u32[]{:S(2)}, u32[]{:S(2)}) collective-permute-start(bf16[1,2,64,128]{3,2,1,0:T(8,128)(2,1)S(1)} %slice.33), channel_id=1, source_target_pairs={{0,8},{4,12},{8,0},{12,4},{1,9},{5,13},{9,1},{13,5},{2,10},{6,14},... | collective-permute-start | bytes 98312 | tf_op jit(solution)/shard_map/ppermute | solution.py:291
  14.7 1.3 %collective-permute-done.7 = bf16[1,2,64,128]{3,2,1,0:T(8,128)(2,1)S(1)} collective-permute-done((bf16[1,2,64,128]{3,2,1,0:T(8,128)(2,1)S(1)}, bf16[1,2,64,128]{3,2,1,0:T(8,128)(2,1)S(1)}, u32[]{:S(2)}, u32[]{:S(2)}) %collective-permute-start.7) | collective-permute-done | bytes 32800 | tf_op jit(solution)/shard_map/ppermute | solution.py:291
  16.1 1.5 %collective-permute-start.8 = (bf16[64,128]{1,0:T(8,128)(2,1)S(1)}, bf16[64,128]{1,0:T(8,128)(2,1)S(1)}, u32[]{:S(2)}, u32[]{:S(2)}) collective-permute-start(bf16[64,128]{1,0:T(8,128)(2,1)S(1)} %get-tuple-element.36), channel_id=1, source_target_pairs={{0,1},{1,2},{2,3},{3,0},{4,5},{5,6},{6,7},{7,4},{8,9},{9,10},{10,1... | collective-permute-start | bytes 49160 | tf_op jit(solution)/shard_map/ppermute | solution.py:297
  17.6 1.1 %collective-permute-start.9 = (bf16[64,128]{1,0:T(8,128)(2,1)S(1)}, bf16[64,128]{1,0:T(8,128)(2,1)S(1)}, u32[]{:S(2)}, u32[]{:S(2)}) collective-permute-start(bf16[64,128]{1,0:T(8,128)(2,1)S(1)} %get-tuple-element.35), channel_id=1, source_target_pairs={{0,2},{1,3},{2,0},{3,1},{4,6},{5,7},{6,4},{7,5},{8,10},{9,11},{10,... | collective-permute-start | bytes 49160 | tf_op jit(solution)/shard_map/ppermute | solution.py:297
  18.7 0.0 collective-permute-done.4
  18.7 2.3 %collective-permute-start.5 = (bf16[64,128]{1,0:T(8,128)(2,1)S(1)}, bf16[64,128]{1,0:T(8,128)(2,1)S(1)}, u32[]{:S(2)}, u32[]{:S(2)}) collective-permute-start(bf16[64,128]{1,0:T(8,128)(2,1)S(1)} %get-tuple-element.37), channel_id=1, source_target_pairs={{0,3},{1,0},{2,1},{3,2},{4,7},{5,4},{6,5},{7,6},{8,11},{9,8},{10,9... | collective-permute-start | bytes 49160 | tf_op jit(solution)/shard_map/ppermute | solution.py:297
  21.0 0.7 %collective-permute-done.8.refs_4_ = bf16[64,128]{1,0:T(8,128)(2,1)S(1)} collective-permute-done((bf16[64,128]{1,0:T(8,128)(2,1)S(1)}, bf16[64,128]{1,0:T(8,128)(2,1)S(1)}, u32[]{:S(2)}, u32[]{:S(2)}) %collective-permute-start.8) | collective-permute-done | bytes 16416 | tf_op jit(solution)/shard_map/ppermute | solution.py:297
  21.7 0.6 %collective-permute-done.9.refs_5_ = bf16[64,128]{1,0:T(8,128)(2,1)S(1)} collective-permute-done((bf16[64,128]{1,0:T(8,128)(2,1)S(1)}, bf16[64,128]{1,0:T(8,128)(2,1)S(1)}, u32[]{:S(2)}, u32[]{:S(2)}) %collective-permute-start.9) | collective-permute-done | bytes 16416 | tf_op jit(solution)/shard_map/ppermute | solution.py:297
  22.2 0.2 %collective-permute-done.5.refs_3_ = bf16[64,128]{1,0:T(8,128)(2,1)S(1)} collective-permute-done((bf16[64,128]{1,0:T(8,128)(2,1)S(1)}, bf16[64,128]{1,0:T(8,128)(2,1)S(1)}, u32[]{:S(2)}, u32[]{:S(2)}) %collective-permute-start.5) | collective-permute-done | bytes 16416 | tf_op jit(solution)/shard_map/ppermute | solution.py:297
  22.5 1.0 %result.1 = f32[8,8,32]{2,1,0:T(8,128)} custom-call(f32[2,128,128]{2,1,0:T(8,128)S(1)} %get-tuple-element.20.refs_0_, bf16[128,256]{1,0:T(8,128)(2,1)S(1)} %get-tuple-element.21.refs_1_, bf16[64,128]{1,0:T(8,128)(2,1)S(1)} %get-tuple-element.38.refs_2_, bf16[64,128]{1,0:T(8,128)(2,1)S(1)} %collective-permute-done.5.refs_3_, ...), custom_call_target="tpu_custom_call" | custom-call | tf_op jit(solution)/shard_map/result/pallas_call | solution.py:403
  (8 shorter events, 0.1 us)
Async XLA Ops:
  0.0 9.8 %copy-start = (s32[8,2]{0,1:T(2,128)S(1)}, s32[8,2]{0,1:T(2,128)}, u32[]{:S(2)}) copy-start(s32[8,2]{0,1:T(2,128)} %param.5) | copy-start | bytes 196
  0.0 9.7 %collective-permute-start = (s32[2,8]{1,0:T(2,128)}, s32[2,8]{1,0:T(2,128)S(1)}, u32[]{:S(2)}, u32[]{:S(2)}) collective-permute-start(s32[2,8]{1,0:T(2,128)} %bitcast.9), channel_id=1, source_target_pairs={{0,1},{1,2},{2,3},{3,0},{4,5},{5,6},{6,7},{7,4},{8,9},{9,10},{10,1... | collective-permute-start | bytes 200 | tf_op jit(solution)/shard_map/ppermute | solution.py:297
  3.0 6.6 %collective-permute-start.1 = (s32[2,8]{1,0:T(2,128)}, s32[2,8]{1,0:T(2,128)S(1)}, u32[]{:S(2)}, u32[]{:S(2)}) collective-permute-start(s32[2,8]{1,0:T(2,128)} %bitcast.10), channel_id=1, source_target_pairs={{0,3},{1,0},{2,1},{3,2},{4,7},{5,4},{6,5},{7,6},{8,11},{9,8},{10,9... | collective-permute-start | bytes 200 | tf_op jit(solution)/shard_map/ppermute | solution.py:297
  5.1 4.7 %collective-permute-start.2 = (s32[2,8]{1,0:T(2,128)}, s32[2,8]{1,0:T(2,128)S(1)}, u32[]{:S(2)}, u32[]{:S(2)}) collective-permute-start(s32[2,8]{1,0:T(2,128)} %bitcast.11), channel_id=1, source_target_pairs={{0,2},{1,3},{2,0},{3,1},{4,6},{5,7},{6,4},{7,5},{8,10},{9,11},{10,... | collective-permute-start | bytes 200 | tf_op jit(solution)/shard_map/ppermute | solution.py:297
  10.6 1.4 %collective-permute-start.6 = (bf16[2,2,64,128]{3,2,1,0:T(8,128)(2,1)S(1)}, bf16[2,2,64,128]{3,2,1,0:T(8,128)(2,1)S(1)}, u32[]{:S(2)}, u32[]{:S(2)}) collective-permute-start(bf16[2,2,64,128]{3,2,1,0:T(8,128)(2,1)S(1)} %get-tuple-element.34), channel_id=1, source_target_pairs={{0,4},{4,0},{8,12},{12,8},{1,5},{5,1},{9,13},{13,9},{2,6},{6,2},{1... | collective-permute-start | bytes 196616 | tf_op jit(solution)/shard_map/ppermute | solution.py:291
  11.5 2.3 %collective-permute-start.3 = (bf16[2,2,64,128]{3,2,1,0:T(8,128)(2,1)S(1)}, bf16[2,2,64,128]{3,2,1,0:T(8,128)(2,1)S(1)}, u32[]{:S(2)}, u32[]{:S(2)}) collective-permute-start(bf16[2,2,64,128]{3,2,1,0:T(8,128)(2,1)S(1)} %get-tuple-element.32), channel_id=1, source_target_pairs={{0,4},{4,0},{8,12},{12,8},{1,5},{5,1},{9,13},{13,9},{2,6},{6,2},{1... | collective-permute-start | bytes 196616 | tf_op jit(solution)/shard_map/ppermute | solution.py:291
  12.1 4.0 %collective-permute-start.7 = (bf16[1,2,64,128]{3,2,1,0:T(8,128)(2,1)S(1)}, bf16[1,2,64,128]{3,2,1,0:T(8,128)(2,1)S(1)}, u32[]{:S(2)}, u32[]{:S(2)}) collective-permute-start(bf16[1,2,64,128]{3,2,1,0:T(8,128)(2,1)S(1)} %slice.37), channel_id=1, source_target_pairs={{0,8},{4,12},{8,0},{12,4},{1,9},{5,13},{9,1},{13,5},{2,10},{6,14},... | collective-permute-start | bytes 98312 | tf_op jit(solution)/shard_map/ppermute | solution.py:291
  13.8 4.8 %collective-permute-start.4 = (bf16[1,2,64,128]{3,2,1,0:T(8,128)(2,1)S(1)}, bf16[1,2,64,128]{3,2,1,0:T(8,128)(2,1)S(1)}, u32[]{:S(2)}, u32[]{:S(2)}) collective-permute-start(bf16[1,2,64,128]{3,2,1,0:T(8,128)(2,1)S(1)} %slice.33), channel_id=1, source_target_pairs={{0,8},{4,12},{8,0},{12,4},{1,9},{5,13},{9,1},{13,5},{2,10},{6,14},... | collective-permute-start | bytes 98312 | tf_op jit(solution)/shard_map/ppermute | solution.py:291
  16.1 5.6 %collective-permute-start.8 = (bf16[64,128]{1,0:T(8,128)(2,1)S(1)}, bf16[64,128]{1,0:T(8,128)(2,1)S(1)}, u32[]{:S(2)}, u32[]{:S(2)}) collective-permute-start(bf16[64,128]{1,0:T(8,128)(2,1)S(1)} %get-tuple-element.36), channel_id=1, source_target_pairs={{0,1},{1,2},{2,3},{3,0},{4,5},{5,6},{6,7},{7,4},{8,9},{9,10},{10,1... | collective-permute-start | bytes 49160 | tf_op jit(solution)/shard_map/ppermute | solution.py:297
  17.6 4.6 %collective-permute-start.9 = (bf16[64,128]{1,0:T(8,128)(2,1)S(1)}, bf16[64,128]{1,0:T(8,128)(2,1)S(1)}, u32[]{:S(2)}, u32[]{:S(2)}) collective-permute-start(bf16[64,128]{1,0:T(8,128)(2,1)S(1)} %get-tuple-element.35), channel_id=1, source_target_pairs={{0,2},{1,3},{2,0},{3,1},{4,6},{5,7},{6,4},{7,5},{8,10},{9,11},{10,... | collective-permute-start | bytes 49160 | tf_op jit(solution)/shard_map/ppermute | solution.py:297
  18.7 3.8 %collective-permute-start.5 = (bf16[64,128]{1,0:T(8,128)(2,1)S(1)}, bf16[64,128]{1,0:T(8,128)(2,1)S(1)}, u32[]{:S(2)}, u32[]{:S(2)}) collective-permute-start(bf16[64,128]{1,0:T(8,128)(2,1)S(1)} %get-tuple-element.37), channel_id=1, source_target_pairs={{0,3},{1,0},{2,1},{3,2},{4,7},{5,4},{6,5},{7,6},{8,11},{9,8},{10,9... | collective-permute-start | bytes 49160 | tf_op jit(solution)/shard_map/ppermute | solution.py:297

commit v8 on v7

--- a/solution.py
+++ b/solution.py
@@ -14,7 +14,7 @@
 PER_LIST = 2 * CAP
 LANES = 128
 GROUP = 8
-CHUNKS = 1
+CHUNKS = 2
 ROWS = 8
 
 LISTS_ORDER = (0, 1, 3, 2)
@@ -77,24 +77,21 @@
 
 
 def spectra_kernel(
-    sizes, probes_hbm, smatrix_hbm, table_hbm, spectra, row_table, turn, select, beam_turns, *scratch
+    sizes, smatrix_hbm, table_hbm, spectra, row_table, beam_turns, *scratch
 ):
     window, kept, n_tile, n_beam = sizes
     share = kept // n_beam
     me_beam = lax.axis_index("beam")
-    me_tile = lax.axis_index("tile")
-    column_table, smatrix, probes, beam_table, sems = scratch
+    column_table, smatrix, beam_table, sems = scratch
     planes = smatrix.shape[1] // CHUNKS
-    chunks = [pl.ds(i * planes, planes) for i in range(CHUNKS)]
-    copies = [
-        pltpu.make_async_copy(smatrix_hbm.at[:, chunk], smatrix.at[:, chunk], sems.at[i])
-        for i, chunk in enumerate(chunks)
-    ]
-    for copy in copies:
-        copy.start()
-    listed = pltpu.make_async_copy(probes_hbm, probes, sems.at[CHUNKS])
-    listed.start()
-    tabled = pltpu.make_async_copy(table_hbm, beam_table, sems.at[CHUNKS + 1])
+
+    def arrival(i):
+        chunk = pl.ds(i * planes, planes)
+        return pltpu.make_async_copy(smatrix_hbm.at[:, chunk], smatrix.at[:, chunk], sems.at[i])
+
+    for i in range(CHUNKS):
+        arrival(i).start()
+    tabled = pltpu.make_async_copy(table_hbm, beam_table, sems.at[CHUNKS])
     tabled.start()
 
     shape = (2 * window, 2 * kept)
@@ -103,6 +100,19 @@
     v, part_out = lane % kept - kept // 2, lane // kept
     index = x * v + (window // 4) * (part_out - part_in)
     column_table[...] = cosine_of(index, window).astype(bf16)
+
+    def transform(i, carry):
+        arrival(i).wait()
+        chunk = pl.ds(i * planes, planes)
+        flat = jnp.concatenate([smatrix[c, chunk].reshape(planes * window, window) for c in range(2)], axis=1)
+        product = jnp.dot(flat, column_table[...], preferred_element_type=f32)
+        product = product.reshape(planes, window // ROWS, ROWS, 2 * kept)
+        rows = pl.ds(pl.multiple_of(i * planes * ROWS, planes * ROWS), planes * ROWS)
+        for t in range(window // ROWS):
+            spectra[t, rows, :] = product[:, t].reshape(planes * ROWS, 2 * kept).astype(bf16)
+        return carry
+
+    lax.fori_loop(0, CHUNKS, transform, 0)
 
     shape = (2 * kept, 2 * window)
     line, turned = iota(shape, 0) % kept, iota(shape, 0) // kept
@@ -115,9 +125,6 @@
     index = u * r + (window // 4) * (turned - part_in)
     row_table[...] = cosine_of(index, window).astype(bf16)
 
-    u = iota((share, LANES), 0) + me_beam * share - kept // 2
-    lane = iota((share, LANES), 1)
-    v = lane % kept - kept // 2
     tabled.wait()
     beams, wide = beam_table.shape[1], beam_turns.shape[1]
     spread = (iota((beams, wide), 1) // ROWS == iota((beams, wide), 0)).astype(f32)
@@ -127,7 +134,15 @@
         wave_numbers * scale, spread, precision=lax.Precision.HIGHEST, preferred_element_type=f32
     )
 
-    listed.wait()
+
+def homing_kernel(sizes, probes, turn, select):
+    window, kept, n_tile, n_beam = sizes
+    share = kept // n_beam
+    me_beam = lax.axis_index("beam")
+    me_tile = lax.axis_index("tile")
+    u = iota((share, LANES), 0) + me_beam * share - kept // 2
+    lane = iota((share, LANES), 1)
+    v = lane % kept - kept // 2
     shape = (select.shape[0], select.shape[1])
     window_of, slot_of = iota(shape, 0) // share, iota(shape, 1) // share
     wanted = (slot_of == -1, slot_of == -1)
@@ -149,15 +164,6 @@
         turn[1, j * share : (j + 1) * share, :] = series(square, 19) * jnp.where(lane < kept, -angle, angle)
     same_line = iota(shape, 0) % share == iota(shape, 1) % share
     select[...] = jnp.where((wanted[0] | wanted[1]) & same_line, 1.0, 0.0).astype(bf16)
-
-    for i, (copy, chunk) in enumerate(zip(copies, chunks)):
-        copy.wait()
-        flat = jnp.concatenate([smatrix[c, chunk].reshape(planes * window, window) for c in range(2)], axis=1)
-        product = jnp.dot(flat, column_table[...], preferred_element_type=f32)
-        product = product.reshape(planes, window // ROWS, ROWS, 2 * kept)
-        for t in range(window // ROWS):
-            rows = slice(i * planes * ROWS, (i + 1) * planes * ROWS)
-            spectra[t, rows, :] = product[:, t].reshape(planes * ROWS, 2 * kept).astype(bf16)
 
 
 def chosen(lists, me_tile, window, n_tile):
@@ -281,6 +287,7 @@
 
 VMEM = pl.BlockSpec(memory_space=pltpu.VMEM)
 HBM = pl.BlockSpec(memory_space=pltpu.HBM)
+SMEM = pl.BlockSpec(memory_space=pltpu.SMEM)
 
 
 def params(mib=16):
@@ -323,23 +330,32 @@
     lists = lax.optimization_barrier(shifted([probes] * n_tile, 1, lists_order))
     lists = dict(zip(lists_order, lists))
 
-    spectra, row_table, turn, select, beam_turns = pl.pallas_call(
+    turn, select = pl.pallas_call(
+        functools.partial(homing_kernel, sizes),
+        in_specs=[SMEM],
+        out_specs=[VMEM] * 2,
+        out_shape=[
+            jax.ShapeDtypeStruct((2, count * share, LANES), f32),
+            jax.ShapeDtypeStruct((count * share, slots * share), bf16),
+        ],
+        compiler_params=params(),
+        cost_estimate=pl.CostEstimate(flops=1 << 28, bytes_accessed=1 << 20, transcendentals=0),
+        name="homing",
+    )(probes)
+    spectra, row_table, beam_turns = pl.pallas_call(
         functools.partial(spectra_kernel, sizes),
-        in_specs=[HBM, HBM, HBM],
-        out_specs=[VMEM] * 5,
+        in_specs=[HBM, HBM],
+        out_specs=[VMEM] * 3,
         out_shape=[
             jax.ShapeDtypeStruct((window // ROWS, beams * ROWS, 2 * kept), bf16),
             jax.ShapeDtypeStruct((2 * kept, 2 * window), bf16),
-            jax.ShapeDtypeStruct((2, count * share, LANES), f32),
-            jax.ShapeDtypeStruct((count * share, slots * share), bf16),
             jax.ShapeDtypeStruct((3, beams * ROWS), f32),
         ],
         scratch_shapes=[
             pltpu.VMEM((2 * window, 2 * kept), bf16),
             pltpu.VMEM(smatrix.shape, bf16),
-            pltpu.SMEM(probes.shape, i32),
             pltpu.VMEM(beam_table.shape, f32),
-            pltpu.SemaphoreType.DMA((CHUNKS + 2,)),
+            pltpu.SemaphoreType.DMA((CHUNKS + 1,)),
         ],
         compiler_params=params(48),
         cost_estimate=pl.CostEstimate(
@@ -347,7 +363,6 @@
         ),
         name="spectra",
     )(
-        pltpu.with_memory_space_constraint(probes, pltpu.HBM),
         pltpu.with_memory_space_constraint(smatrix, pltpu.HBM),
         pltpu.with_memory_space_constraint(beam_table, pltpu.HBM),
     )

time: 23.6 us -> 23.6 us (level)
  Pallas kernels: 6.15 us -> 6.64 us
  starting transfers between devices: 14.2 us -> 13.9 us
  waiting for transfers between devices: 2.95 us -> 2.69 us
    pallas_call x0 -> x1, Pallas kernels: none -> 0.73 us  [per_device(): pl.pallas_call(functools.partial(homing_kernel, sizes), in_specs=[SMEM],...]
    ppermute x6, waiting for transfers between devices: 1.59 us -> 1.33 us  [shifted(): lax.ppermute(arrays[k], 'tile', [(i, (i + way * k) % size) for i in range...]
    ppermute x6, starting transfers between devices: 11 us -> 10.7 us  [shifted(): lax.ppermute(arrays[k], 'tile', [(i, (i + way * k) % size) for i in range...]
  transfers between devices with their start and end apart: 10 -> 10, of which waited for: 5 -> 5; matrix products, arithmetic and copies ran while one was open for 0% -> 0% of each run, Pallas kernels for 18% -> 21%
where the time goes in v8:
time: 23.6 us; the launch traced here: 23.5 us
  starting transfers between devices  13.9 us (59%)
  Pallas kernels  6.64 us (28%)
  waiting for transfers between devices  2.69 us (11%)
    ppermute x6, starting transfers between devices, shifted(): lax.ppermute(arrays[k], 'tile', [(i, (i + way * k) % size) for i in range...  10.7 us
    pallas_call x1, Pallas kernels, per_device(): pl.pallas_call(functools.partial(spectra_kernel, sizes), in_specs=[HBM, H...  3.35 us
    ppermute x4, starting transfers between devices, swapped(): lax.ppermute(array, axis, [(i, i ^ by) for i in range(lax.axis_size(axis))])  3.22 us
    pallas_call x2, Pallas kernels, parts_call(): pl.pallas_call(functools.partial(kernel, sizes), in_specs=[VMEM] * len(op...  1.58 us
    ppermute x4, waiting for transfers between devices, swapped(): lax.ppermute(array, axis, [(i, i ^ by) for i in range(lax.axis_size(axis))])  1.36 us
    ppermute x6, waiting for transfers between devices, shifted(): lax.ppermute(arrays[k], 'tile', [(i, (i + way * k) % size) for i in range...  1.33 us
    pallas_call x1, Pallas kernels, per_device(): pl.pallas_call(functools.partial(result_kernel, sizes, beams * n_beam), i...  0.99 us
    pallas_call x1, Pallas kernels, per_device(): pl.pallas_call(functools.partial(homing_kernel, sizes), in_specs=[SMEM],...  0.73 us
  transfers between devices with their start and end apart: 10, of which 5 were waited for; matrix products, arithmetic and copies ran while one was open for 0% of the time, Pallas kernels for 21%

profile of v8, /device:TPU:0, one launch (start us, length us, event | category | flops | bytes accessed | tf_op | source)
XLA Modules:
  0.0 23.5 jit_solution(15336022889450766176)
XLA Ops:
  0.0 0.0 copy-start
  0.0 3.0 %collective-permute-start = (s32[2,8]{1,0:T(2,128)}, s32[2,8]{1,0:T(2,128)S(1)}, u32[]{:S(2)}, u32[]{:S(2)}) collective-permute-start(s32[2,8]{1,0:T(2,128)} %bitcast.9), channel_id=1, source_target_pairs={{0,1},{1,2},{2,3},{3,0},{4,5},{5,6},{6,7},{7,4},{8,9},{9,10},{10,1... | collective-permute-start | bytes 200 | tf_op jit(solution)/shard_map/ppermute | solution.py:304
  3.0 2.1 %collective-permute-start.1 = (s32[2,8]{1,0:T(2,128)}, s32[2,8]{1,0:T(2,128)S(1)}, u32[]{:S(2)}, u32[]{:S(2)}) collective-permute-start(s32[2,8]{1,0:T(2,128)} %bitcast.10), channel_id=1, source_target_pairs={{0,3},{1,0},{2,1},{3,2},{4,7},{5,4},{6,5},{7,6},{8,11},{9,8},{10,9... | collective-permute-start | bytes 200 | tf_op jit(solution)/shard_map/ppermute | solution.py:304
  5.1 1.0 %collective-permute-start.2 = (s32[2,8]{1,0:T(2,128)}, s32[2,8]{1,0:T(2,128)S(1)}, u32[]{:S(2)}, u32[]{:S(2)}) collective-permute-start(s32[2,8]{1,0:T(2,128)} %bitcast.11), channel_id=1, source_target_pairs={{0,2},{1,3},{2,0},{3,1},{4,6},{5,7},{6,4},{7,5},{8,10},{9,11},{10,... | collective-permute-start | bytes 200 | tf_op jit(solution)/shard_map/ppermute | solution.py:304
  6.1 3.3 %spectra.1 = (bf16[16,512,128]{2,1,0:T(8,128)(2,1)S(1)}, bf16[128,256]{1,0:T(8,128)(2,1)S(1)}, f32[3,512]{1,0:T(4,128)S(1)}) custom-call(bf16[2,64,128,128]{3,2,1,0:T(8,128)(2,1)} %smatrix_hbm.1, f32[3,64]{1,0:T(4,128)} %table_hbm.1), custom_call_target="tpu_custom_call" | custom-call | flops 536870912 | bytes 6291456 | tf_op jit(solution)/shard_map/spectra/pallas_call | solution.py:345
  9.4 0.0 collective-permute-done.refs_2_
  9.4 0.0 collective-permute-done.1.refs_0_
  9.4 0.3 %collective-permute-done.2.refs_1_ = s32[2,8]{1,0:T(2,128)S(1)} collective-permute-done((s32[2,8]{1,0:T(2,128)}, s32[2,8]{1,0:T(2,128)S(1)}, u32[]{:S(2)}, u32[]{:S(2)}) %collective-permute-start.2) | collective-permute-done | bytes 96 | tf_op jit(solution)/shard_map/ppermute | solution.py:304
  9.8 0.0 copy-done
  9.8 0.8 %coefficients.1 = (bf16[2,2,64,128]{3,2,1,0:T(8,128)(2,1)S(1)}, bf16[2,2,64,128]{3,2,1,0:T(8,128)(2,1)S(1)}, bf16[1,2,4,16,512]{4,3,2,1,0:T(8,128)(2,1)S(1)}, s32[8,128]{1,0:T(8,128)S(1)}) custom-call(s32[2,8]{1,0:T(2,128)S(1)} %collective-permute-done.1.refs_0_, s32[2,8]{1,0:T(2,128)S(1)} %collective-permute-done.2.refs_1_, ...), custom_call_target="tpu_custom_call" | custom-call | flops 268435456 | bytes 4194304 | tf_op jit(solution)/shard_map/coefficients/pallas_call | solution.py:374
  10.6 0.1 collective-permute-start.6
  10.7 0.7 %parts.1 = (bf16[2,2,64,128]{3,2,1,0:T(8,128)(2,1)S(1)}, bf16[2,2,64,128]{3,2,1,0:T(8,128)(2,1)S(1)}) custom-call(bf16[1,2,4,16,512]{4,3,2,1,0:T(8,128)(2,1)S(1)} %get-tuple-element.29.coeff, s32[8,128]{1,0:T(8,128)S(1)} %get-tuple-element.30.offsets, bf16[128,256]{1,0:T(8,128)(2,1)S(1)} %get-tuple-element.27.refs_5_.row_table, ...), custom_call_target="tpu_custom_call" | custom-call | flops 268435456 | bytes 4194304 | tf_op jit(solution)/shard_map/parts/pallas_call | solution.py:374
  11.5 0.6 %collective-permute-start.3 = (bf16[2,2,64,128]{3,2,1,0:T(8,128)(2,1)S(1)}, bf16[2,2,64,128]{3,2,1,0:T(8,128)(2,1)S(1)}, u32[]{:S(2)}, u32[]{:S(2)}) collective-permute-start(bf16[2,2,64,128]{3,2,1,0:T(8,128)(2,1)S(1)} %get-tuple-element.32), channel_id=1, source_target_pairs={{0,4},{4,0},{8,12},{12,8},{1,5},{5,1},{9,13},{13,9},{2,6},{6,2},{1... | collective-permute-start | bytes 196616 | tf_op jit(solution)/shard_map/ppermute | solution.py:298
  12.0 0.0 collective-permute-done.6
  12.1 1.7 %collective-permute-start.7 = (bf16[1,2,64,128]{3,2,1,0:T(8,128)(2,1)S(1)}, bf16[1,2,64,128]{3,2,1,0:T(8,128)(2,1)S(1)}, u32[]{:S(2)}, u32[]{:S(2)}) collective-permute-start(bf16[1,2,64,128]{3,2,1,0:T(8,128)(2,1)S(1)} %slice.37), channel_id=1, source_target_pairs={{0,8},{4,12},{8,0},{12,4},{1,9},{5,13},{9,1},{13,5},{2,10},{6,14},... | collective-permute-start | bytes 98312 | tf_op jit(solution)/shard_map/ppermute | solution.py:298
  13.8 0.0 collective-permute-done.3
  13.8 0.9 %collective-permute-start.4 = (bf16[1,2,64,128]{3,2,1,0:T(8,128)(2,1)S(1)}, bf16[1,2,64,128]{3,2,1,0:T(8,128)(2,1)S(1)}, u32[]{:S(2)}, u32[]{:S(2)}) collective-permute-start(bf16[1,2,64,128]{3,2,1,0:T(8,128)(2,1)S(1)} %slice.33), channel_id=1, source_target_pairs={{0,8},{4,12},{8,0},{12,4},{1,9},{5,13},{9,1},{13,5},{2,10},{6,14},... | collective-permute-start | bytes 98312 | tf_op jit(solution)/shard_map/ppermute | solution.py:298
  14.7 1.3 %collective-permute-done.7 = bf16[1,2,64,128]{3,2,1,0:T(8,128)(2,1)S(1)} collective-permute-done((bf16[1,2,64,128]{3,2,1,0:T(8,128)(2,1)S(1)}, bf16[1,2,64,128]{3,2,1,0:T(8,128)(2,1)S(1)}, u32[]{:S(2)}, u32[]{:S(2)}) %collective-permute-start.7) | collective-permute-done | bytes 32800 | tf_op jit(solution)/shard_map/ppermute | solution.py:298
  16.1 1.3 %collective-permute-start.8 = (bf16[64,128]{1,0:T(8,128)(2,1)S(1)}, bf16[64,128]{1,0:T(8,128)(2,1)S(1)}, u32[]{:S(2)}, u32[]{:S(2)}) collective-permute-start(bf16[64,128]{1,0:T(8,128)(2,1)S(1)} %get-tuple-element.36), channel_id=1, source_target_pairs={{0,1},{1,2},{2,3},{3,0},{4,5},{5,6},{6,7},{7,4},{8,9},{9,10},{10,1... | collective-permute-start | bytes 49160 | tf_op jit(solution)/shard_map/ppermute | solution.py:304
  17.4 1.3 %collective-permute-start.9 = (bf16[64,128]{1,0:T(8,128)(2,1)S(1)}, bf16[64,128]{1,0:T(8,128)(2,1)S(1)}, u32[]{:S(2)}, u32[]{:S(2)}) collective-permute-start(bf16[64,128]{1,0:T(8,128)(2,1)S(1)} %get-tuple-element.35), channel_id=1, source_target_pairs={{0,2},{1,3},{2,0},{3,1},{4,6},{5,7},{6,4},{7,5},{8,10},{9,11},{10,... | collective-permute-start | bytes 49160 | tf_op jit(solution)/shard_map/ppermute | solution.py:304
  18.7 0.0 collective-permute-done.4
  18.7 2.1 %collective-permute-start.5 = (bf16[64,128]{1,0:T(8,128)(2,1)S(1)}, bf16[64,128]{1,0:T(8,128)(2,1)S(1)}, u32[]{:S(2)}, u32[]{:S(2)}) collective-permute-start(bf16[64,128]{1,0:T(8,128)(2,1)S(1)} %get-tuple-element.37), channel_id=1, source_target_pairs={{0,3},{1,0},{2,1},{3,2},{4,7},{5,4},{6,5},{7,6},{8,11},{9,8},{10,9... | collective-permute-start | bytes 49160 | tf_op jit(solution)/shard_map/ppermute | solution.py:304
  20.8 0.7 %homing.1 = (f32[2,128,128]{2,1,0:T(8,128)S(1)}, bf16[128,256]{1,0:T(8,128)(2,1)S(1)}) custom-call(s32[2,8]{1,0:T(2,128)S(1)} %bitcast.13), custom_call_target="tpu_custom_call" | custom-call | flops 268435456 | bytes 1048576 | tf_op jit(solution)/shard_map/homing/pallas_call | solution.py:333
  21.5 0.2 collective-permute-done.8.refs_4_
  21.7 0.4 %collective-permute-done.9.refs_5_ = bf16[64,128]{1,0:T(8,128)(2,1)S(1)} collective-permute-done((bf16[64,128]{1,0:T(8,128)(2,1)S(1)}, bf16[64,128]{1,0:T(8,128)(2,1)S(1)}, u32[]{:S(2)}, u32[]{:S(2)}) %collective-permute-start.9) | collective-permute-done | bytes 16416 | tf_op jit(solution)/shard_map/ppermute | solution.py:304
  22.0 0.5 %collective-permute-done.5.refs_3_ = bf16[64,128]{1,0:T(8,128)(2,1)S(1)} collective-permute-done((bf16[64,128]{1,0:T(8,128)(2,1)S(1)}, bf16[64,128]{1,0:T(8,128)(2,1)S(1)}, u32[]{:S(2)}, u32[]{:S(2)}) %collective-permute-start.5) | collective-permute-done | bytes 16416 | tf_op jit(solution)/shard_map/ppermute | solution.py:304
  22.5 1.0 %result.1 = f32[8,8,32]{2,1,0:T(8,128)} custom-call(f32[2,128,128]{2,1,0:T(8,128)S(1)} %get-tuple-element.20.refs_0_, bf16[128,256]{1,0:T(8,128)(2,1)S(1)} %get-tuple-element.21.refs_1_, bf16[64,128]{1,0:T(8,128)(2,1)S(1)} %get-tuple-element.38.refs_2_, bf16[64,128]{1,0:T(8,128)(2,1)S(1)} %collective-permute-done.5.refs_3_, ...), custom_call_target="tpu_custom_call" | custom-call | tf_op jit(solution)/shard_map/result/pallas_call | solution.py:418
  (8 shorter events, 0.1 us)
Async XLA Ops:
  0.0 9.8 %copy-start = (s32[8,2]{0,1:T(2,128)S(1)}, s32[8,2]{0,1:T(2,128)}, u32[]{:S(2)}) copy-start(s32[8,2]{0,1:T(2,128)} %param.5) | copy-start | bytes 196
  0.0 9.4 %collective-permute-start = (s32[2,8]{1,0:T(2,128)}, s32[2,8]{1,0:T(2,128)S(1)}, u32[]{:S(2)}, u32[]{:S(2)}) collective-permute-start(s32[2,8]{1,0:T(2,128)} %bitcast.9), channel_id=1, source_target_pairs={{0,1},{1,2},{2,3},{3,0},{4,5},{5,6},{6,7},{7,4},{8,9},{9,10},{10,1... | collective-permute-start | bytes 200 | tf_op jit(solution)/shard_map/ppermute | solution.py:304
  3.0 6.4 %collective-permute-start.1 = (s32[2,8]{1,0:T(2,128)}, s32[2,8]{1,0:T(2,128)S(1)}, u32[]{:S(2)}, u32[]{:S(2)}) collective-permute-start(s32[2,8]{1,0:T(2,128)} %bitcast.10), channel_id=1, source_target_pairs={{0,3},{1,0},{2,1},{3,2},{4,7},{5,4},{6,5},{7,6},{8,11},{9,8},{10,9... | collective-permute-start | bytes 200 | tf_op jit(solution)/shard_map/ppermute | solution.py:304
  5.1 4.7 %collective-permute-start.2 = (s32[2,8]{1,0:T(2,128)}, s32[2,8]{1,0:T(2,128)S(1)}, u32[]{:S(2)}, u32[]{:S(2)}) collective-permute-start(s32[2,8]{1,0:T(2,128)} %bitcast.11), channel_id=1, source_target_pairs={{0,2},{1,3},{2,0},{3,1},{4,6},{5,7},{6,4},{7,5},{8,10},{9,11},{10,... | collective-permute-start | bytes 200 | tf_op jit(solution)/shard_map/ppermute | solution.py:304
  10.6 1.4 %collective-permute-start.6 = (bf16[2,2,64,128]{3,2,1,0:T(8,128)(2,1)S(1)}, bf16[2,2,64,128]{3,2,1,0:T(8,128)(2,1)S(1)}, u32[]{:S(2)}, u32[]{:S(2)}) collective-permute-start(bf16[2,2,64,128]{3,2,1,0:T(8,128)(2,1)S(1)} %get-tuple-element.34), channel_id=1, source_target_pairs={{0,4},{4,0},{8,12},{12,8},{1,5},{5,1},{9,13},{13,9},{2,6},{6,2},{1... | collective-permute-start | bytes 196616 | tf_op jit(solution)/shard_map/ppermute | solution.py:298
  11.5 2.3 %collective-permute-start.3 = (bf16[2,2,64,128]{3,2,1,0:T(8,128)(2,1)S(1)}, bf16[2,2,64,128]{3,2,1,0:T(8,128)(2,1)S(1)}, u32[]{:S(2)}, u32[]{:S(2)}) collective-permute-start(bf16[2,2,64,128]{3,2,1,0:T(8,128)(2,1)S(1)} %get-tuple-element.32), channel_id=1, source_target_pairs={{0,4},{4,0},{8,12},{12,8},{1,5},{5,1},{9,13},{13,9},{2,6},{6,2},{1... | collective-permute-start | bytes 196616 | tf_op jit(solution)/shard_map/ppermute | solution.py:298
  12.1 4.0 %collective-permute-start.7 = (bf16[1,2,64,128]{3,2,1,0:T(8,128)(2,1)S(1)}, bf16[1,2,64,128]{3,2,1,0:T(8,128)(2,1)S(1)}, u32[]{:S(2)}, u32[]{:S(2)}) collective-permute-start(bf16[1,2,64,128]{3,2,1,0:T(8,128)(2,1)S(1)} %slice.37), channel_id=1, source_target_pairs={{0,8},{4,12},{8,0},{12,4},{1,9},{5,13},{9,1},{13,5},{2,10},{6,14},... | collective-permute-start | bytes 98312 | tf_op jit(solution)/shard_map/ppermute | solution.py:298
  13.8 4.8 %collective-permute-start.4 = (bf16[1,2,64,128]{3,2,1,0:T(8,128)(2,1)S(1)}, bf16[1,2,64,128]{3,2,1,0:T(8,128)(2,1)S(1)}, u32[]{:S(2)}, u32[]{:S(2)}) collective-permute-start(bf16[1,2,64,128]{3,2,1,0:T(8,128)(2,1)S(1)} %slice.33), channel_id=1, source_target_pairs={{0,8},{4,12},{8,0},{12,4},{1,9},{5,13},{9,1},{13,5},{2,10},{6,14},... | collective-permute-start | bytes 98312 | tf_op jit(solution)/shard_map/ppermute | solution.py:298
  16.1 5.6 %collective-permute-start.8 = (bf16[64,128]{1,0:T(8,128)(2,1)S(1)}, bf16[64,128]{1,0:T(8,128)(2,1)S(1)}, u32[]{:S(2)}, u32[]{:S(2)}) collective-permute-start(bf16[64,128]{1,0:T(8,128)(2,1)S(1)} %get-tuple-element.36), channel_id=1, source_target_pairs={{0,1},{1,2},{2,3},{3,0},{4,5},{5,6},{6,7},{7,4},{8,9},{9,10},{10,1... | collective-permute-start | bytes 49160 | tf_op jit(solution)/shard_map/ppermute | solution.py:304
  17.4 4.6 %collective-permute-start.9 = (bf16[64,128]{1,0:T(8,128)(2,1)S(1)}, bf16[64,128]{1,0:T(8,128)(2,1)S(1)}, u32[]{:S(2)}, u32[]{:S(2)}) collective-permute-start(bf16[64,128]{1,0:T(8,128)(2,1)S(1)} %get-tuple-element.35), channel_id=1, source_target_pairs={{0,2},{1,3},{2,0},{3,1},{4,6},{5,7},{6,4},{7,5},{8,10},{9,11},{10,... | collective-permute-start | bytes 49160 | tf_op jit(solution)/shard_map/ppermute | solution.py:304
  18.7 3.8 %collective-permute-start.5 = (bf16[64,128]{1,0:T(8,128)(2,1)S(1)}, bf16[64,128]{1,0:T(8,128)(2,1)S(1)}, u32[]{:S(2)}, u32[]{:S(2)}) collective-permute-start(bf16[64,128]{1,0:T(8,128)(2,1)S(1)} %get-tuple-element.37), channel_id=1, source_target_pairs={{0,3},{1,0},{2,1},{3,2},{4,7},{5,4},{6,5},{7,6},{8,11},{9,8},{10,9... | collective-permute-start | bytes 49160 | tf_op jit(solution)/shard_map/ppermute | solution.py:304

commit v9 on v8

--- a/solution.py
+++ b/solution.py
@@ -100,6 +100,17 @@
     v, part_out = lane % kept - kept // 2, lane // kept
     index = x * v + (window // 4) * (part_out - part_in)
     column_table[...] = cosine_of(index, window).astype(bf16)
+
+    shape = (2 * kept, 2 * window)
+    line, turned = iota(shape, 0) % kept, iota(shape, 0) // kept
+    r, part_in = iota(shape, 1) % window, iota(shape, 1) // window
+    block = line // share
+    owner = jnp.zeros_like(block)
+    for pos in range(n_beam):
+        owner = jnp.where(block == pos, jnp.bitwise_xor(me_beam, bit_reversed(pos, n_beam)), owner)
+    u = owner * share + line % share - kept // 2
+    index = u * r + (window // 4) * (turned - part_in)
+    row_table[...] = cosine_of(index, window).astype(bf16)
 
     def transform(i, carry):
         arrival(i).wait()
@@ -114,25 +125,17 @@
 
     lax.fori_loop(0, CHUNKS, transform, 0)
 
-    shape = (2 * kept, 2 * window)
-    line, turned = iota(shape, 0) % kept, iota(shape, 0) // kept
-    r, part_in = iota(shape, 1) % window, iota(shape, 1) // window
-    block = line // share
-    owner = jnp.zeros_like(block)
-    for pos in range(n_beam):
-        owner = jnp.where(block == pos, jnp.bitwise_xor(me_beam, bit_reversed(pos, n_beam)), owner)
-    u = owner * share + line % share - kept // 2
-    index = u * r + (window // 4) * (turned - part_in)
-    row_table[...] = cosine_of(index, window).astype(bf16)
-
     tabled.wait()
     beams, wide = beam_table.shape[1], beam_turns.shape[1]
-    spread = (iota((beams, wide), 1) // ROWS == iota((beams, wide), 0)).astype(f32)
-    wave_numbers = beam_table[...]
-    scale = jnp.where(iota(wave_numbers.shape, 0) < 2, 1.0 / (window * IF), 1.0 / two_pi)
-    beam_turns[...] = jnp.dot(
-        wave_numbers * scale, spread, precision=lax.Precision.HIGHEST, preferred_element_type=f32
-    )
+    spread = (iota((beams, wide), 1) // ROWS == iota((beams, wide), 0)).astype(f32).astype(bf16)
+    left = beam_table[...]
+    left = left * jnp.where(iota(left.shape, 0) < 2, 1.0 / (window * IF), 1.0 / two_pi)
+    pieces = []
+    for _ in range(3):
+        piece = left.astype(bf16)
+        left = left - piece.astype(f32)
+        pieces.append(jnp.dot(piece, spread, preferred_element_type=f32))
+    beam_turns[...] = pieces[0] + (pieces[1] + pieces[2])
 
 
 def homing_kernel(sizes, probes, turn, select):

time: 23.6 us -> 23.6 us (level)
  waiting for transfers between devices: 2.69 us -> 3.01 us
    ppermute x6, waiting for transfers between devices: 1.33 us -> 1.65 us  [shifted(): lax.ppermute(arrays[k], 'tile', [(i, (i + way * k) % size) for i in range...]
  transfers between devices with their start and end apart: 10 -> 10, of which waited for: 5 -> 5; matrix products, arithmetic and copies ran while one was open for 0% -> 0% of each run, Pallas kernels for 21% -> 20%
where the time goes in v9:
time: 23.6 us; the launch traced here: 23.5 us
  starting transfers between devices  13.8 us (58%)
  Pallas kernels  6.48 us (27%)
  waiting for transfers between devices  3.01 us (13%)
    ppermute x6, starting transfers between devices, shifted(): lax.ppermute(arrays[k], 'tile', [(i, (i + way * k) % size) for i in range...  10.6 us
    ppermute x4, starting transfers between devices, swapped(): lax.ppermute(array, axis, [(i, i ^ by) for i in range(lax.axis_size(axis))])  3.22 us
    pallas_call x1, Pallas kernels, per_device(): pl.pallas_call(functools.partial(spectra_kernel, sizes), in_specs=[HBM, H...  3.19 us
    ppermute x6, waiting for transfers between devices, shifted(): lax.ppermute(arrays[k], 'tile', [(i, (i + way * k) % size) for i in range...  1.65 us
    pallas_call x2, Pallas kernels, parts_call(): pl.pallas_call(functools.partial(kernel, sizes), in_specs=[VMEM] * len(op...  1.58 us
    ppermute x4, waiting for transfers between devices, swapped(): lax.ppermute(array, axis, [(i, i ^ by) for i in range(lax.axis_size(axis))])  1.36 us
    pallas_call x1, Pallas kernels, per_device(): pl.pallas_call(functools.partial(result_kernel, sizes, beams * n_beam), i...  0.99 us
    pallas_call x1, Pallas kernels, per_device(): pl.pallas_call(functools.partial(homing_kernel, sizes), in_specs=[SMEM],...  0.73 us
  transfers between devices with their start and end apart: 10, of which 5 were waited for; matrix products, arithmetic and copies ran while one was open for 0% of the time, Pallas kernels for 20%

profile of v9, /device:TPU:0, one launch (start us, length us, event | category | flops | bytes accessed | tf_op | source)
XLA Modules:
  0.0 23.5 jit_solution(8042467632365494547)
XLA Ops:
  0.0 0.0 copy-start
  0.0 3.0 %collective-permute-start = (s32[2,8]{1,0:T(2,128)}, s32[2,8]{1,0:T(2,128)S(1)}, u32[]{:S(2)}, u32[]{:S(2)}) collective-permute-start(s32[2,8]{1,0:T(2,128)} %bitcast.9), channel_id=1, source_target_pairs={{0,1},{1,2},{2,3},{3,0},{4,5},{5,6},{6,7},{7,4},{8,9},{9,10},{10,1... | collective-permute-start | bytes 200 | tf_op jit(solution)/shard_map/ppermute | solution.py:307
  3.0 2.1 %collective-permute-start.1 = (s32[2,8]{1,0:T(2,128)}, s32[2,8]{1,0:T(2,128)S(1)}, u32[]{:S(2)}, u32[]{:S(2)}) collective-permute-start(s32[2,8]{1,0:T(2,128)} %bitcast.10), channel_id=1, source_target_pairs={{0,3},{1,0},{2,1},{3,2},{4,7},{5,4},{6,5},{7,6},{8,11},{9,8},{10,9... | collective-permute-start | bytes 200 | tf_op jit(solution)/shard_map/ppermute | solution.py:307
  5.1 1.0 %collective-permute-start.2 = (s32[2,8]{1,0:T(2,128)}, s32[2,8]{1,0:T(2,128)S(1)}, u32[]{:S(2)}, u32[]{:S(2)}) collective-permute-start(s32[2,8]{1,0:T(2,128)} %bitcast.11), channel_id=1, source_target_pairs={{0,2},{1,3},{2,0},{3,1},{4,6},{5,7},{6,4},{7,5},{8,10},{9,11},{10,... | collective-permute-start | bytes 200 | tf_op jit(solution)/shard_map/ppermute | solution.py:307
  6.1 3.2 %spectra.1 = (bf16[16,512,128]{2,1,0:T(8,128)(2,1)S(1)}, bf16[128,256]{1,0:T(8,128)(2,1)S(1)}, f32[3,512]{1,0:T(4,128)S(1)}) custom-call(bf16[2,64,128,128]{3,2,1,0:T(8,128)(2,1)} %smatrix_hbm.1, f32[3,64]{1,0:T(4,128)} %table_hbm.1), custom_call_target="tpu_custom_call" | custom-call | flops 536870912 | bytes 6291456 | tf_op jit(solution)/shard_map/spectra/pallas_call | solution.py:348
  9.3 0.0 collective-permute-done.refs_2_
  9.3 0.0 collective-permute-done.1.refs_0_
  9.3 0.5 %collective-permute-done.2.refs_1_ = s32[2,8]{1,0:T(2,128)S(1)} collective-permute-done((s32[2,8]{1,0:T(2,128)}, s32[2,8]{1,0:T(2,128)S(1)}, u32[]{:S(2)}, u32[]{:S(2)}) %collective-permute-start.2) | collective-permute-done | bytes 96 | tf_op jit(solution)/shard_map/ppermute | solution.py:307
  9.8 0.0 copy-done
  9.8 0.8 %coefficients.1 = (bf16[2,2,64,128]{3,2,1,0:T(8,128)(2,1)S(1)}, bf16[2,2,64,128]{3,2,1,0:T(8,128)(2,1)S(1)}, bf16[1,2,4,16,512]{4,3,2,1,0:T(8,128)(2,1)S(1)}, s32[8,128]{1,0:T(8,128)S(1)}) custom-call(s32[2,8]{1,0:T(2,128)S(1)} %collective-permute-done.1.refs_0_, s32[2,8]{1,0:T(2,128)S(1)} %collective-permute-done.2.refs_1_, ...), custom_call_target="tpu_custom_call" | custom-call | flops 268435456 | bytes 4194304 | tf_op jit(solution)/shard_map/coefficients/pallas_call | solution.py:377
  10.6 0.1 collective-permute-start.6
  10.7 0.7 %parts.1 = (bf16[2,2,64,128]{3,2,1,0:T(8,128)(2,1)S(1)}, bf16[2,2,64,128]{3,2,1,0:T(8,128)(2,1)S(1)}) custom-call(bf16[1,2,4,16,512]{4,3,2,1,0:T(8,128)(2,1)S(1)} %get-tuple-element.29.coeff, s32[8,128]{1,0:T(8,128)S(1)} %get-tuple-element.30.offsets, bf16[128,256]{1,0:T(8,128)(2,1)S(1)} %get-tuple-element.27.refs_5_.row_table, ...), custom_call_target="tpu_custom_call" | custom-call | flops 268435456 | bytes 4194304 | tf_op jit(solution)/shard_map/parts/pallas_call | solution.py:377
  11.5 0.6 %collective-permute-start.3 = (bf16[2,2,64,128]{3,2,1,0:T(8,128)(2,1)S(1)}, bf16[2,2,64,128]{3,2,1,0:T(8,128)(2,1)S(1)}, u32[]{:S(2)}, u32[]{:S(2)}) collective-permute-start(bf16[2,2,64,128]{3,2,1,0:T(8,128)(2,1)S(1)} %get-tuple-element.32), channel_id=1, source_target_pairs={{0,4},{4,0},{8,12},{12,8},{1,5},{5,1},{9,13},{13,9},{2,6},{6,2},{1... | collective-permute-start | bytes 196616 | tf_op jit(solution)/shard_map/ppermute | solution.py:301
  12.0 0.0 collective-permute-done.6
  12.1 1.7 %collective-permute-start.7 = (bf16[1,2,64,128]{3,2,1,0:T(8,128)(2,1)S(1)}, bf16[1,2,64,128]{3,2,1,0:T(8,128)(2,1)S(1)}, u32[]{:S(2)}, u32[]{:S(2)}) collective-permute-start(bf16[1,2,64,128]{3,2,1,0:T(8,128)(2,1)S(1)} %slice.37), channel_id=1, source_target_pairs={{0,8},{4,12},{8,0},{12,4},{1,9},{5,13},{9,1},{13,5},{2,10},{6,14},... | collective-permute-start | bytes 98312 | tf_op jit(solution)/shard_map/ppermute | solution.py:301
  13.8 0.0 collective-permute-done.3
  13.8 0.9 %collective-permute-start.4 = (bf16[1,2,64,128]{3,2,1,0:T(8,128)(2,1)S(1)}, bf16[1,2,64,128]{3,2,1,0:T(8,128)(2,1)S(1)}, u32[]{:S(2)}, u32[]{:S(2)}) collective-permute-start(bf16[1,2,64,128]{3,2,1,0:T(8,128)(2,1)S(1)} %slice.33), channel_id=1, source_target_pairs={{0,8},{4,12},{8,0},{12,4},{1,9},{5,13},{9,1},{13,5},{2,10},{6,14},... | collective-permute-start | bytes 98312 | tf_op jit(solution)/shard_map/ppermute | solution.py:301
  14.7 1.3 %collective-permute-done.7 = bf16[1,2,64,128]{3,2,1,0:T(8,128)(2,1)S(1)} collective-permute-done((bf16[1,2,64,128]{3,2,1,0:T(8,128)(2,1)S(1)}, bf16[1,2,64,128]{3,2,1,0:T(8,128)(2,1)S(1)}, u32[]{:S(2)}, u32[]{:S(2)}) %collective-permute-start.7) | collective-permute-done | bytes 32800 | tf_op jit(solution)/shard_map/ppermute | solution.py:301
  16.1 1.2 %collective-permute-start.8 = (bf16[64,128]{1,0:T(8,128)(2,1)S(1)}, bf16[64,128]{1,0:T(8,128)(2,1)S(1)}, u32[]{:S(2)}, u32[]{:S(2)}) collective-permute-start(bf16[64,128]{1,0:T(8,128)(2,1)S(1)} %get-tuple-element.36), channel_id=1, source_target_pairs={{0,1},{1,2},{2,3},{3,0},{4,5},{5,6},{6,7},{7,4},{8,9},{9,10},{10,1... | collective-permute-start | bytes 49160 | tf_op jit(solution)/shard_map/ppermute | solution.py:307
  17.2 1.4 %collective-permute-start.9 = (bf16[64,128]{1,0:T(8,128)(2,1)S(1)}, bf16[64,128]{1,0:T(8,128)(2,1)S(1)}, u32[]{:S(2)}, u32[]{:S(2)}) collective-permute-start(bf16[64,128]{1,0:T(8,128)(2,1)S(1)} %get-tuple-element.35), channel_id=1, source_target_pairs={{0,2},{1,3},{2,0},{3,1},{4,6},{5,7},{6,4},{7,5},{8,10},{9,11},{10,... | collective-permute-start | bytes 49160 | tf_op jit(solution)/shard_map/ppermute | solution.py:307
  18.7 0.0 collective-permute-done.4
  18.7 1.9 %collective-permute-start.5 = (bf16[64,128]{1,0:T(8,128)(2,1)S(1)}, bf16[64,128]{1,0:T(8,128)(2,1)S(1)}, u32[]{:S(2)}, u32[]{:S(2)}) collective-permute-start(bf16[64,128]{1,0:T(8,128)(2,1)S(1)} %get-tuple-element.37), channel_id=1, source_target_pairs={{0,3},{1,0},{2,1},{3,2},{4,7},{5,4},{6,5},{7,6},{8,11},{9,8},{10,9... | collective-permute-start | bytes 49160 | tf_op jit(solution)/shard_map/ppermute | solution.py:307
  20.6 0.7 %homing.1 = (f32[2,128,128]{2,1,0:T(8,128)S(1)}, bf16[128,256]{1,0:T(8,128)(2,1)S(1)}) custom-call(s32[2,8]{1,0:T(2,128)S(1)} %bitcast.13), custom_call_target="tpu_custom_call" | custom-call | flops 268435456 | bytes 1048576 | tf_op jit(solution)/shard_map/homing/pallas_call | solution.py:336
  21.3 0.3 %collective-permute-done.8.refs_4_ = bf16[64,128]{1,0:T(8,128)(2,1)S(1)} collective-permute-done((bf16[64,128]{1,0:T(8,128)(2,1)S(1)}, bf16[64,128]{1,0:T(8,128)(2,1)S(1)}, u32[]{:S(2)}, u32[]{:S(2)}) %collective-permute-start.8) | collective-permute-done | bytes 16416 | tf_op jit(solution)/shard_map/ppermute | solution.py:307
  21.7 0.2 collective-permute-done.9.refs_5_
  21.9 0.6 %collective-permute-done.5.refs_3_ = bf16[64,128]{1,0:T(8,128)(2,1)S(1)} collective-permute-done((bf16[64,128]{1,0:T(8,128)(2,1)S(1)}, bf16[64,128]{1,0:T(8,128)(2,1)S(1)}, u32[]{:S(2)}, u32[]{:S(2)}) %collective-permute-start.5) | collective-permute-done | bytes 16416 | tf_op jit(solution)/shard_map/ppermute | solution.py:307
  22.5 1.0 %result.1 = f32[8,8,32]{2,1,0:T(8,128)} custom-call(f32[2,128,128]{2,1,0:T(8,128)S(1)} %get-tuple-element.20.refs_0_, bf16[128,256]{1,0:T(8,128)(2,1)S(1)} %get-tuple-element.21.refs_1_, bf16[64,128]{1,0:T(8,128)(2,1)S(1)} %get-tuple-element.38.refs_2_, bf16[64,128]{1,0:T(8,128)(2,1)S(1)} %collective-permute-done.5.refs_3_, ...), custom_call_target="tpu_custom_call" | custom-call | tf_op jit(solution)/shard_map/result/pallas_call | solution.py:421
  (8 shorter events, 0.1 us)
Async XLA Ops:
  0.0 9.8 %copy-start = (s32[8,2]{0,1:T(2,128)S(1)}, s32[8,2]{0,1:T(2,128)}, u32[]{:S(2)}) copy-start(s32[8,2]{0,1:T(2,128)} %param.5) | copy-start | bytes 196
  0.0 9.3 %collective-permute-start = (s32[2,8]{1,0:T(2,128)}, s32[2,8]{1,0:T(2,128)S(1)}, u32[]{:S(2)}, u32[]{:S(2)}) collective-permute-start(s32[2,8]{1,0:T(2,128)} %bitcast.9), channel_id=1, source_target_pairs={{0,1},{1,2},{2,3},{3,0},{4,5},{5,6},{6,7},{7,4},{8,9},{9,10},{10,1... | collective-permute-start | bytes 200 | tf_op jit(solution)/shard_map/ppermute | solution.py:307
  3.0 6.3 %collective-permute-start.1 = (s32[2,8]{1,0:T(2,128)}, s32[2,8]{1,0:T(2,128)S(1)}, u32[]{:S(2)}, u32[]{:S(2)}) collective-permute-start(s32[2,8]{1,0:T(2,128)} %bitcast.10), channel_id=1, source_target_pairs={{0,3},{1,0},{2,1},{3,2},{4,7},{5,4},{6,5},{7,6},{8,11},{9,8},{10,9... | collective-permute-start | bytes 200 | tf_op jit(solution)/shard_map/ppermute | solution.py:307
  5.1 4.7 %collective-permute-start.2 = (s32[2,8]{1,0:T(2,128)}, s32[2,8]{1,0:T(2,128)S(1)}, u32[]{:S(2)}, u32[]{:S(2)}) collective-permute-start(s32[2,8]{1,0:T(2,128)} %bitcast.11), channel_id=1, source_target_pairs={{0,2},{1,3},{2,0},{3,1},{4,6},{5,7},{6,4},{7,5},{8,10},{9,11},{10,... | collective-permute-start | bytes 200 | tf_op jit(solution)/shard_map/ppermute | solution.py:307
  10.6 1.4 %collective-permute-start.6 = (bf16[2,2,64,128]{3,2,1,0:T(8,128)(2,1)S(1)}, bf16[2,2,64,128]{3,2,1,0:T(8,128)(2,1)S(1)}, u32[]{:S(2)}, u32[]{:S(2)}) collective-permute-start(bf16[2,2,64,128]{3,2,1,0:T(8,128)(2,1)S(1)} %get-tuple-element.34), channel_id=1, source_target_pairs={{0,4},{4,0},{8,12},{12,8},{1,5},{5,1},{9,13},{13,9},{2,6},{6,2},{1... | collective-permute-start | bytes 196616 | tf_op jit(solution)/shard_map/ppermute | solution.py:301
  11.5 2.3 %collective-permute-start.3 = (bf16[2,2,64,128]{3,2,1,0:T(8,128)(2,1)S(1)}, bf16[2,2,64,128]{3,2,1,0:T(8,128)(2,1)S(1)}, u32[]{:S(2)}, u32[]{:S(2)}) collective-permute-start(bf16[2,2,64,128]{3,2,1,0:T(8,128)(2,1)S(1)} %get-tuple-element.32), channel_id=1, source_target_pairs={{0,4},{4,0},{8,12},{12,8},{1,5},{5,1},{9,13},{13,9},{2,6},{6,2},{1... | collective-permute-start | bytes 196616 | tf_op jit(solution)/shard_map/ppermute | solution.py:301
  12.1 4.0 %collective-permute-start.7 = (bf16[1,2,64,128]{3,2,1,0:T(8,128)(2,1)S(1)}, bf16[1,2,64,128]{3,2,1,0:T(8,128)(2,1)S(1)}, u32[]{:S(2)}, u32[]{:S(2)}) collective-permute-start(bf16[1,2,64,128]{3,2,1,0:T(8,128)(2,1)S(1)} %slice.37), channel_id=1, source_target_pairs={{0,8},{4,12},{8,0},{12,4},{1,9},{5,13},{9,1},{13,5},{2,10},{6,14},... | collective-permute-start | bytes 98312 | tf_op jit(solution)/shard_map/ppermute | solution.py:301
  13.8 4.8 %collective-permute-start.4 = (bf16[1,2,64,128]{3,2,1,0:T(8,128)(2,1)S(1)}, bf16[1,2,64,128]{3,2,1,0:T(8,128)(2,1)S(1)}, u32[]{:S(2)}, u32[]{:S(2)}) collective-permute-start(bf16[1,2,64,128]{3,2,1,0:T(8,128)(2,1)S(1)} %slice.33), channel_id=1, source_target_pairs={{0,8},{4,12},{8,0},{12,4},{1,9},{5,13},{9,1},{13,5},{2,10},{6,14},... | collective-permute-start | bytes 98312 | tf_op jit(solution)/shard_map/ppermute | solution.py:301
  16.1 5.6 %collective-permute-start.8 = (bf16[64,128]{1,0:T(8,128)(2,1)S(1)}, bf16[64,128]{1,0:T(8,128)(2,1)S(1)}, u32[]{:S(2)}, u32[]{:S(2)}) collective-permute-start(bf16[64,128]{1,0:T(8,128)(2,1)S(1)} %get-tuple-element.36), channel_id=1, source_target_pairs={{0,1},{1,2},{2,3},{3,0},{4,5},{5,6},{6,7},{7,4},{8,9},{9,10},{10,1... | collective-permute-start | bytes 49160 | tf_op jit(solution)/shard_map/ppermute | solution.py:307
  17.2 4.6 %collective-permute-start.9 = (bf16[64,128]{1,0:T(8,128)(2,1)S(1)}, bf16[64,128]{1,0:T(8,128)(2,1)S(1)}, u32[]{:S(2)}, u32[]{:S(2)}) collective-permute-start(bf16[64,128]{1,0:T(8,128)(2,1)S(1)} %get-tuple-element.35), channel_id=1, source_target_pairs={{0,2},{1,3},{2,0},{3,1},{4,6},{5,7},{6,4},{7,5},{8,10},{9,11},{10,... | collective-permute-start | bytes 49160 | tf_op jit(solution)/shard_map/ppermute | solution.py:307
  18.7 3.8 %collective-permute-start.5 = (bf16[64,128]{1,0:T(8,128)(2,1)S(1)}, bf16[64,128]{1,0:T(8,128)(2,1)S(1)}, u32[]{:S(2)}, u32[]{:S(2)}) collective-permute-start(bf16[64,128]{1,0:T(8,128)(2,1)S(1)} %get-tuple-element.37), channel_id=1, source_target_pairs={{0,3},{1,0},{2,1},{3,2},{4,7},{5,4},{6,5},{7,6},{8,11},{9,8},{10,9... | collective-permute-start | bytes 49160 | tf_op jit(solution)/shard_map/ppermute | solution.py:307

commit v10 on v8

--- a/solution.py
+++ b/solution.py
@@ -135,16 +135,19 @@
     )
 
 
-def homing_kernel(sizes, probes, turn, select):
+def homing_kernel(sizes, probes, turn, select, bins):
     window, kept, n_tile, n_beam = sizes
     share = kept // n_beam
     me_beam = lax.axis_index("beam")
     me_tile = lax.axis_index("tile")
-    u = iota((share, LANES), 0) + me_beam * share - kept // 2
-    lane = iota((share, LANES), 1)
+    each = share // BIN
+    height = select.shape[0] // BIN
+    u = iota((each, LANES), 0) * BIN + me_beam * share - kept // 2
+    lane = iota((each, LANES), 1)
     v = lane % kept - kept // 2
     shape = (select.shape[0], select.shape[1])
-    window_of, slot_of = iota(shape, 0) // share, iota(shape, 1) // share
+    line = iota(shape, 0)
+    window_of, slot_of = line % height // each, iota(shape, 1) // share
     wanted = (slot_of == -1, slot_of == -1)
     tiles = []
     for j in range(probes.shape[1]):
@@ -158,11 +161,15 @@
         ]
         wanted = [w | ((window_of == j) & (slot_of == spot)) for w, spot in zip(wanted, spots)]
         shift = jnp.right_shift(probes[1, j], 2) - window // 2
-        angle = angle_of(u * offset + v * shift, window)
-        square = angle * angle
-        turn[0, j * share : (j + 1) * share, :] = series(square, 18)
-        turn[1, j * share : (j + 1) * share, :] = series(square, 19) * jnp.where(lane < kept, -angle, angle)
-    same_line = iota(shape, 0) % share == iota(shape, 1) % share
+        for b in range(BIN):
+            angle = angle_of((u + b) * offset + v * shift, window)
+            square = angle * angle
+            place = slice(b * height + j * each, b * height + (j + 1) * each)
+            turn[0, place, :] = series(square, 18)
+            turn[1, place, :] = series(square, 19) * jnp.where(lane < kept, -angle, angle)
+    same_line = line % height % each * BIN + line // height == iota(shape, 1) % share
+    spread = (iota(bins.shape, 0) % kept // BIN == iota(bins.shape, 1)).astype(f32)
+    bins[...] = spread.astype(bf16)
     select[...] = jnp.where((wanted[0] | wanted[1]) & same_line, 1.0, 0.0).astype(bf16)
 
 
@@ -263,22 +270,18 @@
 
 def result_kernel(sizes, all_beams, *refs):
     window, kept, n_tile, n_beam = sizes
-    turn, select = refs[:2]
-    blocks = in_order(refs[2 : 2 + n_tile], orders(n_tile)[1])
-    out, intensity = refs[2 + n_tile :]
+    turn, select, bins = refs[:3]
+    blocks = in_order(refs[3 : 3 + n_tile], orders(n_tile)[1])
+    out = refs[3 + n_tile]
     height = select.shape[0] // BIN
-    shape = (2 * LANES, kept // BIN)
-    bins = (iota(shape, 0) % kept // BIN == iota(shape, 1)).astype(f32).astype(bf16)
     arrived = jnp.concatenate([block[...] for block in blocks], axis=0)
     field = jnp.dot(select[...], arrived, preferred_element_type=f32)
     field = field * turn[0] + times_i(field) * turn[1]
-    intensity[...] = field * field
-    summed = intensity[pl.ds(0, height, stride=BIN), :]
-    for b in range(1, BIN):
-        summed = summed + intensity[pl.ds(b, height, stride=BIN), :]
+    intensity = field * field
+    summed = sum([intensity[b * height : (b + 1) * height] for b in range(1, BIN)], intensity[:height])
     high = summed.astype(bf16)
     low = (summed - high.astype(f32)).astype(bf16)
-    binned = jnp.dot(jnp.concatenate([high, low], axis=1), bins, preferred_element_type=f32)
+    binned = jnp.dot(jnp.concatenate([high, low], axis=1), bins[...], preferred_element_type=f32)
     binned = binned * (1.0 / (BIN * BIN * window * window * all_beams))
     each = height // out.shape[0]
     for j in range(out.shape[0]):
@@ -330,13 +333,14 @@
     lists = lax.optimization_barrier(shifted([probes] * n_tile, 1, lists_order))
     lists = dict(zip(lists_order, lists))
 
-    turn, select = pl.pallas_call(
+    turn, select, bins = pl.pallas_call(
         functools.partial(homing_kernel, sizes),
         in_specs=[SMEM],
-        out_specs=[VMEM] * 2,
+        out_specs=[VMEM] * 3,
         out_shape=[
             jax.ShapeDtypeStruct((2, count * share, LANES), f32),
             jax.ShapeDtypeStruct((count * share, slots * share), bf16),
+            jax.ShapeDtypeStruct((2 * LANES, kept // BIN), bf16),
         ],
         compiler_params=params(),
         cost_estimate=pl.CostEstimate(flops=1 << 28, bytes_accessed=1 << 20, transcendentals=0),
@@ -417,13 +421,12 @@
 
     return pl.pallas_call(
         functools.partial(result_kernel, sizes, beams * n_beam),
-        in_specs=[VMEM] * (2 + n_tile),
+        in_specs=[VMEM] * (3 + n_tile),
         out_specs=VMEM,
         out_shape=jax.ShapeDtypeStruct((count, share // BIN, kept // BIN), f32),
-        scratch_shapes=[pltpu.VMEM((count * share, LANES), f32)],
         compiler_params=params(),
         name="result",
-    )(turn, select, *blocks)
+    )(turn, select, bins, *blocks)
 
 
 def solution(mesh):

time: 23.6 us -> 23.6 us (level)
  no operation moved by 1% of the time
where the time goes in v10:
time: 23.6 us; the launch traced here: 23.5 us
  starting transfers between devices  13.9 us (59%)
  Pallas kernels  6.69 us (28%)
  waiting for transfers between devices  2.62 us (11%)
    ppermute x6, starting transfers between devices, shifted(): lax.ppermute(arrays[k], 'tile', [(i, (i + way * k) % size) for i in range...  10.7 us
    pallas_call x1, Pallas kernels, per_device(): pl.pallas_call(functools.partial(spectra_kernel, sizes), in_specs=[HBM, H...  3.35 us
    ppermute x4, starting transfers between devices, swapped(): lax.ppermute(array, axis, [(i, i ^ by) for i in range(lax.axis_size(axis))])  3.22 us
    pallas_call x2, Pallas kernels, parts_call(): pl.pallas_call(functools.partial(kernel, sizes), in_specs=[VMEM] * len(op...  1.58 us
    ppermute x4, waiting for transfers between devices, swapped(): lax.ppermute(array, axis, [(i, i ^ by) for i in range(lax.axis_size(axis))])  1.36 us
    ppermute x6, waiting for transfers between devices, shifted(): lax.ppermute(arrays[k], 'tile', [(i, (i + way * k) % size) for i in range...  1.26 us
    pallas_call x1, Pallas kernels, per_device(): pl.pallas_call(functools.partial(result_kernel, sizes, beams * n_beam), i...  0.98 us
    pallas_call x1, Pallas kernels, per_device(): pl.pallas_call(functools.partial(homing_kernel, sizes), in_specs=[SMEM],...  0.79 us
  transfers between devices with their start and end apart: 10, of which 5 were waited for; matrix products, arithmetic and copies ran while one was open for 0% of the time, Pallas kernels for 21%

profile of v10, /device:TPU:0, one launch (start us, length us, event | category | flops | bytes accessed | tf_op | source)
XLA Modules:
  0.0 23.5 jit_solution(1241169372405176565)
XLA Ops:
  0.0 0.0 copy-start
  0.0 3.0 %collective-permute-start = (s32[2,8]{1,0:T(2,128)}, s32[2,8]{1,0:T(2,128)S(1)}, u32[]{:S(2)}, u32[]{:S(2)}) collective-permute-start(s32[2,8]{1,0:T(2,128)} %bitcast.9), channel_id=1, source_target_pairs={{0,1},{1,2},{2,3},{3,0},{4,5},{5,6},{6,7},{7,4},{8,9},{9,10},{10,1... | collective-permute-start | bytes 200 | tf_op jit(solution)/shard_map/ppermute | solution.py:307
  3.0 2.1 %collective-permute-start.1 = (s32[2,8]{1,0:T(2,128)}, s32[2,8]{1,0:T(2,128)S(1)}, u32[]{:S(2)}, u32[]{:S(2)}) collective-permute-start(s32[2,8]{1,0:T(2,128)} %bitcast.10), channel_id=1, source_target_pairs={{0,3},{1,0},{2,1},{3,2},{4,7},{5,4},{6,5},{7,6},{8,11},{9,8},{10,9... | collective-permute-start | bytes 200 | tf_op jit(solution)/shard_map/ppermute | solution.py:307
  5.1 1.0 %collective-permute-start.2 = (s32[2,8]{1,0:T(2,128)}, s32[2,8]{1,0:T(2,128)S(1)}, u32[]{:S(2)}, u32[]{:S(2)}) collective-permute-start(s32[2,8]{1,0:T(2,128)} %bitcast.11), channel_id=1, source_target_pairs={{0,2},{1,3},{2,0},{3,1},{4,6},{5,7},{6,4},{7,5},{8,10},{9,11},{10,... | collective-permute-start | bytes 200 | tf_op jit(solution)/shard_map/ppermute | solution.py:307
  6.1 3.3 %spectra.1 = (bf16[16,512,128]{2,1,0:T(8,128)(2,1)S(1)}, bf16[128,256]{1,0:T(8,128)(2,1)S(1)}, f32[3,512]{1,0:T(4,128)S(1)}) custom-call(bf16[2,64,128,128]{3,2,1,0:T(8,128)(2,1)} %smatrix_hbm.1, f32[3,64]{1,0:T(4,128)} %table_hbm.1), custom_call_target="tpu_custom_call" | custom-call | flops 536870912 | bytes 6291456 | tf_op jit(solution)/shard_map/spectra/pallas_call | solution.py:349
  9.4 0.0 collective-permute-done.refs_2_
  9.4 0.0 collective-permute-done.1.refs_0_
  9.4 0.3 %collective-permute-done.2.refs_1_ = s32[2,8]{1,0:T(2,128)S(1)} collective-permute-done((s32[2,8]{1,0:T(2,128)}, s32[2,8]{1,0:T(2,128)S(1)}, u32[]{:S(2)}, u32[]{:S(2)}) %collective-permute-start.2) | collective-permute-done | bytes 96 | tf_op jit(solution)/shard_map/ppermute | solution.py:307
  9.8 0.0 copy-done
  9.8 0.8 %coefficients.1 = (bf16[2,2,64,128]{3,2,1,0:T(8,128)(2,1)S(1)}, bf16[2,2,64,128]{3,2,1,0:T(8,128)(2,1)S(1)}, bf16[1,2,4,16,512]{4,3,2,1,0:T(8,128)(2,1)S(1)}, s32[8,128]{1,0:T(8,128)S(1)}) custom-call(s32[2,8]{1,0:T(2,128)S(1)} %collective-permute-done.1.refs_0_, s32[2,8]{1,0:T(2,128)S(1)} %collective-permute-done.2.refs_1_, ...), custom_call_target="tpu_custom_call" | custom-call | flops 268435456 | bytes 4194304 | tf_op jit(solution)/shard_map/coefficients/pallas_call | solution.py:378
  10.6 0.1 collective-permute-start.6
  10.7 0.7 %parts.1 = (bf16[2,2,64,128]{3,2,1,0:T(8,128)(2,1)S(1)}, bf16[2,2,64,128]{3,2,1,0:T(8,128)(2,1)S(1)}) custom-call(bf16[1,2,4,16,512]{4,3,2,1,0:T(8,128)(2,1)S(1)} %get-tuple-element.31.coeff, s32[8,128]{1,0:T(8,128)S(1)} %get-tuple-element.32.offsets, bf16[128,256]{1,0:T(8,128)(2,1)S(1)} %get-tuple-element.29.refs_5_.row_table, ...), custom_call_target="tpu_custom_call" | custom-call | flops 268435456 | bytes 4194304 | tf_op jit(solution)/shard_map/parts/pallas_call | solution.py:378
  11.5 0.6 %collective-permute-start.3 = (bf16[2,2,64,128]{3,2,1,0:T(8,128)(2,1)S(1)}, bf16[2,2,64,128]{3,2,1,0:T(8,128)(2,1)S(1)}, u32[]{:S(2)}, u32[]{:S(2)}) collective-permute-start(bf16[2,2,64,128]{3,2,1,0:T(8,128)(2,1)S(1)} %get-tuple-element.34), channel_id=1, source_target_pairs={{0,4},{4,0},{8,12},{12,8},{1,5},{5,1},{9,13},{13,9},{2,6},{6,2},{1... | collective-permute-start | bytes 196616 | tf_op jit(solution)/shard_map/ppermute | solution.py:301
  12.0 0.0 collective-permute-done.6
  12.1 1.7 %collective-permute-start.7 = (bf16[1,2,64,128]{3,2,1,0:T(8,128)(2,1)S(1)}, bf16[1,2,64,128]{3,2,1,0:T(8,128)(2,1)S(1)}, u32[]{:S(2)}, u32[]{:S(2)}) collective-permute-start(bf16[1,2,64,128]{3,2,1,0:T(8,128)(2,1)S(1)} %slice.37), channel_id=1, source_target_pairs={{0,8},{4,12},{8,0},{12,4},{1,9},{5,13},{9,1},{13,5},{2,10},{6,14},... | collective-permute-start | bytes 98312 | tf_op jit(solution)/shard_map/ppermute | solution.py:301
  13.8 0.0 collective-permute-done.3
  13.8 0.9 %collective-permute-start.4 = (bf16[1,2,64,128]{3,2,1,0:T(8,128)(2,1)S(1)}, bf16[1,2,64,128]{3,2,1,0:T(8,128)(2,1)S(1)}, u32[]{:S(2)}, u32[]{:S(2)}) collective-permute-start(bf16[1,2,64,128]{3,2,1,0:T(8,128)(2,1)S(1)} %slice.33), channel_id=1, source_target_pairs={{0,8},{4,12},{8,0},{12,4},{1,9},{5,13},{9,1},{13,5},{2,10},{6,14},... | collective-permute-start | bytes 98312 | tf_op jit(solution)/shard_map/ppermute | solution.py:301
  14.7 1.4 %collective-permute-done.7 = bf16[1,2,64,128]{3,2,1,0:T(8,128)(2,1)S(1)} collective-permute-done((bf16[1,2,64,128]{3,2,1,0:T(8,128)(2,1)S(1)}, bf16[1,2,64,128]{3,2,1,0:T(8,128)(2,1)S(1)}, u32[]{:S(2)}, u32[]{:S(2)}) %collective-permute-start.7) | collective-permute-done | bytes 32800 | tf_op jit(solution)/shard_map/ppermute | solution.py:301
  16.1 1.3 %collective-permute-start.8 = (bf16[64,128]{1,0:T(8,128)(2,1)S(1)}, bf16[64,128]{1,0:T(8,128)(2,1)S(1)}, u32[]{:S(2)}, u32[]{:S(2)}) collective-permute-start(bf16[64,128]{1,0:T(8,128)(2,1)S(1)} %get-tuple-element.38), channel_id=1, source_target_pairs={{0,1},{1,2},{2,3},{3,0},{4,5},{5,6},{6,7},{7,4},{8,9},{9,10},{10,1... | collective-permute-start | bytes 49160 | tf_op jit(solution)/shard_map/ppermute | solution.py:307
  17.4 1.3 %collective-permute-start.9 = (bf16[64,128]{1,0:T(8,128)(2,1)S(1)}, bf16[64,128]{1,0:T(8,128)(2,1)S(1)}, u32[]{:S(2)}, u32[]{:S(2)}) collective-permute-start(bf16[64,128]{1,0:T(8,128)(2,1)S(1)} %get-tuple-element.37), channel_id=1, source_target_pairs={{0,2},{1,3},{2,0},{3,1},{4,6},{5,7},{6,4},{7,5},{8,10},{9,11},{10,... | collective-permute-start | bytes 49160 | tf_op jit(solution)/shard_map/ppermute | solution.py:307
  18.7 0.0 collective-permute-done.4
  18.7 2.1 %collective-permute-start.5 = (bf16[64,128]{1,0:T(8,128)(2,1)S(1)}, bf16[64,128]{1,0:T(8,128)(2,1)S(1)}, u32[]{:S(2)}, u32[]{:S(2)}) collective-permute-start(bf16[64,128]{1,0:T(8,128)(2,1)S(1)} %get-tuple-element.39), channel_id=1, source_target_pairs={{0,3},{1,0},{2,1},{3,2},{4,7},{5,4},{6,5},{7,6},{8,11},{9,8},{10,9... | collective-permute-start | bytes 49160 | tf_op jit(solution)/shard_map/ppermute | solution.py:307
  20.8 0.8 %homing.1 = (f32[2,128,128]{2,1,0:T(8,128)S(1)}, bf16[128,256]{1,0:T(8,128)(2,1)S(1)}, bf16[256,32]{1,0:T(8,128)(2,1)S(1)}) custom-call(s32[2,8]{1,0:T(2,128)S(1)} %bitcast.13), custom_call_target="tpu_custom_call" | custom-call | flops 268435456 | bytes 1048576 | tf_op jit(solution)/shard_map/homing/pallas_call | solution.py:336
  21.6 0.1 collective-permute-done.8.refs_5_
  21.7 0.4 %collective-permute-done.9.refs_6_ = bf16[64,128]{1,0:T(8,128)(2,1)S(1)} collective-permute-done((bf16[64,128]{1,0:T(8,128)(2,1)S(1)}, bf16[64,128]{1,0:T(8,128)(2,1)S(1)}, u32[]{:S(2)}, u32[]{:S(2)}) %collective-permute-start.9) | collective-permute-done | bytes 16416 | tf_op jit(solution)/shard_map/ppermute | solution.py:307
  22.0 0.5 %collective-permute-done.5.refs_4_ = bf16[64,128]{1,0:T(8,128)(2,1)S(1)} collective-permute-done((bf16[64,128]{1,0:T(8,128)(2,1)S(1)}, bf16[64,128]{1,0:T(8,128)(2,1)S(1)}, u32[]{:S(2)}, u32[]{:S(2)}) %collective-permute-start.5) | collective-permute-done | bytes 16416 | tf_op jit(solution)/shard_map/ppermute | solution.py:307
  22.5 1.0 %result.1 = f32[8,8,32]{2,1,0:T(8,128)} custom-call(f32[2,128,128]{2,1,0:T(8,128)S(1)} %get-tuple-element.21.refs_0_, bf16[128,256]{1,0:T(8,128)(2,1)S(1)} %get-tuple-element.22.refs_1_, bf16[256,32]{1,0:T(8,128)(2,1)S(1)} %get-tuple-element.23.refs_2_, bf16[64,128]{1,0:T(8,128)(2,1)S(1)} %get-tuple-element.40.refs_3_, ...), custom_call_target="tpu_custom_call" | custom-call | tf_op jit(solution)/shard_map/result/pallas_call | solution.py:422
  (8 shorter events, 0.1 us)
Async XLA Ops:
  0.0 9.8 %copy-start = (s32[8,2]{0,1:T(2,128)S(1)}, s32[8,2]{0,1:T(2,128)}, u32[]{:S(2)}) copy-start(s32[8,2]{0,1:T(2,128)} %param.5) | copy-start | bytes 196
  0.0 9.4 %collective-permute-start = (s32[2,8]{1,0:T(2,128)}, s32[2,8]{1,0:T(2,128)S(1)}, u32[]{:S(2)}, u32[]{:S(2)}) collective-permute-start(s32[2,8]{1,0:T(2,128)} %bitcast.9), channel_id=1, source_target_pairs={{0,1},{1,2},{2,3},{3,0},{4,5},{5,6},{6,7},{7,4},{8,9},{9,10},{10,1... | collective-permute-start | bytes 200 | tf_op jit(solution)/shard_map/ppermute | solution.py:307
  3.0 6.4 %collective-permute-start.1 = (s32[2,8]{1,0:T(2,128)}, s32[2,8]{1,0:T(2,128)S(1)}, u32[]{:S(2)}, u32[]{:S(2)}) collective-permute-start(s32[2,8]{1,0:T(2,128)} %bitcast.10), channel_id=1, source_target_pairs={{0,3},{1,0},{2,1},{3,2},{4,7},{5,4},{6,5},{7,6},{8,11},{9,8},{10,9... | collective-permute-start | bytes 200 | tf_op jit(solution)/shard_map/ppermute | solution.py:307
  5.1 4.7 %collective-permute-start.2 = (s32[2,8]{1,0:T(2,128)}, s32[2,8]{1,0:T(2,128)S(1)}, u32[]{:S(2)}, u32[]{:S(2)}) collective-permute-start(s32[2,8]{1,0:T(2,128)} %bitcast.11), channel_id=1, source_target_pairs={{0,2},{1,3},{2,0},{3,1},{4,6},{5,7},{6,4},{7,5},{8,10},{9,11},{10,... | collective-permute-start | bytes 200 | tf_op jit(solution)/shard_map/ppermute | solution.py:307
  10.6 1.4 %collective-permute-start.6 = (bf16[2,2,64,128]{3,2,1,0:T(8,128)(2,1)S(1)}, bf16[2,2,64,128]{3,2,1,0:T(8,128)(2,1)S(1)}, u32[]{:S(2)}, u32[]{:S(2)}) collective-permute-start(bf16[2,2,64,128]{3,2,1,0:T(8,128)(2,1)S(1)} %get-tuple-element.36), channel_id=1, source_target_pairs={{0,4},{4,0},{8,12},{12,8},{1,5},{5,1},{9,13},{13,9},{2,6},{6,2},{1... | collective-permute-start | bytes 196616 | tf_op jit(solution)/shard_map/ppermute | solution.py:301
  11.5 2.3 %collective-permute-start.3 = (bf16[2,2,64,128]{3,2,1,0:T(8,128)(2,1)S(1)}, bf16[2,2,64,128]{3,2,1,0:T(8,128)(2,1)S(1)}, u32[]{:S(2)}, u32[]{:S(2)}) collective-permute-start(bf16[2,2,64,128]{3,2,1,0:T(8,128)(2,1)S(1)} %get-tuple-element.34), channel_id=1, source_target_pairs={{0,4},{4,0},{8,12},{12,8},{1,5},{5,1},{9,13},{13,9},{2,6},{6,2},{1... | collective-permute-start | bytes 196616 | tf_op jit(solution)/shard_map/ppermute | solution.py:301
  12.1 4.0 %collective-permute-start.7 = (bf16[1,2,64,128]{3,2,1,0:T(8,128)(2,1)S(1)}, bf16[1,2,64,128]{3,2,1,0:T(8,128)(2,1)S(1)}, u32[]{:S(2)}, u32[]{:S(2)}) collective-permute-start(bf16[1,2,64,128]{3,2,1,0:T(8,128)(2,1)S(1)} %slice.37), channel_id=1, source_target_pairs={{0,8},{4,12},{8,0},{12,4},{1,9},{5,13},{9,1},{13,5},{2,10},{6,14},... | collective-permute-start | bytes 98312 | tf_op jit(solution)/shard_map/ppermute | solution.py:301
  13.8 4.8 %collective-permute-start.4 = (bf16[1,2,64,128]{3,2,1,0:T(8,128)(2,1)S(1)}, bf16[1,2,64,128]{3,2,1,0:T(8,128)(2,1)S(1)}, u32[]{:S(2)}, u32[]{:S(2)}) collective-permute-start(bf16[1,2,64,128]{3,2,1,0:T(8,128)(2,1)S(1)} %slice.33), channel_id=1, source_target_pairs={{0,8},{4,12},{8,0},{12,4},{1,9},{5,13},{9,1},{13,5},{2,10},{6,14},... | collective-permute-start | bytes 98312 | tf_op jit(solution)/shard_map/ppermute | solution.py:301
  16.1 5.6 %collective-permute-start.8 = (bf16[64,128]{1,0:T(8,128)(2,1)S(1)}, bf16[64,128]{1,0:T(8,128)(2,1)S(1)}, u32[]{:S(2)}, u32[]{:S(2)}) collective-permute-start(bf16[64,128]{1,0:T(8,128)(2,1)S(1)} %get-tuple-element.38), channel_id=1, source_target_pairs={{0,1},{1,2},{2,3},{3,0},{4,5},{5,6},{6,7},{7,4},{8,9},{9,10},{10,1... | collective-permute-start | bytes 49160 | tf_op jit(solution)/shard_map/ppermute | solution.py:307
  17.4 4.6 %collective-permute-start.9 = (bf16[64,128]{1,0:T(8,128)(2,1)S(1)}, bf16[64,128]{1,0:T(8,128)(2,1)S(1)}, u32[]{:S(2)}, u32[]{:S(2)}) collective-permute-start(bf16[64,128]{1,0:T(8,128)(2,1)S(1)} %get-tuple-element.37), channel_id=1, source_target_pairs={{0,2},{1,3},{2,0},{3,1},{4,6},{5,7},{6,4},{7,5},{8,10},{9,11},{10,... | collective-permute-start | bytes 49160 | tf_op jit(solution)/shard_map/ppermute | solution.py:307
  18.7 3.8 %collective-permute-start.5 = (bf16[64,128]{1,0:T(8,128)(2,1)S(1)}, bf16[64,128]{1,0:T(8,128)(2,1)S(1)}, u32[]{:S(2)}, u32[]{:S(2)}) collective-permute-start(bf16[64,128]{1,0:T(8,128)(2,1)S(1)} %get-tuple-element.39), channel_id=1, source_target_pairs={{0,3},{1,0},{2,1},{3,2},{4,7},{5,4},{6,5},{7,6},{8,11},{9,8},{10,9... | collective-permute-start | bytes 49160 | tf_op jit(solution)/shard_map/ppermute | solution.py:307

commit v11 on v8

--- a/solution.py
+++ b/solution.py
@@ -14,7 +14,7 @@
 PER_LIST = 2 * CAP
 LANES = 128
 GROUP = 8
-CHUNKS = 2
+CHUNKS = 4
 ROWS = 8
 
 LISTS_ORDER = (0, 1, 3, 2)

time: 23.6 us -> 23.6 us (level)
  transfers between devices with their start and end apart: 10 -> 10, of which waited for: 5 -> 5; matrix products, arithmetic and copies ran while one was open for 0% -> 0% of each run, Pallas kernels for 21% -> 20%
where the time goes in v11:
time: 23.6 us; the launch traced here: 23.5 us
  starting transfers between devices  13.9 us (59%)
  Pallas kernels  6.59 us (28%)
  waiting for transfers between devices  2.74 us (12%)
    ppermute x6, starting transfers between devices, shifted(): lax.ppermute(arrays[k], 'tile', [(i, (i + way * k) % size) for i in range...  10.7 us
    pallas_call x1, Pallas kernels, per_device(): pl.pallas_call(functools.partial(spectra_kernel, sizes), in_specs=[HBM, H...  3.3 us
    ppermute x4, starting transfers between devices, swapped(): lax.ppermute(array, axis, [(i, i ^ by) for i in range(lax.axis_size(axis))])  3.22 us
    pallas_call x2, Pallas kernels, parts_call(): pl.pallas_call(functools.partial(kernel, sizes), in_specs=[VMEM] * len(op...  1.58 us
    ppermute x6, waiting for transfers between devices, shifted(): lax.ppermute(arrays[k], 'tile', [(i, (i + way * k) % size) for i in range...  1.38 us
    ppermute x4, waiting for transfers between devices, swapped(): lax.ppermute(array, axis, [(i, i ^ by) for i in range(lax.axis_size(axis))])  1.36 us
    pallas_call x1, Pallas kernels, per_device(): pl.pallas_call(functools.partial(result_kernel, sizes, beams * n_beam), i...  0.99 us
    pallas_call x1, Pallas kernels, per_device(): pl.pallas_call(functools.partial(homing_kernel, sizes), in_specs=[SMEM],...  0.73 us
  transfers between devices with their start and end apart: 10, of which 5 were waited for; matrix products, arithmetic and copies ran while one was open for 0% of the time, Pallas kernels for 20%

profile of v11, /device:TPU:0, one launch (start us, length us, event | category | flops | bytes accessed | tf_op | source)
XLA Modules:
  0.0 23.5 jit_solution(7331667559407449001)
XLA Ops:
  0.0 0.0 copy-start
  0.0 3.0 %collective-permute-start = (s32[2,8]{1,0:T(2,128)}, s32[2,8]{1,0:T(2,128)S(1)}, u32[]{:S(2)}, u32[]{:S(2)}) collective-permute-start(s32[2,8]{1,0:T(2,128)} %bitcast.9), channel_id=1, source_target_pairs={{0,1},{1,2},{2,3},{3,0},{4,5},{5,6},{6,7},{7,4},{8,9},{9,10},{10,1... | collective-permute-start | bytes 200 | tf_op jit(solution)/shard_map/ppermute | solution.py:304
  3.0 2.1 %collective-permute-start.1 = (s32[2,8]{1,0:T(2,128)}, s32[2,8]{1,0:T(2,128)S(1)}, u32[]{:S(2)}, u32[]{:S(2)}) collective-permute-start(s32[2,8]{1,0:T(2,128)} %bitcast.10), channel_id=1, source_target_pairs={{0,3},{1,0},{2,1},{3,2},{4,7},{5,4},{6,5},{7,6},{8,11},{9,8},{10,9... | collective-permute-start | bytes 200 | tf_op jit(solution)/shard_map/ppermute | solution.py:304
  5.1 1.0 %collective-permute-start.2 = (s32[2,8]{1,0:T(2,128)}, s32[2,8]{1,0:T(2,128)S(1)}, u32[]{:S(2)}, u32[]{:S(2)}) collective-permute-start(s32[2,8]{1,0:T(2,128)} %bitcast.11), channel_id=1, source_target_pairs={{0,2},{1,3},{2,0},{3,1},{4,6},{5,7},{6,4},{7,5},{8,10},{9,11},{10,... | collective-permute-start | bytes 200 | tf_op jit(solution)/shard_map/ppermute | solution.py:304
  6.1 3.3 %spectra.1 = (bf16[16,512,128]{2,1,0:T(8,128)(2,1)S(1)}, bf16[128,256]{1,0:T(8,128)(2,1)S(1)}, f32[3,512]{1,0:T(4,128)S(1)}) custom-call(bf16[2,64,128,128]{3,2,1,0:T(8,128)(2,1)} %smatrix_hbm.1, f32[3,64]{1,0:T(4,128)} %table_hbm.1), custom_call_target="tpu_custom_call" | custom-call | flops 536870912 | bytes 6291456 | tf_op jit(solution)/shard_map/spectra/pallas_call | solution.py:345
  9.4 0.0 collective-permute-done.refs_2_
  9.4 0.0 collective-permute-done.1.refs_0_
  9.4 0.4 %collective-permute-done.2.refs_1_ = s32[2,8]{1,0:T(2,128)S(1)} collective-permute-done((s32[2,8]{1,0:T(2,128)}, s32[2,8]{1,0:T(2,128)S(1)}, u32[]{:S(2)}, u32[]{:S(2)}) %collective-permute-start.2) | collective-permute-done | bytes 96 | tf_op jit(solution)/shard_map/ppermute | solution.py:304
  9.8 0.0 copy-done
  9.8 0.8 %coefficients.1 = (bf16[2,2,64,128]{3,2,1,0:T(8,128)(2,1)S(1)}, bf16[2,2,64,128]{3,2,1,0:T(8,128)(2,1)S(1)}, bf16[1,2,4,16,512]{4,3,2,1,0:T(8,128)(2,1)S(1)}, s32[8,128]{1,0:T(8,128)S(1)}) custom-call(s32[2,8]{1,0:T(2,128)S(1)} %collective-permute-done.1.refs_0_, s32[2,8]{1,0:T(2,128)S(1)} %collective-permute-done.2.refs_1_, ...), custom_call_target="tpu_custom_call" | custom-call | flops 268435456 | bytes 4194304 | tf_op jit(solution)/shard_map/coefficients/pallas_call | solution.py:374
  10.6 0.1 collective-permute-start.6
  10.7 0.7 %parts.1 = (bf16[2,2,64,128]{3,2,1,0:T(8,128)(2,1)S(1)}, bf16[2,2,64,128]{3,2,1,0:T(8,128)(2,1)S(1)}) custom-call(bf16[1,2,4,16,512]{4,3,2,1,0:T(8,128)(2,1)S(1)} %get-tuple-element.29.coeff, s32[8,128]{1,0:T(8,128)S(1)} %get-tuple-element.30.offsets, bf16[128,256]{1,0:T(8,128)(2,1)S(1)} %get-tuple-element.27.refs_5_.row_table, ...), custom_call_target="tpu_custom_call" | custom-call | flops 268435456 | bytes 4194304 | tf_op jit(solution)/shard_map/parts/pallas_call | solution.py:374
  11.5 0.6 %collective-permute-start.3 = (bf16[2,2,64,128]{3,2,1,0:T(8,128)(2,1)S(1)}, bf16[2,2,64,128]{3,2,1,0:T(8,128)(2,1)S(1)}, u32[]{:S(2)}, u32[]{:S(2)}) collective-permute-start(bf16[2,2,64,128]{3,2,1,0:T(8,128)(2,1)S(1)} %get-tuple-element.32), channel_id=1, source_target_pairs={{0,4},{4,0},{8,12},{12,8},{1,5},{5,1},{9,13},{13,9},{2,6},{6,2},{1... | collective-permute-start | bytes 196616 | tf_op jit(solution)/shard_map/ppermute | solution.py:298
  12.0 0.0 collective-permute-done.6
  12.1 1.7 %collective-permute-start.7 = (bf16[1,2,64,128]{3,2,1,0:T(8,128)(2,1)S(1)}, bf16[1,2,64,128]{3,2,1,0:T(8,128)(2,1)S(1)}, u32[]{:S(2)}, u32[]{:S(2)}) collective-permute-start(bf16[1,2,64,128]{3,2,1,0:T(8,128)(2,1)S(1)} %slice.37), channel_id=1, source_target_pairs={{0,8},{4,12},{8,0},{12,4},{1,9},{5,13},{9,1},{13,5},{2,10},{6,14},... | collective-permute-start | bytes 98312 | tf_op jit(solution)/shard_map/ppermute | solution.py:298
  13.8 0.0 collective-permute-done.3
  13.8 0.9 %collective-permute-start.4 = (bf16[1,2,64,128]{3,2,1,0:T(8,128)(2,1)S(1)}, bf16[1,2,64,128]{3,2,1,0:T(8,128)(2,1)S(1)}, u32[]{:S(2)}, u32[]{:S(2)}) collective-permute-start(bf16[1,2,64,128]{3,2,1,0:T(8,128)(2,1)S(1)} %slice.33), channel_id=1, source_target_pairs={{0,8},{4,12},{8,0},{12,4},{1,9},{5,13},{9,1},{13,5},{2,10},{6,14},... | collective-permute-start | bytes 98312 | tf_op jit(solution)/shard_map/ppermute | solution.py:298
  14.7 1.3 %collective-permute-done.7 = bf16[1,2,64,128]{3,2,1,0:T(8,128)(2,1)S(1)} collective-permute-done((bf16[1,2,64,128]{3,2,1,0:T(8,128)(2,1)S(1)}, bf16[1,2,64,128]{3,2,1,0:T(8,128)(2,1)S(1)}, u32[]{:S(2)}, u32[]{:S(2)}) %collective-permute-start.7) | collective-permute-done | bytes 32800 | tf_op jit(solution)/shard_map/ppermute | solution.py:298
  16.1 1.3 %collective-permute-start.8 = (bf16[64,128]{1,0:T(8,128)(2,1)S(1)}, bf16[64,128]{1,0:T(8,128)(2,1)S(1)}, u32[]{:S(2)}, u32[]{:S(2)}) collective-permute-start(bf16[64,128]{1,0:T(8,128)(2,1)S(1)} %get-tuple-element.36), channel_id=1, source_target_pairs={{0,1},{1,2},{2,3},{3,0},{4,5},{5,6},{6,7},{7,4},{8,9},{9,10},{10,1... | collective-permute-start | bytes 49160 | tf_op jit(solution)/shard_map/ppermute | solution.py:304
  17.4 1.3 %collective-permute-start.9 = (bf16[64,128]{1,0:T(8,128)(2,1)S(1)}, bf16[64,128]{1,0:T(8,128)(2,1)S(1)}, u32[]{:S(2)}, u32[]{:S(2)}) collective-permute-start(bf16[64,128]{1,0:T(8,128)(2,1)S(1)} %get-tuple-element.35), channel_id=1, source_target_pairs={{0,2},{1,3},{2,0},{3,1},{4,6},{5,7},{6,4},{7,5},{8,10},{9,11},{10,... | collective-permute-start | bytes 49160 | tf_op jit(solution)/shard_map/ppermute | solution.py:304
  18.7 0.0 collective-permute-done.4
  18.7 2.1 %collective-permute-start.5 = (bf16[64,128]{1,0:T(8,128)(2,1)S(1)}, bf16[64,128]{1,0:T(8,128)(2,1)S(1)}, u32[]{:S(2)}, u32[]{:S(2)}) collective-permute-start(bf16[64,128]{1,0:T(8,128)(2,1)S(1)} %get-tuple-element.37), channel_id=1, source_target_pairs={{0,3},{1,0},{2,1},{3,2},{4,7},{5,4},{6,5},{7,6},{8,11},{9,8},{10,9... | collective-permute-start | bytes 49160 | tf_op jit(solution)/shard_map/ppermute | solution.py:304
  20.8 0.7 %homing.1 = (f32[2,128,128]{2,1,0:T(8,128)S(1)}, bf16[128,256]{1,0:T(8,128)(2,1)S(1)}) custom-call(s32[2,8]{1,0:T(2,128)S(1)} %bitcast.13), custom_call_target="tpu_custom_call" | custom-call | flops 268435456 | bytes 1048576 | tf_op jit(solution)/shard_map/homing/pallas_call | solution.py:333
  21.5 0.2 collective-permute-done.8.refs_4_
  21.7 0.4 %collective-permute-done.9.refs_5_ = bf16[64,128]{1,0:T(8,128)(2,1)S(1)} collective-permute-done((bf16[64,128]{1,0:T(8,128)(2,1)S(1)}, bf16[64,128]{1,0:T(8,128)(2,1)S(1)}, u32[]{:S(2)}, u32[]{:S(2)}) %collective-permute-start.9) | collective-permute-done | bytes 16416 | tf_op jit(solution)/shard_map/ppermute | solution.py:304
  22.0 0.5 %collective-permute-done.5.refs_3_ = bf16[64,128]{1,0:T(8,128)(2,1)S(1)} collective-permute-done((bf16[64,128]{1,0:T(8,128)(2,1)S(1)}, bf16[64,128]{1,0:T(8,128)(2,1)S(1)}, u32[]{:S(2)}, u32[]{:S(2)}) %collective-permute-start.5) | collective-permute-done | bytes 16416 | tf_op jit(solution)/shard_map/ppermute | solution.py:304
  22.5 1.0 %result.1 = f32[8,8,32]{2,1,0:T(8,128)} custom-call(f32[2,128,128]{2,1,0:T(8,128)S(1)} %get-tuple-element.20.refs_0_, bf16[128,256]{1,0:T(8,128)(2,1)S(1)} %get-tuple-element.21.refs_1_, bf16[64,128]{1,0:T(8,128)(2,1)S(1)} %get-tuple-element.38.refs_2_, bf16[64,128]{1,0:T(8,128)(2,1)S(1)} %collective-permute-done.5.refs_3_, ...), custom_call_target="tpu_custom_call" | custom-call | tf_op jit(solution)/shard_map/result/pallas_call | solution.py:418
  (8 shorter events, 0.1 us)
Async XLA Ops:
  0.0 9.8 %copy-start = (s32[8,2]{0,1:T(2,128)S(1)}, s32[8,2]{0,1:T(2,128)}, u32[]{:S(2)}) copy-start(s32[8,2]{0,1:T(2,128)} %param.5) | copy-start | bytes 196
  0.0 9.4 %collective-permute-start = (s32[2,8]{1,0:T(2,128)}, s32[2,8]{1,0:T(2,128)S(1)}, u32[]{:S(2)}, u32[]{:S(2)}) collective-permute-start(s32[2,8]{1,0:T(2,128)} %bitcast.9), channel_id=1, source_target_pairs={{0,1},{1,2},{2,3},{3,0},{4,5},{5,6},{6,7},{7,4},{8,9},{9,10},{10,1... | collective-permute-start | bytes 200 | tf_op jit(solution)/shard_map/ppermute | solution.py:304
  3.0 6.4 %collective-permute-start.1 = (s32[2,8]{1,0:T(2,128)}, s32[2,8]{1,0:T(2,128)S(1)}, u32[]{:S(2)}, u32[]{:S(2)}) collective-permute-start(s32[2,8]{1,0:T(2,128)} %bitcast.10), channel_id=1, source_target_pairs={{0,3},{1,0},{2,1},{3,2},{4,7},{5,4},{6,5},{7,6},{8,11},{9,8},{10,9... | collective-permute-start | bytes 200 | tf_op jit(solution)/shard_map/ppermute | solution.py:304
  5.1 4.7 %collective-permute-start.2 = (s32[2,8]{1,0:T(2,128)}, s32[2,8]{1,0:T(2,128)S(1)}, u32[]{:S(2)}, u32[]{:S(2)}) collective-permute-start(s32[2,8]{1,0:T(2,128)} %bitcast.11), channel_id=1, source_target_pairs={{0,2},{1,3},{2,0},{3,1},{4,6},{5,7},{6,4},{7,5},{8,10},{9,11},{10,... | collective-permute-start | bytes 200 | tf_op jit(solution)/shard_map/ppermute | solution.py:304
  10.6 1.4 %collective-permute-start.6 = (bf16[2,2,64,128]{3,2,1,0:T(8,128)(2,1)S(1)}, bf16[2,2,64,128]{3,2,1,0:T(8,128)(2,1)S(1)}, u32[]{:S(2)}, u32[]{:S(2)}) collective-permute-start(bf16[2,2,64,128]{3,2,1,0:T(8,128)(2,1)S(1)} %get-tuple-element.34), channel_id=1, source_target_pairs={{0,4},{4,0},{8,12},{12,8},{1,5},{5,1},{9,13},{13,9},{2,6},{6,2},{1... | collective-permute-start | bytes 196616 | tf_op jit(solution)/shard_map/ppermute | solution.py:298
  11.5 2.3 %collective-permute-start.3 = (bf16[2,2,64,128]{3,2,1,0:T(8,128)(2,1)S(1)}, bf16[2,2,64,128]{3,2,1,0:T(8,128)(2,1)S(1)}, u32[]{:S(2)}, u32[]{:S(2)}) collective-permute-start(bf16[2,2,64,128]{3,2,1,0:T(8,128)(2,1)S(1)} %get-tuple-element.32), channel_id=1, source_target_pairs={{0,4},{4,0},{8,12},{12,8},{1,5},{5,1},{9,13},{13,9},{2,6},{6,2},{1... | collective-permute-start | bytes 196616 | tf_op jit(solution)/shard_map/ppermute | solution.py:298
  12.1 4.0 %collective-permute-start.7 = (bf16[1,2,64,128]{3,2,1,0:T(8,128)(2,1)S(1)}, bf16[1,2,64,128]{3,2,1,0:T(8,128)(2,1)S(1)}, u32[]{:S(2)}, u32[]{:S(2)}) collective-permute-start(bf16[1,2,64,128]{3,2,1,0:T(8,128)(2,1)S(1)} %slice.37), channel_id=1, source_target_pairs={{0,8},{4,12},{8,0},{12,4},{1,9},{5,13},{9,1},{13,5},{2,10},{6,14},... | collective-permute-start | bytes 98312 | tf_op jit(solution)/shard_map/ppermute | solution.py:298
  13.8 4.8 %collective-permute-start.4 = (bf16[1,2,64,128]{3,2,1,0:T(8,128)(2,1)S(1)}, bf16[1,2,64,128]{3,2,1,0:T(8,128)(2,1)S(1)}, u32[]{:S(2)}, u32[]{:S(2)}) collective-permute-start(bf16[1,2,64,128]{3,2,1,0:T(8,128)(2,1)S(1)} %slice.33), channel_id=1, source_target_pairs={{0,8},{4,12},{8,0},{12,4},{1,9},{5,13},{9,1},{13,5},{2,10},{6,14},... | collective-permute-start | bytes 98312 | tf_op jit(solution)/shard_map/ppermute | solution.py:298
  16.1 5.6 %collective-permute-start.8 = (bf16[64,128]{1,0:T(8,128)(2,1)S(1)}, bf16[64,128]{1,0:T(8,128)(2,1)S(1)}, u32[]{:S(2)}, u32[]{:S(2)}) collective-permute-start(bf16[64,128]{1,0:T(8,128)(2,1)S(1)} %get-tuple-element.36), channel_id=1, source_target_pairs={{0,1},{1,2},{2,3},{3,0},{4,5},{5,6},{6,7},{7,4},{8,9},{9,10},{10,1... | collective-permute-start | bytes 49160 | tf_op jit(solution)/shard_map/ppermute | solution.py:304
  17.4 4.6 %collective-permute-start.9 = (bf16[64,128]{1,0:T(8,128)(2,1)S(1)}, bf16[64,128]{1,0:T(8,128)(2,1)S(1)}, u32[]{:S(2)}, u32[]{:S(2)}) collective-permute-start(bf16[64,128]{1,0:T(8,128)(2,1)S(1)} %get-tuple-element.35), channel_id=1, source_target_pairs={{0,2},{1,3},{2,0},{3,1},{4,6},{5,7},{6,4},{7,5},{8,10},{9,11},{10,... | collective-permute-start | bytes 49160 | tf_op jit(solution)/shard_map/ppermute | solution.py:304
  18.7 3.8 %collective-permute-start.5 = (bf16[64,128]{1,0:T(8,128)(2,1)S(1)}, bf16[64,128]{1,0:T(8,128)(2,1)S(1)}, u32[]{:S(2)}, u32[]{:S(2)}) collective-permute-start(bf16[64,128]{1,0:T(8,128)(2,1)S(1)} %get-tuple-element.37), channel_id=1, source_target_pairs={{0,3},{1,0},{2,1},{3,2},{4,7},{5,4},{6,5},{7,6},{8,11},{9,8},{10,9... | collective-permute-start | bytes 49160 | tf_op jit(solution)/shard_map/ppermute | solution.py:304
